TPU v7x, 32 devices: a whole 2x2x4 slice. The times are simulated.
32 devices in a mesh: gy: 16 (over z, x, core), gz: 2 (over y).
Axes of the slice: x: 2, y: 2, z: 4, core: 2. Of those that a mesh axis runs over, the one named last changes fastest.
Arguments:
- velocity: float32 [3, 384, 1024], P(None, ('gy', 'gz')), may hold values from -6 to 6
- explicit: float32 [3, 384, 1024], P(None, ('gy', 'gz')), may hold values from -6 to 6
- bands: float32 [2, 5, 384], P(None, None, 'gy'), may hold values from -0.6 to 0.6
- inverse: float32 [384, 24, 512], P('gy', None, 'gz'), may hold values from -1.25 to 1.25
- spikes: float32 [2, 2, 384, 512], P(None, None, 'gy', 'gz'), may hold values from -1.4 to 1.4
Outputs:
- updated: float32 [3, 384, 1024], P(None, 'gy', 'gz')
All inputs are finite; a program needn't handle non-finite values.
Results may differ from a plain program's by a relative error of at most 0.00024.
Values sent between devices are 32-bit elements; how exact they have to be, the bound alone decides.
No kernel may reach another device: no remote copies, remote signals or barrier semaphores. Data moves between devices by JAX's collectives and lax.ppermute only.
A program may use at most 64 MiB of HBM per device.

v0:
```python
import jax
import jax.numpy as jnp
from jax import lax
from jax.sharding import PartitionSpec as P


def extended(cells, sides, width):
    for axis, dim in sides:
        count = lax.axis_size(axis)
        ends = count - 1
        head = lax.slice_in_dim(cells, 0, width, axis=dim)
        tail = lax.slice_in_dim(cells, cells.shape[dim] - width, cells.shape[dim], axis=dim)
        cells = jnp.concatenate(
            [
                lax.ppermute(tail, axis, [(i, (i + 1) % count) for i in range(ends)]),
                cells,
                lax.ppermute(head, axis, [((i + 1) % count, i) for i in range(ends)]),
            ],
            axis=dim,
        )
    return cells


def prefix_2(value, axis, join, neutral, backward):
    count, mine = (lax.axis_size(axis), lax.axis_index(axis))
    pieces = jax.tree.map(lambda part: lax.all_gather(part, axis), value)
    if backward:
        pieces = jax.tree.map(lambda part: part[::-1], pieces)
        mine = count - 1 - mine
    total = jax.tree.map(
        lambda part, zero: jnp.full_like(part, 0) + jnp.asarray(zero, part.dtype), value, neutral
    )

    def lap(position, total):
        longer = join(total, jax.tree.map(lambda part: part[position], pieces))
        return jax.tree.map(lambda new, old: jnp.where(position < mine, new, old), longer, total)

    return lax.fori_loop(0, count - 1, lap, total)


def couple(spike, state):
    first = spike[..., 0, :, :][..., None, :, :, None] * state[..., :, 0, :, :][..., :, None, :, :]
    second = spike[..., 1, :, :][..., None, :, :, None] * state[..., :, 1, :, :][..., :, None, :, :]
    return first + second


def apply_map(matrix, state):
    first = matrix[..., :, 0, :][..., None, :, :, None] * state[..., :, 0, :, :][..., :, None, :, :]
    second = (
        matrix[..., :, 1, :][..., None, :, :, None] * state[..., :, 1, :, :][..., :, None, :, :]
    )
    return first + second


def compose(later, earlier):
    first = later[..., :, 0, :][..., :, None, :] * earlier[..., 0, :, :][..., None, :, :]
    second = later[..., :, 1, :][..., :, None, :] * earlier[..., 1, :, :][..., None, :, :]
    return first + second


def combine(earlier, later):
    return (compose(later[0], earlier[0]), apply_map(later[0], earlier[1]) + later[1])


def per_device(velocity, explicit, bands, inverse, spikes):
    stacked = jnp.stack([velocity, velocity + explicit])
    moved = lax.all_to_all(stacked, "gz", split_axis=3, concat_axis=2, tiled=True)
    rows = moved.shape[2]
    modes = inverse.shape[2]
    padded = extended(moved, (("gy", 2),), 2)
    rhs = jnp.zeros(moved.shape[1:], jnp.float32)
    for offset in range(5):
        rhs = rhs + bands[0, offset][None, :, None] * padded[1][:, offset : offset + rows]
        rhs = rhs + bands[1, offset][None, :, None] * padded[0][:, offset : offset + rows]
    rhs_modes = rhs.reshape(3, rows, modes, 2)
    local = jnp.einsum("rcm,fcmp->frmp", inverse, rhs_modes, precision=lax.Precision.HIGHEST)
    lower = spikes[0]
    upper = spikes[1]
    down_map = -jnp.transpose(lower[:, rows - 2 :], (1, 0, 2))
    up_map = -jnp.transpose(upper[:, 0:2], (1, 0, 2))
    eye_map = jnp.broadcast_to(jnp.eye(2, dtype=jnp.float32)[:, :, None], (2, 2, modes))
    zero_state = jnp.zeros((3, 2, modes, 2), jnp.float32)
    prefix = prefix_2((down_map, local[:, rows - 2 :]), "gy", combine, (eye_map, zero_state), False)
    before = prefix[1]
    zvals = local - couple(lower, before)
    suffix = prefix_2((up_map, zvals[:, 0:2]), "gy", combine, (eye_map, zero_state), True)
    after = suffix[1]
    result = zvals - couple(upper, after)
    return result.reshape(3, rows, 2 * modes)


def solution(mesh):
    placed = (
        P(None, ("gy", "gz"), None),
        P(None, ("gy", "gz"), None),
        P(None, None, "gy"),
        P("gy", None, "gz"),
        P(None, None, "gy", "gz"),
    )
    return jax.shard_map(
        per_device, mesh=mesh, in_specs=placed, out_specs=P(None, "gy", "gz"), check_vma=False
    )
```

profile of v0, /device:TPU:0, one launch (start us, length us, event | category | flops | bytes accessed | tf_op | source)
XLA Modules:
  0.0 144.2 jit_solution(3540932697578752592)
XLA Ops:
  0.0 1.0 stack.9
  1.0 1.0 add.108
  2.2 0.3 pad_maximum_fusion.1
  2.5 2.2 %copy.83 = f32[2,3,12,1024]{2,0,1,3:T(2,128)S(1)} copy(f32[2,3,12,1024]{3,0,2,1:T(2,128)S(1)} %pad_maximum_fusion.1) | data formatting | bytes 589824 | tf_op jit(solution)/shard_map/stack | solution.py:66
  4.7 5.8 %reshape.39 = f32[2,1,36864]{2,1,0:T(1,128)} reshape(f32[1024,3,2,12]{3,2,1,0:T(2,128)S(1)} %bitcast.116) | data formatting | bytes 589824
  10.5 4.4 %all-to-all-start = ((f32[2,1,36864]{2,1,0:T(1,128)}), f32[2,1,36864]{2,1,0:T(1,128)S(1)}, u32[]{:S(2)}, u32[]{:S(2)}) async-start(f32[2,1,36864]{2,1,0:T(1,128)} %reshape.39), calls=%async_computation | async-start | bytes 589824 | tf_op jit(solution)/shard_map/all_to_all | solution.py:67
  14.9 3.1 %copy.105 = f32[24,24,256,1]{1,0,3,2:T(8,128)} copy(f32[24,24,256,1]{2,1,0,3:T(8,128)} %bitcast.126) | data formatting | bytes 1179648 | tf_op args[3]
  18.1 0.8 copy.90
  18.8 0.8 copy.95
  19.6 22.5 %all-gather.2 = f32[32,2,256]{2,1,0:T(2,128)S(1)} all-gather(f32[2,2,256]{2,1,0:T(2,128)S(1)} %fusion.12), channel_id=4, replica_groups=mesh['gy'=16,'gz'=2] {'gy'}, dimensions={0}, use_global_device_ids=true | all-gather | bytes 69632 | tf_op jit(solution)/shard_map/all_gather | solution.py:26
  42.1 0.6 rev.6
  42.7 0.7 copy.102
  43.5 0.7 copy.97
  44.2 0.5 broadcast.20
  44.8 1.5 %reduce = f32[2,36864]{1,0:T(2,128)S(1)} reduce(f32[2,1,36864]{2,1,0:T(1,128)S(1)} %all-to-all-done, f32[]{:T(128)} %broadcast.20), dimensions={1}, to_apply=%all_to_all.13.reduce_sub_computation | reduce | bytes 589828 | tf_op jit(solution)/shard_map/all_to_all | solution.py:67
  46.2 4.8 %reshape.40 = f32[1024,3,2,12]{3,2,1,0:T(2,128)S(1)} reshape(f32[2,36864]{1,0:T(2,128)S(1)} %reduce) | data formatting | bytes 589824
  51.0 2.3 %copy.85 = f32[2,3,2,12,512]{4,0,3,2,1:T(2,128)S(1)} copy(f32[2,3,2,12,512]{3,0,1,4,2:T(2,128)S(1)} %bitcast.117) | data formatting | bytes 589824 | tf_op jit(solution)/shard_map/all_to_all | solution.py:67
  53.3 2.2 %collective-permute-start = (f32[2,3,2,512]{3,0,2,1:T(2,128)S(1)}, f32[2,3,2,512]{3,0,2,1:T(2,128)S(1)}, u32[]{:S(2)}, u32[]{:S(2)}) collective-permute-start(f32[2,3,2,512]{3,0,2,1:T(2,128)S(1)} %get-tuple-element.306), channel_id=1, source_target_pairs={{0,2},{2,4},{4,6},{6,8},{8,10},{10,12},{12,14},{14,16},{16,18},{18... | collective-permute-start | bytes 73736 | tf_op jit(solution)/shard_map/ppermute | solution.py:15
  55.6 1.3 collective-permute-start.1
  56.9 19.7 %all-gather = f32[32,2,256]{2,1,0:T(2,128)S(1)} all-gather(f32[2,2,256]{2,1,0:T(2,128)S(1)} %fusion.13), channel_id=2, replica_groups=mesh['gy'=16,'gz'=2] {'gy'}, dimensions={0}, use_global_device_ids=true | all-gather | bytes 69632 | tf_op jit(solution)/shard_map/all_gather | solution.py:26
  76.8 0.3 fusion.14
  77.4 0.3 copy.87
  77.6 7.2 %convolution_bitcast_fusion = f32[3,24,256,2]{1,0,3,2:T(4,128)S(1)} fusion(f32[24,24,256,1]{1,0,3,2:T(8,128)} %copy.105, f32[3,24,256,2]{1,3,2,0:T(2,128)S(1)} %bitcast.120), kind=kOutput, calls=%fused_computation.18 | convolution fusion | flops 10616832 | bytes 884736 | tf_op jit(solution)/shard_map/rcm,fcmp->frmp/dot_general | solution.py:76
  84.8 0.6 slice.255
  85.4 0.4 copy.92
  85.9 18.0 %all-gather.1 = f32[48,2,256,2]{2,3,1,0:T(2,128)S(1)} all-gather(f32[3,2,256,2]{2,3,1,0:T(2,128)S(1)} %copy.92), channel_id=3, replica_groups=mesh['gy'=16,'gz'=2] {'gy'}, dimensions={0}, use_global_device_ids=true | all-gather | bytes 208896 | tf_op jit(solution)/shard_map/all_gather | solution.py:26
  103.8 1.8 %while.28 = (s32[]{:T(128)}, f32[3,2,256,2]{2,3,1,0:T(2,128)S(1)}, s32[]{:T(128)}, f32[16,2,2,256]{3,2,1,0:T(2,128)S(1)}, f32[16,3,2,256,2]{3,4,2,1,0:T(2,128)S(1)}, /*index=5*/s32[]{:T(128)}, s32[]{:T(128)}) while((s32[]{:T(128)}, f32[3,2,256,2]{2,3,1,0:T(2,128)S(1)}, s32[]{:T(128)}, f32[16,2,2,256]{3,2,1,0:T(2,128)S(1)}, ...), condition=%wide.region_1.2_spmd.clone, body=%wide.region_0.1_spmd.clone.sunk | while | flops 21508 | bytes 127082 | solution.py:38
  106.0 2.2 %add_subtract_fusion.1 = f32[3,24,256,2]{1,0,3,2:T(4,128)S(1)} fusion(f32[3,24,256,2]{1,0,3,2:T(4,128)S(1)} %convolution_bitcast_fusion, f32[3,256,2]{0,2,1:T(2,128)S(1)} %copy.96, f32[24,256]{0,1:T(8,128)S(1)} %copy-done.1, f32[3,256,2]{0,2,1:T(2,128)S(1)} %copy.94, f32[24,256]{0,1:T(8,128)S(1)} %copy-done), kind=kLoop, calls=%fused_computation.21 | loop fusion | flops 147456 | bytes 356352 | tf_op jit(solution)/shard_map/sub | solution.py:85
  108.2 0.4 copy.99
  108.7 19.3 %all-gather.3 = f32[48,2,256,2]{2,3,1,0:T(2,128)S(1)} all-gather(f32[3,2,256,2]{2,3,1,0:T(2,128)S(1)} %copy.99), channel_id=5, replica_groups=mesh['gy'=16,'gz'=2] {'gy'}, dimensions={0}, use_global_device_ids=true | all-gather | bytes 208896 | tf_op jit(solution)/shard_map/all_gather | solution.py:26
  128.0 11.5 %while.29 = (s32[]{:T(128)}, f32[3,2,256,2]{2,3,1,0:T(2,128)S(1)}, s32[]{:T(128)}, f32[16,2,2,256]{3,2,1,0:T(2,128)}, f32[16,3,2,256,2]{3,4,2,1,0:T(2,128)S(1)}, /*index=5*/s32[]{:T(128)}, s32[]{:T(128)}) while((s32[]{:T(128)}, f32[3,2,256,2]{2,3,1,0:T(2,128)S(1)}, s32[]{:T(128)}, f32[16,2,2,256]{3,2,1,0:T(2,128)}, ...), condition=%wide.region_3.4_spmd.clone, body=%wide.region_2.3_spmd.clone.sunk | while | flops 21508 | bytes 127082 | solution.py:38
  128.0 0.7 constant_dynamic-slice_fusion.5
  128.8 0.7 constant_dynamic-slice_fusion.5
  129.5 0.7 constant_dynamic-slice_fusion.5
  130.3 0.7 constant_dynamic-slice_fusion.5
  131.1 0.7 constant_dynamic-slice_fusion.5
  131.8 0.7 constant_dynamic-slice_fusion.5
  132.6 0.7 constant_dynamic-slice_fusion.5
  133.4 0.7 constant_dynamic-slice_fusion.5
  134.1 0.7 constant_dynamic-slice_fusion.5
  134.9 0.7 constant_dynamic-slice_fusion.5
  135.7 0.7 constant_dynamic-slice_fusion.5
  136.5 0.7 constant_dynamic-slice_fusion.5
  137.2 0.7 constant_dynamic-slice_fusion.5
  138.0 0.7 constant_dynamic-slice_fusion.5
  138.7 0.7 constant_dynamic-slice_fusion.5
  139.9 3.4 %add_subtract_fusion = f32[3,24,256,2]{1,0,3,2:T(4,128)S(1)} fusion(f32[3,256,2]{0,2,1:T(2,128)S(1)} %copy.103, f32[24,256]{0,1:T(8,128)S(1)} %copy-done.2, f32[3,256,2]{0,2,1:T(2,128)S(1)} %copy.101, f32[24,256]{0,1:T(8,128)} %copy.97, f32[3,24,256,2]{1,0,3,2:T(4,128)S(1)} %convolution_bitcast_fusion, f32[3,256,2]{0,2,1:T(2,128)S(1)} %copy.96, ...), kind=kLoop, calls=%fused_computation.20 | loop fusion | flops 294912 | bytes 417792 | tf_op jit(solution)/shard_map/sub | solution.py:88
  143.3 0.9 copy.104
  (200 shorter events, 3.0 us)
Async XLA Ops:
  2.5 12.4 %copy-start.3 = (f32[2,2,24,256]{3,2,1,0:T(8,128)S(1)}, f32[2,2,24,256]{3,2,1,0:T(8,128)}, u32[]{:S(2)}) copy-start(f32[2,2,24,256]{3,2,1,0:T(8,128)} %param.13) | copy-start | bytes 294916
  10.5 33.7 %copy-start.4 = (f32[2,5,24]{2,0,1:T(2,128)S(1)}, f32[2,5,24]{2,0,1:T(2,128)}, u32[]{:S(2)}) copy-start(f32[2,5,24]{2,0,1:T(2,128)} %param.11) | copy-start | bytes 2884
  10.5 33.7 %all-to-all-start = ((f32[2,1,36864]{2,1,0:T(1,128)}), f32[2,1,36864]{2,1,0:T(1,128)S(1)}, u32[]{:S(2)}, u32[]{:S(2)}) async-start(f32[2,1,36864]{2,1,0:T(1,128)} %reshape.39), calls=%async_computation | async-start | bytes 589824 | tf_op jit(solution)/shard_map/all_to_all | solution.py:67
  53.3 23.3 %collective-permute-start = (f32[2,3,2,512]{3,0,2,1:T(2,128)S(1)}, f32[2,3,2,512]{3,0,2,1:T(2,128)S(1)}, u32[]{:S(2)}, u32[]{:S(2)}) collective-permute-start(f32[2,3,2,512]{3,0,2,1:T(2,128)S(1)} %get-tuple-element.306), channel_id=1, source_target_pairs={{0,2},{2,4},{4,6},{6,8},{8,10},{10,12},{12,14},{14,16},{16,18},{18... | collective-permute-start | bytes 73736 | tf_op jit(solution)/shard_map/ppermute | solution.py:15
  55.6 21.0 %collective-permute-start.1 = (f32[2,3,2,512]{3,0,2,1:T(2,128)S(1)}, f32[2,3,2,512]{3,0,2,1:T(2,128)S(1)}, u32[]{:S(2)}, u32[]{:S(2)}) collective-permute-start(f32[2,3,2,512]{3,0,2,1:T(2,128)S(1)} %get-tuple-element.307), channel_id=1, source_target_pairs={{2,0},{4,2},{6,4},{8,6},{10,8},{12,10},{14,12},{16,14},{18,16},{20... | collective-permute-start | bytes 73736 | tf_op jit(solution)/shard_map/ppermute | solution.py:17
  84.8 21.2 %copy-start = (f32[24,256]{0,1:T(8,128)S(1)}, f32[24,256]{0,1:T(8,128)}, u32[]{:S(2)}) copy-start(f32[24,256]{0,1:T(8,128)} %copy.90) | copy-start | bytes 73732
  84.8 21.2 %copy-start.1 = (f32[24,256]{0,1:T(8,128)S(1)}, f32[24,256]{0,1:T(8,128)}, u32[]{:S(2)}) copy-start(f32[24,256]{0,1:T(8,128)} %copy.95) | copy-start | bytes 73732
  105.8 34.1 %copy-start.2 = (f32[24,256]{0,1:T(8,128)S(1)}, f32[24,256]{0,1:T(8,128)}, u32[]{:S(2)}) copy-start(f32[24,256]{0,1:T(8,128)} %copy.102) | copy-start | bytes 73732
where the time goes:
time: 145 us; the launch traced here: 144 us
  blocking collectives  79.4 us (55%)
  local copies, waits for them, and re-layouts  38.1 us (26%)
  other arithmetic  9.82 us (7%)
  starting transfers between devices  7.91 us (5%)
  matrix products  7.18 us (5%)
    all_gather x4, blocking collectives, prefix_2(): pieces = jax.tree.map(lambda part: lax.all_gather(part, axis), value)  79.4 us
    unnamed x17, local copies, waits for them, and re-layouts  13.8 us
    dynamic_slice x60, local copies, waits for them, and re-layouts, lap(): longer = join(total, jax.tree.map(lambda part: part[position], pieces))  10.6 us
    dot_general x1, matrix products, per_device(): jnp.einsum('rcm,fcmp->frmp', inverse, rhs_modes, precision=lax.Precision....  7.18 us
    all_to_all x1, starting transfers between devices, per_device(): lax.all_to_all(stacked, 'gz', split_axis=3, concat_axis=2, tiled=True)  4.37 us
    sub x1, other arithmetic, per_device(): result = zvals - couple(upper, after)  3.4 us
    another operation x3, local copies, waits for them, and re-layouts, per_device(): stacked = jnp.stack([velocity, velocity + explicit])  3.37 us
  transfers between devices with their start and end apart: 3, of which 0 were waited for; matrix products, arithmetic and copies ran while one was open for 5% of the time, Pallas kernels for 0%

commit v1 on v0

v1 whole, which is shorter than its diff:
```python
import functools

import jax
import jax.numpy as jnp
from jax import lax
from jax.experimental import pallas as pl
from jax.experimental.pallas import tpu as pltpu
from jax.sharding import PartitionSpec as P

F32 = jnp.float32
BF16 = jnp.bfloat16
LANES = 128
HALO = 2


def vmem_call(body, out_shapes, args, scratch=(), flops=0, name=None):
    spec = pl.BlockSpec(memory_space=pltpu.VMEM)
    nbytes = sum(a.size * 4 for a in args)
    return pl.pallas_call(
        body,
        out_shape=[jax.ShapeDtypeStruct(s, F32) for s in out_shapes],
        in_specs=[spec] * len(args),
        out_specs=[spec] * len(out_shapes),
        scratch_shapes=list(scratch),
        compiler_params=pltpu.CompilerParams(vmem_limit_bytes=16 * 2**20),
        cost_estimate=pl.CostEstimate(flops=flops, bytes_accessed=nbytes, transcendentals=0),
        name=name,
    )(*args)


def window(rows, own, groups):
    for wide in range(8, rows + 1, 8):
        firsts = []
        for g in range(groups):
            low = max(g * own - HALO, 0)
            first = min(low // 8 * 8, rows - wide)
            if min(g * own + own + HALO, rows) > first + wide:
                break
            firsts.append(first)
        if len(firsts) == groups:
            return wide, firsts
    return rows, [0] * groups


def pick(values, index):
    result = jnp.int32(values[0])
    for i, value in enumerate(values[1:], 1):
        result = jnp.where(index == i, jnp.int32(value), result)
    return result


def exact_parts(x):
    high = x.astype(BF16)
    rest = x - high.astype(F32)
    mid = rest.astype(BF16)
    low = (rest - mid.astype(F32)).astype(BF16)
    return high, mid, low


def by_ones(x, ones):
    high, mid, low = exact_parts(x)
    dot = functools.partial(jnp.dot, preferred_element_type=F32)
    return dot(high, ones) + (dot(mid, ones) + dot(low, ones))


def doubled(x):
    row = lax.broadcasted_iota(jnp.int32, (LANES, 2 * LANES), 0)
    col = lax.broadcasted_iota(jnp.int32, (LANES, 2 * LANES), 1)
    ones = (row == lax.shift_right_logical(col, 1)).astype(F32).astype(BF16)
    parts = [by_ones(x[:, i : i + LANES], ones) for i in range(0, x.shape[1], LANES)]
    return jnp.concatenate(parts, axis=1)


def interleave_ones(back):
    a = lax.broadcasted_iota(jnp.int32, (2 * LANES, 2 * LANES), 1 if back else 0)
    b = lax.broadcasted_iota(jnp.int32, (2 * LANES, 2 * LANES), 0 if back else 1)
    place = 2 * (b % LANES) + b // LANES
    return (a == place).astype(F32).astype(BF16)


def edges_kernel(groups, velocity, explicit, out):
    g = lax.axis_index("gz")
    own = velocity.shape[1]
    head = pl.ds(0, HALO)
    tail = pl.ds(own - HALO, HALO)
    for f in range(3):
        for row, which in ((f, None), (f + 3, explicit)):
            top, bottom = velocity[f, head], velocity[f, tail]
            if which is not None:
                top, bottom = top + which[f, head], bottom + which[f, tail]
            out[row] = jnp.where(g == 0, top, bottom)


def prepare_kernel(bands, spikes, inverse, maps, lu, inv4, coef, square):
    rows = inverse.shape[1]
    lu2 = doubled(spikes[...].reshape(4 * rows, -1))
    lu[...] = lu2.reshape(lu.shape)
    for k in range(2):
        for j in range(2):
            maps[2 * k + j : 2 * k + j + 1] = -lu[0, j, rows - 2 + k : rows - 1 + k]
            maps[4 + 2 * k + j : 5 + 2 * k + j] = -lu[0, j, k : k + 1]
            maps[8 + 2 * k + j : 9 + 2 * k + j] = -lu[1, j, k : k + 1]
    near = jnp.concatenate([inverse[0:2], inverse[rows - 2 : rows]], axis=0)
    inv4[...] = doubled(near.reshape(4 * rows, -1)).reshape(inv4.shape)
    square[...] = jnp.zeros_like(square)
    square[0:5, 0:rows] = bands[0]
    square[8:13, 0:rows] = bands[1]
    turned = jnp.transpose(square[...])
    for a in range(2):
        for d in range(5):
            column = turned[0:rows, 8 * a + d : 8 * a + d + 1]
            coef[5 * a + d] = jnp.broadcast_to(column, (rows, LANES))


def stencil_kernel(wide, firsts, velocity, explicit, halo, coef, *refs):
    outs, (vel, tot) = refs[:-2], refs[-2:]
    groups = len(firsts)
    own, lanes = velocity.shape[1:]
    rows = coef.shape[1]
    part = lanes // groups
    g = lax.axis_index("gz")
    gy, count = lax.axis_index("gy"), lax.axis_size("gy")
    vel[...] = jnp.zeros_like(vel)
    tot[...] = jnp.zeros_like(tot)
    for k in range(groups):
        base = 8 + k * own - firsts[k]

        @pl.when(g == k)
        def _(base=base):
            for f in range(3):
                vel[f, base : base + own] = velocity[f]
                tot[f, base : base + own] = velocity[f] + explicit[f]

    first = pl.multiple_of(pick(firsts, g), 8)
    weights = [coef[i, pl.ds(first, wide)] for i in range(10)]
    below = (g == 0) & (gy < count - 1)
    above = (g == groups - 1) & (gy > 0)

    def beside(low, high):
        chosen = []
        for kind in (5, 0):
            one = 0.0 if high is None else coef[kind + high[0], high[1] : high[1] + 1]
            two = 0.0 if low is None else coef[kind + low[0], low[1] : low[1] + 1]
            chosen.append(jnp.where(below, one, jnp.where(above, two, jnp.zeros((1, LANES), F32))))
        return chosen

    sides = [
        [beside((0, 0), (4, rows - 2)), beside((1, 0), None)],
        [beside(None, (3, rows - 1)), beside((0, 1), (4, rows - 1))],
    ]
    for shift, out in enumerate(outs):
        begin = lax.rem(g + shift, groups) * part
        for lane in range(0, part, LANES):
            at = pl.ds(pl.multiple_of(begin + lane, LANES), LANES)
            to = pl.ds(lane, LANES)
            for f in range(3):
                total = None
                for d in range(5):
                    low = pl.ds(8 + d - 2, wide)
                    term = weights[d] * tot[f, low, at] + weights[5 + d] * vel[f, low, at]
                    total = term if total is None else total + term
                out[f * wide : f * wide + wide, to] = total
                for i in range(2):
                    total = None
                    for j in range(2):
                        term = sides[i][j][0] * halo[f, j : j + 1, at] + sides[i][j][1] * halo[f + 3, j : j + 1, at]
                        total = term if total is None else total + term
                    row = 3 * wide + 2 * f + i
                    out[row : row + 1, to] = total


def interface_kernel(wide, firsts, inv4, maps, *refs):
    groups = len(firsts)
    pieces, (rhs, message) = refs[:groups], refs[groups:]
    rows = rhs.shape[1]
    g = lax.axis_index("gz")
    rhs[...] = jnp.zeros_like(rhs)
    for shift, piece in enumerate(pieces):
        source = lax.rem(g - shift + groups, groups)
        at = pl.ds(pl.multiple_of(pick(firsts, source), 8), wide)
        for f in range(3):
            rhs[f, at] += piece[f * wide : f * wide + wide]
            side = piece[3 * wide + 2 * f : 3 * wide + 2 * f + 2]
            rhs[f, 0:2] += jnp.where(source == groups - 1, side, 0.0)
            rhs[f, rows - 2 : rows] += jnp.where(source == 0, side, 0.0)
    for f in range(3):
        for r in range(4):
            value = jnp.sum(inv4[r] * rhs[f], axis=0, keepdims=True)
            row = (6 if r < 2 else 0) + 3 * (r % 2) + f
            message[row : row + 1] = value
    message[12:24] = maps[...]


class Piece:
    def __init__(self, ref):
        self.p = [ref[0:3], ref[3:6]]
        self.q = [ref[6:9], ref[9:12]]
        grid = lambda at: [[ref[at + 2 * k + j : at + 2 * k + j + 1] for j in range(2)] for k in range(2)]
        self.F, self.H, self.G = grid(12), grid(16), grid(20)


def act(matrix, vector, plus=None):
    out = [matrix[k][0] * vector[0] + matrix[k][1] * vector[1] for k in range(2)]
    return out if plus is None else [plus[k] + out[k] for k in range(2)]


def times(a, b, plus=None):
    out = [[a[k][0] * b[0][j] + a[k][1] * b[1][j] for j in range(2)] for k in range(2)]
    return out if plus is None else [[plus[k][j] + out[k][j] for j in range(2)] for k in range(2)]


def after(state, piece):
    if state is None:
        return piece.p, piece.F
    return act(piece.F, state[0], piece.p), times(piece.F, state[1])


def before(piece, state):
    if state is None:
        return piece.q, piece.H, piece.G
    q, H, G = state
    q = act(piece.G, act(H, piece.p, q), piece.q)
    H = times(piece.G, times(H, piece.F), piece.H)
    return q, H, times(piece.G, G)


def choose(flag, new, old):
    return jax.tree.map(lambda a, b: jnp.where(flag, a, b), new, old)


def store_vector(ref, at, vector):
    ref[at : at + 3] = vector[0]
    ref[at + 3 : at + 6] = vector[1]


def store_matrix(ref, at, matrix):
    for k in range(2):
        for j in range(2):
            ref[at + 2 * k + j : at + 2 * k + j + 1] = matrix[k][j]


def sorted_pieces(base, pieces, board):
    size = len(pieces)
    position = lax.rem(lax.div(lax.axis_index("gy"), base), size)
    for x, piece in enumerate(pieces):
        board[jnp.bitwise_xor(position, x)] = piece[...]
    return position, [Piece(board.at[i]) for i in range(size)]


def compose_kernel(base, *refs):
    *pieces, out, board = refs
    _, run = sorted_pieces(base, pieces, board)
    up = down = None
    for piece in run:
        up = after(up, piece)
    for piece in run[::-1]:
        down = before(piece, down)
    store_vector(out, 0, up[0])
    store_vector(out, 6, down[0])
    store_matrix(out, 12, up[1])
    store_matrix(out, 16, down[1])
    store_matrix(out, 20, down[2])


def around(base, pieces, board):
    position, run = sorted_pieces(base, pieces, board)
    mine = Piece(pieces[0])
    one, none = jnp.ones_like(mine.F[0][0]), jnp.zeros_like(mine.F[0][0])
    zero = jnp.zeros_like(mine.p[0])
    unit = [[one, none], [none, one]]
    blank = [[none, none], [none, none]]
    up = ([zero, zero], unit)
    for i, piece in enumerate(run[:-1]):
        up = choose(i < position, after(up, piece), up)
    down = ([zero, zero], blank, unit)
    for i in range(len(run) - 1, 0, -1):
        down = choose(i > position, before(run[i], down), down)
    return mine, up, down


def widen(base, pieces, board, known):
    mine, (pl_, Fl), (q, H, G) = around(base, pieces, board)
    top = act(mine.F, pl_, mine.p)
    e = act(H, top, q)
    E = times(H, times(mine.F, Fl))
    if known is None:
        return pl_, Fl, e, E, G
    a, A, b, B, D = known
    return (
        act(A, pl_, a),
        times(A, Fl),
        act(D, e, act(B, pl_, b)),
        times(D, E, times(B, Fl)),
        times(D, G),
    )


def read_known(ref):
    piece = Piece(ref)
    return piece.p, piece.F, piece.q, piece.H, piece.G


def widen_kernel(base, start, *refs):
    *pieces, out, board = refs
    known = None
    if not start:
        known = read_known(pieces.pop())
    a, A, b, B, D = widen(base, pieces, board, known)
    store_vector(out, 0, a)
    store_vector(out, 6, b)
    store_matrix(out, 12, A)
    store_matrix(out, 16, B)
    store_matrix(out, 20, D)


def block_kernel(inverse, rhs, local, split, solved):
    fields, rows, lanes = rhs.shape
    apart, together = interleave_ones(False), interleave_ones(True)
    flat = rhs[...].reshape(fields * rows, lanes)
    for at in range(0, lanes, 2 * LANES):
        turned = by_ones(flat[:, at : at + 2 * LANES], apart)
        split[:, :, at : at + 2 * LANES] = turned.reshape(fields, rows, 2 * LANES)
    for tile in range(lanes // (2 * LANES)):
        modes = pl.ds(tile * LANES, LANES)
        for f in range(fields):
            for p in range(2):
                at = pl.ds((2 * tile + p) * LANES, LANES)
                value = split[f, :, at]
                solved[f, :, at] = jnp.sum(inverse[:, :, modes] * value[None], axis=1)
    flat = solved[...].reshape(fields * rows, lanes)
    for at in range(0, lanes, 2 * LANES):
        turned = by_ones(flat[:, at : at + 2 * LANES], together)
        local[:, :, at : at + 2 * LANES] = turned.reshape(fields, rows, 2 * LANES)


def final_kernel(base, start, local, lu, *refs):
    *pieces, out, board = refs
    known = None
    if not start:
        known = read_known(pieces.pop())
    t, _, s, _, _ = widen(base, pieces, board, known)
    for f in range(3):
        value = local[f]
        for k in range(2):
            value = value - lu[0, k] * t[k][f : f + 1] - lu[1, k] * s[k][f : f + 1]
        out[f] = value


def ring_halo(gy, gz):
    at = lambda y, z: y * gz + z
    pairs = []
    for y in range(gy):
        for z in range(gz):
            if gz == 1:
                continue
            if z == gz - 1:
                pairs.append((at(y, z), at(y + 1, z) if y < gy - 1 else at(y, 0)))
            elif z == 0:
                pairs.append((at(y, z), at(y - 1, z) if y > 0 else at(y, gz - 1)))
    return pairs


def groups_of(count):
    steps, base = [], 1
    while base < count:
        size = 4 if base > 1 and base * 4 <= count else 2
        steps.append((base, size))
        base *= size
    return steps


def per_device(velocity, explicit, bands, inverse, spikes):
    gy, gz = lax.axis_size("gy"), lax.axis_size("gz")
    own, columns = velocity.shape[1:]
    rows, modes = inverse.shape[0], inverse.shape[2]
    lanes = 2 * modes
    wide, firsts = window(rows, own, gz)

    (edges,) = vmem_call(
        functools.partial(edges_kernel, gz), [(6, HALO, columns)], [velocity, explicit], name="edges"
    )
    halo = lax.ppermute(edges, ("gy", "gz"), ring_halo(gy, gz))
    maps, lu, inv4, coef = vmem_call(
        prepare_kernel,
        [(12, lanes), (2, 2, rows, lanes), (4, rows, lanes), (10, rows, LANES)],
        [bands, spikes, inverse],
        scratch=[pltpu.VMEM((LANES, LANES), F32)],
        flops=2 * 10**8,
        name="prepare",
    )
    padded = pltpu.VMEM((3, wide + 24, columns), F32)
    shares = vmem_call(
        functools.partial(stencil_kernel, wide, firsts),
        [(3 * wide + 8, lanes)] * gz,
        [velocity, explicit, halo, coef],
        scratch=[padded, padded],
        name="stencil",
    )
    pieces = [shares[0]]
    for shift in range(1, gz):
        ring = [(i, (i + shift) % gz) for i in range(gz)]
        pieces.append(lax.ppermute(shares[shift], "gz", ring))
    rhs, message = vmem_call(
        functools.partial(interface_kernel, wide, firsts),
        [(3, rows, lanes), (24, lanes)],
        [inv4, maps, *pieces],
        name="interface",
    )

    known, local = None, None
    steps = groups_of(gy)
    for number, (base, size) in enumerate(steps):
        gathered = [message]
        for x in range(1, size):
            mask = x * base if number == 0 else (x * base) | 1
            gathered.append(lax.ppermute(message, "gy", [(i, i ^ mask) for i in range(gy)]))
        board = [pltpu.VMEM((size, 24, lanes), F32)]
        have = [] if known is None else [known]
        if number == 1 or len(steps) == 1:
            (local,) = vmem_call(
                block_kernel,
                [(3, rows, lanes)],
                [inverse, rhs],
                scratch=[pltpu.VMEM((3, rows, lanes), F32)] * 2,
                flops=2 * 10**8,
                name="block",
            )
        if number == len(steps) - 1:
            (out,) = vmem_call(
                functools.partial(final_kernel, base, known is None),
                [(3, rows, lanes)],
                [local, lu, *gathered, *have],
                scratch=board,
                name="final",
            )
            return out
        (message,) = vmem_call(
            functools.partial(compose_kernel, base), [(24, lanes)], gathered, scratch=board, name="compose"
        )
        (known,) = vmem_call(
            functools.partial(widen_kernel, base, known is None),
            [(24, lanes)],
            [*gathered, *have],
            scratch=board,
            flops=10**7,
            name="widen",
        )


def solution(mesh):
    placed = (
        P(None, ("gy", "gz"), None),
        P(None, ("gy", "gz"), None),
        P(None, None, "gy"),
        P("gy", None, "gz"),
        P(None, None, "gy", "gz"),
    )
    return jax.shard_map(
        per_device, mesh=mesh, in_specs=placed, out_specs=P(None, "gy", "gz"), check_vma=False
    )
```

time: 145 us -> 26.5 us (0.18)
  blocking collectives: 79.4 us -> 0 us
  local copies, waits for them, and re-layouts: 38.1 us -> 3.27 us
  other arithmetic: 9.82 us -> 0 us
  waiting for transfers between devices: 0.01 us -> 9.1 us
  matrix products: 7.18 us -> 0 us
  Pallas kernels: 0 us -> 3.06 us
  starting transfers between devices: 7.91 us -> 10.8 us
    all_gather x4 -> x0, blocking collectives: 79.4 us -> none  [prefix_2(): pieces = jax.tree.map(lambda part: lax.all_gather(part, axis), value)]
    dynamic_slice x60 -> x0, local copies, waits for them, and re-layouts: 10.6 us -> none  [lap(): longer = join(total, jax.tree.map(lambda part: part[position], pieces))]
    unnamed x17, local copies, waits for them, and re-layouts: 13.8 us -> 3.27 us
    ppermute x2 -> x7, waiting for transfers between devices: 0.01 us -> 9.1 us  [the longest x5 5.83 us: per_device(): lax.ppermute(message, 'gy', [(i, i ^ mask) for i in range(gy)])]
    ppermute x2 -> x7, starting transfers between devices: 3.54 us -> 10.8 us  [the longest x5 5.67 us: per_device(): lax.ppermute(message, 'gy', [(i, i ^ mask) for i in range(gy)])]
    dot_general x1 -> x0, matrix products: 7.18 us -> none  [per_device(): jnp.einsum('rcm,fcmp->frmp', inverse, rhs_modes, precision=lax.Precision....]
    sub x2 -> x0, other arithmetic: 5.61 us -> none  [the longest x1 3.4 us: per_device(): result = zvals - couple(upper, after)]
    all_to_all x1 -> x0, starting transfers between devices: 4.37 us -> none  [per_device(): lax.all_to_all(stacked, 'gz', split_axis=3, concat_axis=2, tiled=True)]
  transfers between devices with their start and end apart: 3 -> 7, of which waited for: 0 -> 7; matrix products, arithmetic and copies ran while one was open for 5% -> 0% of each run, Pallas kernels for 0% -> 6%
where the time goes in v1:
time: 26.5 us; the launch traced here: 26.3 us
  starting transfers between devices  10.8 us (41%)
  waiting for transfers between devices  9.1 us (34%)
  local copies, waits for them, and re-layouts  3.27 us (12%)
  Pallas kernels  3.06 us (12%)
    ppermute x5, waiting for transfers between devices, per_device(): lax.ppermute(message, 'gy', [(i, i ^ mask) for i in range(gy)])  5.83 us
    ppermute x5, starting transfers between devices, per_device(): lax.ppermute(message, 'gy', [(i, i ^ mask) for i in range(gy)])  5.67 us
    unnamed x17, local copies, waits for them, and re-layouts  3.27 us
    pallas_call x10, Pallas kernels, vmem_call(): pl.pallas_call(body, out_shape=[jax.ShapeDtypeStruct(s, F32) for s in out...  3.06 us
    ppermute x1, starting transfers between devices, per_device(): halo = lax.ppermute(edges, ('gy', 'gz'), ring_halo(gy, gz))  3.02 us
    ppermute x1, waiting for transfers between devices, per_device(): pieces.append(lax.ppermute(shares[shift], 'gz', ring))  2.91 us
    ppermute x1, starting transfers between devices, per_device(): pieces.append(lax.ppermute(shares[shift], 'gz', ring))  2.07 us
  transfers between devices with their start and end apart: 7, of which 7 were waited for; matrix products, arithmetic and copies ran while one was open for 0% of the time, Pallas kernels for 6%

profile of v1, /device:TPU:0, one launch (start us, length us, event | category | flops | bytes accessed | tf_op | source)
XLA Modules:
  0.0 26.3 jit_solution(9412412038077251430)
XLA Ops:
  0.0 0.0 copy-start
  0.0 0.9 %copy-done = f32[3,12,1024]{2,1,0:T(8,128)S(1)} copy-done((f32[3,12,1024]{2,1,0:T(8,128)S(1)}, f32[3,12,1024]{2,1,0:T(8,128)}, u32[]{:S(2)}) %copy-start) | copy-done | bytes 147480
  0.9 0.0 copy-start.2
  0.9 0.9 %copy-done.2 = f32[3,12,1024]{2,1,0:T(8,128)S(1)} copy-done((f32[3,12,1024]{2,1,0:T(8,128)S(1)}, f32[3,12,1024]{2,1,0:T(8,128)}, u32[]{:S(2)}) %copy-start.2) | copy-done | bytes 147480
  1.9 0.0 copy-start.7
  1.9 0.0 copy-start.6
  1.9 3.0 %collective-permute-start = (f32[6,2,1024]{2,1,0:T(2,128)S(1)}, f32[6,2,1024]{2,1,0:T(2,128)S(1)}, u32[]{:S(2)}, u32[]{:S(2)}) collective-permute-start(f32[6,2,1024]{2,1,0:T(2,128)S(1)} %edges.1), channel_id=1, source_target_pairs={{0,1},{1,3},{2,0},{3,5},{4,2},{5,7},{6,4},{7,9},{8,6},{9,11},{10,8... | collective-permute-start | bytes 147464 | tf_op jit(solution)/shard_map/ppermute | solution.py:382
  4.9 0.0 copy-done.7
  4.9 0.0 copy-done.6
  4.9 0.0 copy-start.4
  4.9 1.1 %copy-done.4 = f32[24,24,256]{2,1,0:T(8,128)S(1)} copy-done((f32[24,24,256]{2,1,0:T(8,128)S(1)}, f32[24,24,256]{2,1,0:T(8,128)}, u32[]{:S(2)}) %copy-start.4) | copy-done | bytes 589848
  6.0 0.0 copy-start.1
  6.0 0.0 copy-start.3
  6.0 0.3 %prepare.1 = (f32[12,512]{1,0:T(8,128)S(1)}, f32[2,2,24,512]{3,2,1,0:T(8,128)S(1)}, f32[4,24,512]{2,1,0:T(8,128)S(1)}, f32[10,24,128]{2,1,0:T(8,128)S(1)}) custom-call(f32[2,5,24]{2,1,0:T(8,128)S(1)} %copy.6.bands, f32[2,2,24,256]{3,2,1,0:T(8,128)S(1)} %copy-done.6, f32[24,24,256]{2,1,0:T(8,128)S(1)} %copy-done.4), custom_call_target="tpu_custom_call" | custom-call | flops 200000000 | bytes 689088 | tf_op jit(solution)/shard_map/prepare/pallas_call | solution.py:19
  6.3 0.4 %collective-permute-done.halo = f32[6,2,1024]{2,1,0:T(2,128)S(1)} collective-permute-done((f32[6,2,1024]{2,1,0:T(2,128)S(1)}, f32[6,2,1024]{2,1,0:T(2,128)S(1)}, u32[]{:S(2)}, u32[]{:S(2)}) %collective-permute-start) | collective-permute-done | bytes 49184 | tf_op jit(solution)/shard_map/ppermute | solution.py:382
  6.7 0.2 copy-done.1
  6.9 0.1 copy-done.3
  7.0 0.0 copy-start.5
  7.0 0.4 %stencil.1 = (f32[56,512]{1,0:T(8,128)S(1)}, f32[56,512]{1,0:T(8,128)S(1)}) custom-call(f32[3,12,1024]{2,1,0:T(8,128)S(1)} %copy-done.1, f32[3,12,1024]{2,1,0:T(8,128)S(1)} %copy-done.3, f32[6,2,1024]{2,1,0:T(2,128)S(1)} %collective-permute-done.halo, f32[10,24,128]{2,1,0:T(8,128)S(1)} %get-tuple-element.15.coef), custom_call_target="tpu_custom_call" | custom-call | bytes 466944 | tf_op jit(solution)/shard_map/stencil/pallas_call | solution.py:19
  7.4 2.1 %collective-permute-start.1 = (f32[56,512]{1,0:T(8,128)S(1)}, f32[56,512]{1,0:T(8,128)S(1)}, u32[]{:S(2)}, u32[]{:S(2)}) collective-permute-start(f32[56,512]{1,0:T(8,128)S(1)} %get-tuple-element.17), channel_id=1, source_target_pairs={{0,1},{1,0},{2,3},{3,2},{4,5},{5,4},{6,7},{7,6},{8,9},{9,8},{10,11... | collective-permute-start | bytes 344072 | tf_op jit(solution)/shard_map/ppermute | solution.py:402
  9.5 2.9 %collective-permute-done.1.refs_1_ = f32[56,512]{1,0:T(8,128)S(1)} collective-permute-done((f32[56,512]{1,0:T(8,128)S(1)}, f32[56,512]{1,0:T(8,128)S(1)}, u32[]{:S(2)}, u32[]{:S(2)}) %collective-permute-start.1) | collective-permute-done | bytes 114720 | tf_op jit(solution)/shard_map/ppermute | solution.py:402
  12.4 0.2 interface.1
  12.6 0.1 collective-permute-start.2
  12.7 1.2 %collective-permute-done.2.refs_1_ = f32[24,512]{1,0:T(8,128)S(1)} collective-permute-done((f32[24,512]{1,0:T(8,128)S(1)}, f32[24,512]{1,0:T(8,128)S(1)}, u32[]{:S(2)}, u32[]{:S(2)}) %collective-permute-start.2) | collective-permute-done | bytes 49184 | tf_op jit(solution)/shard_map/ppermute | solution.py:416
  13.9 0.1 compose.2.refs_0_
  13.9 2.6 %collective-permute-start.5 = (f32[24,512]{1,0:T(8,128)S(1)}, f32[24,512]{1,0:T(8,128)S(1)}, u32[]{:S(2)}, u32[]{:S(2)}) collective-permute-start(f32[24,512]{1,0:T(8,128)S(1)} %compose.2.refs_0_), channel_id=1, source_target_pairs={{0,14},{2,12},{4,10},{6,8},{8,6},{10,4},{12,2},{14,0},{16,30},{18,... | collective-permute-start | bytes 147464 | tf_op jit(solution)/shard_map/ppermute | solution.py:416
  16.5 0.4 %collective-permute-start.4 = (f32[24,512]{1,0:T(8,128)S(1)}, f32[24,512]{1,0:T(8,128)S(1)}, u32[]{:S(2)}, u32[]{:S(2)}) collective-permute-start(f32[24,512]{1,0:T(8,128)S(1)} %compose.2.refs_0_), channel_id=1, source_target_pairs={{0,10},{2,8},{4,14},{6,12},{8,2},{10,0},{12,6},{14,4},{16,26},{18,... | collective-permute-start | bytes 147464 | tf_op jit(solution)/shard_map/ppermute | solution.py:416
  16.9 0.2 collective-permute-start.3
  17.1 1.5 %collective-permute-done.5.refs_3_ = f32[24,512]{1,0:T(8,128)S(1)} collective-permute-done((f32[24,512]{1,0:T(8,128)S(1)}, f32[24,512]{1,0:T(8,128)S(1)}, u32[]{:S(2)}, u32[]{:S(2)}) %collective-permute-start.5) | collective-permute-done | bytes 49184 | tf_op jit(solution)/shard_map/ppermute | solution.py:416
  18.6 1.4 %collective-permute-done.4.refs_2_ = f32[24,512]{1,0:T(8,128)S(1)} collective-permute-done((f32[24,512]{1,0:T(8,128)S(1)}, f32[24,512]{1,0:T(8,128)S(1)}, u32[]{:S(2)}, u32[]{:S(2)}) %collective-permute-start.4) | collective-permute-done | bytes 49184 | tf_op jit(solution)/shard_map/ppermute | solution.py:416
  20.0 0.6 %collective-permute-done.3.refs_1_ = f32[24,512]{1,0:T(8,128)S(1)} collective-permute-done((f32[24,512]{1,0:T(8,128)S(1)}, f32[24,512]{1,0:T(8,128)S(1)}, u32[]{:S(2)}, u32[]{:S(2)}) %collective-permute-start.3) | collective-permute-done | bytes 49184 | tf_op jit(solution)/shard_map/ppermute | solution.py:416
  20.6 0.1 compose.3.refs_0_
  20.7 2.4 %collective-permute-start.6 = (f32[24,512]{1,0:T(8,128)S(1)}, f32[24,512]{1,0:T(8,128)S(1)}, u32[]{:S(2)}, u32[]{:S(2)}) collective-permute-start(f32[24,512]{1,0:T(8,128)S(1)} %compose.3.refs_0_), channel_id=1, source_target_pairs={{0,18},{2,16},{4,22},{6,20},{8,26},{10,24},{12,30},{14,28},{16,2},... | collective-permute-start | bytes 147464 | tf_op jit(solution)/shard_map/ppermute | solution.py:416
  23.2 0.0 copy-done.5
  23.2 0.9 %block.1.local = f32[3,24,512]{2,1,0:T(8,128)S(1)} custom-call(f32[24,24,256]{2,1,0:T(8,128)S(1)} %copy-done.5, f32[3,24,512]{2,1,0:T(8,128)S(1)} %get-tuple-element.18.rhs), custom_call_target="tpu_custom_call" | custom-call | flops 200000000 | bytes 737280 | tf_op jit(solution)/shard_map/block/pallas_call | solution.py:19
  24.1 0.1 widen.2.refs_4_
  24.2 0.2 widen.3.refs_2_
  24.4 1.1 %collective-permute-done.6.refs_1_ = f32[24,512]{1,0:T(8,128)S(1)} collective-permute-done((f32[24,512]{1,0:T(8,128)S(1)}, f32[24,512]{1,0:T(8,128)S(1)}, u32[]{:S(2)}, u32[]{:S(2)}) %collective-permute-start.6) | collective-permute-done | bytes 49184 | tf_op jit(solution)/shard_map/ppermute | solution.py:416
  25.5 0.8 %final.1 = f32[3,24,512]{2,1,0:T(8,128)} custom-call(f32[3,24,512]{2,1,0:T(8,128)S(1)} %block.1.local, f32[2,2,24,512]{3,2,1,0:T(8,128)S(1)} %get-tuple-element.19.lu, f32[24,512]{1,0:T(8,128)S(1)} %compose.3.refs_0_, f32[24,512]{1,0:T(8,128)S(1)} %collective-permute-done.6.refs_1_, f32[24,512]{1,0:T(8,128)S(1)} %widen.3.refs_2_), custom_call_target="tpu_custom_call" | custom-call | bytes 491520 | tf_op jit(solution)/shard_map/final/pallas_call | solution.py:19
  (2 shorter events, 0.0 us)
Async XLA Ops:
  0.0 0.9 %copy-start = (f32[3,12,1024]{2,1,0:T(8,128)S(1)}, f32[3,12,1024]{2,1,0:T(8,128)}, u32[]{:S(2)}) copy-start(f32[3,12,1024]{2,1,0:T(8,128)} %velocity.3) | copy-start | bytes 442372
  0.9 0.9 %copy-start.2 = (f32[3,12,1024]{2,1,0:T(8,128)S(1)}, f32[3,12,1024]{2,1,0:T(8,128)}, u32[]{:S(2)}) copy-start(f32[3,12,1024]{2,1,0:T(8,128)} %explicit.3) | copy-start | bytes 442372
  1.9 3.1 %copy-start.7 = (f32[2,5,24]{2,0,1:T(2,128)S(1)}, f32[2,5,24]{2,0,1:T(2,128)}, u32[]{:S(2)}) copy-start(f32[2,5,24]{2,0,1:T(2,128)} %param.7) | copy-start | bytes 2884
  1.9 3.1 %copy-start.6 = (f32[2,2,24,256]{3,2,1,0:T(8,128)S(1)}, f32[2,2,24,256]{3,2,1,0:T(8,128)}, u32[]{:S(2)}) copy-start(f32[2,2,24,256]{3,2,1,0:T(8,128)} %spikes.1) | copy-start | bytes 294916
  1.9 4.8 %collective-permute-start = (f32[6,2,1024]{2,1,0:T(2,128)S(1)}, f32[6,2,1024]{2,1,0:T(2,128)S(1)}, u32[]{:S(2)}, u32[]{:S(2)}) collective-permute-start(f32[6,2,1024]{2,1,0:T(2,128)S(1)} %edges.1), channel_id=1, source_target_pairs={{0,1},{1,3},{2,0},{3,5},{4,2},{5,7},{6,4},{7,9},{8,6},{9,11},{10,8... | collective-permute-start | bytes 147464 | tf_op jit(solution)/shard_map/ppermute | solution.py:382
  4.9 1.1 %copy-start.4 = (f32[24,24,256]{2,1,0:T(8,128)S(1)}, f32[24,24,256]{2,1,0:T(8,128)}, u32[]{:S(2)}) copy-start(f32[24,24,256]{2,1,0:T(8,128)} %inverse.3) | copy-start | bytes 1769476
  6.0 0.9 %copy-start.1 = (f32[3,12,1024]{2,1,0:T(8,128)S(1)}, f32[3,12,1024]{2,1,0:T(8,128)}, u32[]{:S(2)}) copy-start(f32[3,12,1024]{2,1,0:T(8,128)} %velocity.3) | copy-start | bytes 442372
  6.0 1.0 %copy-start.3 = (f32[3,12,1024]{2,1,0:T(8,128)S(1)}, f32[3,12,1024]{2,1,0:T(8,128)}, u32[]{:S(2)}) copy-start(f32[3,12,1024]{2,1,0:T(8,128)} %explicit.3) | copy-start | bytes 442372
  7.0 16.1 %copy-start.5 = (f32[24,24,256]{2,1,0:T(8,128)S(1)}, f32[24,24,256]{2,1,0:T(8,128)}, u32[]{:S(2)}) copy-start(f32[24,24,256]{2,1,0:T(8,128)} %inverse.3) | copy-start | bytes 1769476
  7.4 5.0 %collective-permute-start.1 = (f32[56,512]{1,0:T(8,128)S(1)}, f32[56,512]{1,0:T(8,128)S(1)}, u32[]{:S(2)}, u32[]{:S(2)}) collective-permute-start(f32[56,512]{1,0:T(8,128)S(1)} %get-tuple-element.17), channel_id=1, source_target_pairs={{0,1},{1,0},{2,3},{3,2},{4,5},{5,4},{6,7},{7,6},{8,9},{9,8},{10,11... | collective-permute-start | bytes 344072 | tf_op jit(solution)/shard_map/ppermute | solution.py:402
  12.6 1.3 %collective-permute-start.2 = (f32[24,512]{1,0:T(8,128)S(1)}, f32[24,512]{1,0:T(8,128)S(1)}, u32[]{:S(2)}, u32[]{:S(2)}) collective-permute-start(f32[24,512]{1,0:T(8,128)S(1)} %get-tuple-element.20.refs_0_), channel_id=1, source_target_pairs={{0,2},{2,0},{4,6},{6,4},{8,10},{10,8},{12,14},{14,12},{16,18},{18,... | collective-permute-start | bytes 147464 | tf_op jit(solution)/shard_map/ppermute | solution.py:416
  13.9 4.7 %collective-permute-start.5 = (f32[24,512]{1,0:T(8,128)S(1)}, f32[24,512]{1,0:T(8,128)S(1)}, u32[]{:S(2)}, u32[]{:S(2)}) collective-permute-start(f32[24,512]{1,0:T(8,128)S(1)} %compose.2.refs_0_), channel_id=1, source_target_pairs={{0,14},{2,12},{4,10},{6,8},{8,6},{10,4},{12,2},{14,0},{16,30},{18,... | collective-permute-start | bytes 147464 | tf_op jit(solution)/shard_map/ppermute | solution.py:416
  16.5 3.5 %collective-permute-start.4 = (f32[24,512]{1,0:T(8,128)S(1)}, f32[24,512]{1,0:T(8,128)S(1)}, u32[]{:S(2)}, u32[]{:S(2)}) collective-permute-start(f32[24,512]{1,0:T(8,128)S(1)} %compose.2.refs_0_), channel_id=1, source_target_pairs={{0,10},{2,8},{4,14},{6,12},{8,2},{10,0},{12,6},{14,4},{16,26},{18,... | collective-permute-start | bytes 147464 | tf_op jit(solution)/shard_map/ppermute | solution.py:416
  16.9 3.7 %collective-permute-start.3 = (f32[24,512]{1,0:T(8,128)S(1)}, f32[24,512]{1,0:T(8,128)S(1)}, u32[]{:S(2)}, u32[]{:S(2)}) collective-permute-start(f32[24,512]{1,0:T(8,128)S(1)} %compose.2.refs_0_), channel_id=1, source_target_pairs={{0,6},{2,4},{4,2},{6,0},{8,14},{10,12},{12,10},{14,8},{16,22},{18,... | collective-permute-start | bytes 147464 | tf_op jit(solution)/shard_map/ppermute | solution.py:416
  20.7 4.7 %collective-permute-start.6 = (f32[24,512]{1,0:T(8,128)S(1)}, f32[24,512]{1,0:T(8,128)S(1)}, u32[]{:S(2)}, u32[]{:S(2)}) collective-permute-start(f32[24,512]{1,0:T(8,128)S(1)} %compose.3.refs_0_), channel_id=1, source_target_pairs={{0,18},{2,16},{4,22},{6,20},{8,26},{10,24},{12,30},{14,28},{16,2},... | collective-permute-start | bytes 147464 | tf_op jit(solution)/shard_map/ppermute | solution.py:416

commit v2 on v1

v2 whole, which is shorter than its diff:
```python
import functools

import jax
import jax.numpy as jnp
from jax import lax
from jax.experimental import pallas as pl
from jax.experimental.pallas import tpu as pltpu
from jax.sharding import PartitionSpec as P

F32 = jnp.float32
BF16 = jnp.bfloat16
LANES = 128
HALO = 2


def vmem_call(body, out_shapes, args, scratch=(), flops=0, name=None, far=0, far_out=False):
    near, away = pl.BlockSpec(memory_space=pltpu.VMEM), pl.BlockSpec(memory_space=pltpu.HBM)
    nbytes = sum(a.size * 4 for a in args)
    args = [pltpu.with_memory_space_constraint(a, pltpu.HBM) for a in args[:far]] + args[far:]
    return pl.pallas_call(
        body,
        out_shape=[jax.ShapeDtypeStruct(s, F32) for s in out_shapes],
        in_specs=[away] * far + [near] * (len(args) - far),
        out_specs=[away if far_out else near] * len(out_shapes),
        scratch_shapes=list(scratch),
        compiler_params=pltpu.CompilerParams(vmem_limit_bytes=16 * 2**20),
        cost_estimate=pl.CostEstimate(flops=flops, bytes_accessed=nbytes, transcendentals=0),
        name=name,
    )(*args)


def window(rows, own, groups):
    spans = [(max(g * own - HALO, 0), min(g * own + own + HALO, rows)) for g in range(groups)]
    wide = max(high - low for low, high in spans)
    return wide, [min(low, rows - wide) for low, _ in spans]


def exact_parts(x):
    high = x.astype(BF16)
    rest = x - high.astype(F32)
    mid = rest.astype(BF16)
    low = (rest - mid.astype(F32)).astype(BF16)
    return high, mid, low


def by_ones(x, ones):
    high, mid, low = exact_parts(x)
    dot = functools.partial(jnp.dot, preferred_element_type=F32)
    return dot(high, ones) + (dot(mid, ones) + dot(low, ones))


def doubled(x):
    row = lax.broadcasted_iota(jnp.int32, (LANES, 2 * LANES), 0)
    col = lax.broadcasted_iota(jnp.int32, (LANES, 2 * LANES), 1)
    ones = (row == lax.shift_right_logical(col, 1)).astype(F32).astype(BF16)
    parts = [by_ones(x[:, i : i + LANES], ones) for i in range(0, x.shape[1], LANES)]
    return jnp.concatenate(parts, axis=1)


def interleave_ones(back):
    a = lax.broadcasted_iota(jnp.int32, (2 * LANES, 2 * LANES), 1 if back else 0)
    b = lax.broadcasted_iota(jnp.int32, (2 * LANES, 2 * LANES), 0 if back else 1)
    place = 2 * (b % LANES) + b // LANES
    return (a == place).astype(F32).astype(BF16)


def side_weights(coef, upper):
    rows = coef.shape[1]
    if upper:
        taps = [[(4, rows - 2), None], [(3, rows - 1), (4, rows - 1)]]
    else:
        taps = [[(0, 0), (1, 0)], [None, (0, 1)]]
    none = jnp.zeros((1, LANES), F32)
    get = lambda tap, kind: none if tap is None else coef[2 * tap[0] + kind, tap[1] : tap[1] + 1]
    return [[[get(tap, kind) for kind in range(2)] for tap in row] for row in taps]


def beside(weights, planes):
    return [
        sum(weights[i][j][kind] * planes(kind, j) for j in range(2) for kind in range(2)) for i in range(2)
    ]


def planes_of(ref, at):
    return lambda kind, j: ref[at + 6 * kind + 3 * j : at + 6 * kind + 3 * j + 3]


def stencil_kernel(wide, firsts, velocity, explicit, bands, *refs):
    groups = len(firsts)
    outs, (edges, coef, here, there, taps, square, weight, vel, tot, sems) = refs[:groups], refs[groups:]
    own, lanes = velocity.shape[1:]
    rows = coef.shape[1]
    part = lanes // groups
    g = lax.axis_index("gz")
    copies = [
        pltpu.make_async_copy(source, target, sems.at[i])
        for i, (source, target) in enumerate(((bands, taps), (velocity, here), (explicit, there)))
    ]
    for copy in copies:
        copy.start()
    square[...] = jnp.zeros_like(square)
    vel[...] = jnp.zeros_like(vel)
    tot[...] = jnp.zeros_like(tot)
    copies[0].wait()
    for d in range(5):
        square[2 * d : 2 * d + 2, 0:rows] = taps[d]
    turned = jnp.transpose(square[...])
    for i in range(10):
        coef[i] = jnp.broadcast_to(turned[0:rows, i : i + 1], (rows, LANES))
    copies[1].wait()
    copies[2].wait()
    for k in range(groups):
        base = 8 + k * own - firsts[k]

        @pl.when(g == k)
        def _(base=base, first=firsts[k]):
            for i in range(10):
                weight[i] = coef[i, first : first + wide]
            for f in range(3):
                vel[f, base : base + own] = here[f]
                tot[f, base : base + own] = here[f] + there[f]

    for f in range(3):
        for j in range(HALO):
            top, bottom = here[f, j : j + 1], here[f, own - HALO + j : own - HALO + j + 1]
            edges[6 + 3 * j + f : 7 + 3 * j + f] = jnp.where(g == 0, top, bottom)
            top += there[f, j : j + 1]
            bottom += there[f, own - HALO + j : own - HALO + j + 1]
            edges[3 * j + f : 3 * j + f + 1] = jnp.where(g == 0, top, bottom)
    weights = [weight[i] for i in range(10)]
    for shift in range(groups - 1, -1, -1):
        out = outs[shift]
        begin = lax.rem(g + shift, groups) * part
        for lane in range(0, part, LANES):
            at = pl.ds(pl.multiple_of(begin + lane, LANES), LANES)
            to = pl.ds(lane, LANES)
            for f in range(3):
                total = None
                for d in range(5):
                    low = pl.ds(8 + d - 2, wide)
                    term = weights[2 * d] * tot[f, low, at] + weights[2 * d + 1] * vel[f, low, at]
                    total = term if total is None else total + term
                out[f * wide : f * wide + wide, to] = total
            out[3 * wide : 3 * wide + 12, to] = edges[0:12, at]


def relay_kernel(groups, edges, beside_edges, *outs):
    core = lax.rem(lax.axis_index("gy"), 2)
    mine = jnp.where(lax.axis_index("gz") == 0, core == 0, core == 1)
    part = edges.shape[1] // groups
    for step, out in enumerate(outs):
        begin = (2 * step + 1 - core) * part
        for lane in range(0, part, LANES):
            at = pl.ds(pl.multiple_of(begin + lane, LANES), LANES)
            out[:, lane : lane + LANES] = jnp.where(mine, edges[:, at], beside_edges[:, at])


def prepare_kernel(spikes, inverse, coef, lu, inv4, fixed, outer, inside, near, sems):
    rows = inverse.shape[1]
    lanes = lu.shape[3]
    core = lax.rem(lax.axis_index("gy"), 2)
    gy, count = lax.axis_index("gy"), lax.axis_size("gy")
    copies = [
        pltpu.make_async_copy(spikes, near, sems.at[0]),
        pltpu.make_async_copy(inverse, inside, sems.at[1]),
    ]
    for copy in copies:
        copy.start()
    wide = lambda row: jnp.concatenate([row] * (lanes // LANES), axis=1)
    lower, upper = side_weights(coef, False), side_weights(coef, True)
    used = jnp.where(core == 0, gy > 0, gy < count - 1)
    for i in range(2):
        for j in range(2):
            for kind in range(2):
                at = 4 * i + 2 * j + kind
                low, high = lower[i][j][kind], upper[i][j][kind]
                fixed[20 + at : 21 + at] = wide(jnp.where(core == 0, high, low))
                outer[at : at + 1] = wide(jnp.where(used, jnp.where(core == 0, low, high), 0.0))
    copies[0].wait()
    lu[...] = doubled(near[...].reshape(4 * rows, -1)).reshape(lu.shape)
    for k in range(2):
        for j in range(2):
            fixed[2 * k + j : 2 * k + j + 1] = -lu[0, j, rows - 2 + k : rows - 1 + k]
            fixed[4 + 2 * k + j : 5 + 2 * k + j] = -lu[0, j, k : k + 1]
            fixed[8 + 2 * k + j : 9 + 2 * k + j] = -lu[1, j, k : k + 1]
    copies[1].wait()
    ends = jnp.concatenate([inside[0:2], inside[rows - 2 : rows]], axis=0)
    inv4[...] = doubled(ends.reshape(4 * rows, -1)).reshape(inv4.shape)
    for k in range(4):
        for i in range(2):
            low, high = inv4[k, i : i + 1], inv4[k, rows - 2 + i : rows - 1 + i]
            at = 12 + 2 * ((k + 2) % 4) + i
            fixed[at : at + 1] = jnp.where(core == 0, high, low)


def rows_of(ref, at):
    return [[[ref[at + 4 * i + 2 * j + kind : at + 4 * i + 2 * j + kind + 1] for kind in range(2)] for j in range(2)] for i in range(2)]


def interface_kernel(wide, firsts, inv4, fixed, outer, *refs):
    groups = len(firsts)
    pieces, ends, (rhs, message) = refs[:groups], refs[groups:-2], refs[-2:]
    rows = rhs.shape[1]
    g = lax.axis_index("gz")
    core = lax.rem(lax.axis_index("gy"), 2)
    rhs[...] = jnp.zeros_like(rhs)
    for shift, piece in enumerate(pieces):
        source = lax.rem(g - shift + groups, groups)
        for k in range(groups):

            @pl.when(source == k)
            def _(piece=piece, k=k):
                for f in range(3):
                    rhs[f, firsts[k] : firsts[k] + wide] += piece[f * wide : f * wide + wide]
                if k in (0, groups - 1):

                    @pl.when(core == (1 if k == 0 else 0))
                    def _():
                        message[24:36] = piece[3 * wide : 3 * wide + 12]

    end = ends[0][...]
    for step in range(1, len(ends)):
        end = jnp.where(g // 2 == step, ends[step][...], end)
    side = beside(rows_of(outer, 0), lambda kind, j: end[6 * kind + 3 * j : 6 * kind + 3 * j + 3])
    low = [jnp.where(core == 0, side[i], 0.0) for i in range(2)]
    high = [jnp.where(core == 0, 0.0, side[i]) for i in range(2)]
    for f in range(3):
        for i in range(2):
            rhs[f, i : i + 1] += low[i][f : f + 1]
            rhs[f, rows - 2 + i : rows - 1 + i] += high[i][f : f + 1]
    for f in range(3):
        for r in range(4):
            value = jnp.sum(inv4[r] * rhs[f], axis=0, keepdims=True)
            row = (6 if r < 2 else 0) + 3 * (r % 2) + f
            message[row : row + 1] = value
    message[12:24] = fixed[0:12]
    message[36:52] = fixed[12:28]


class Piece:
    def __init__(self, ref):
        self.p = [ref[0:3], ref[3:6]]
        self.q = [ref[6:9], ref[9:12]]
        grid = lambda at: [[ref[at + 2 * k + j : at + 2 * k + j + 1] for j in range(2)] for k in range(2)]
        self.F, self.H, self.G = grid(12), grid(16), grid(20)


def act(matrix, vector, plus=None):
    out = [matrix[k][0] * vector[0] + matrix[k][1] * vector[1] for k in range(2)]
    return out if plus is None else [plus[k] + out[k] for k in range(2)]


def times(a, b, plus=None):
    out = [[a[k][0] * b[0][j] + a[k][1] * b[1][j] for j in range(2)] for k in range(2)]
    return out if plus is None else [[plus[k][j] + out[k][j] for j in range(2)] for k in range(2)]


def after(state, piece):
    if state is None:
        return piece.p, piece.F
    return act(piece.F, state[0], piece.p), times(piece.F, state[1])


def before(piece, state):
    if state is None:
        return piece.q, piece.H, piece.G
    q, H, G = state
    q = act(piece.G, act(H, piece.p, q), piece.q)
    H = times(piece.G, times(H, piece.F), piece.H)
    return q, H, times(piece.G, G)


def choose(flag, new, old):
    return jax.tree.map(lambda a, b: jnp.where(flag, a, b), new, old)


def store_vector(ref, at, vector):
    ref[at : at + 3] = vector[0]
    ref[at + 3 : at + 6] = vector[1]


def store_matrix(ref, at, matrix):
    for k in range(2):
        for j in range(2):
            ref[at + 2 * k + j : at + 2 * k + j + 1] = matrix[k][j]


def sorted_pieces(base, pieces, board):
    size = len(pieces)
    position = lax.rem(lax.div(lax.axis_index("gy"), base), size)
    for x, piece in enumerate(pieces):
        board[jnp.bitwise_xor(position, x)] = piece[...]
    return position, [Piece(board.at[i]) for i in range(size)]


def compose_kernel(base, *refs):
    *pieces, out, board = refs
    _, run = sorted_pieces(base, pieces, board)
    up = down = None
    for piece in run:
        up = after(up, piece)
    for piece in run[::-1]:
        down = before(piece, down)
    store_vector(out, 0, up[0])
    store_vector(out, 6, down[0])
    store_matrix(out, 12, up[1])
    store_matrix(out, 16, down[1])
    store_matrix(out, 20, down[2])


def pair_kernel(mine, other, out, fixed_mine, fixed_other):
    core = lax.rem(lax.axis_index("gy"), 2)
    both = []
    for ref, near, target in ((mine, other, fixed_mine), (other, mine, fixed_other)):
        side = beside(rows_of(ref, 44), planes_of(near, 24))
        target[12:24] = ref[12:24]
        for k in range(4):
            value = ref[3 * k : 3 * k + 3]
            for i in range(2):
                value = value + ref[36 + 2 * k + i : 37 + 2 * k + i] * side[i]
            target[3 * k : 3 * k + 3] = value
    low, high = (
        [jnp.where(core == i, fixed_mine[...], fixed_other[...])] for i in range(2)
    )
    low, high = Piece(low[0]), Piece(high[0])
    up, down = after(after(None, low), high), before(low, before(high, None))
    store_vector(out, 0, up[0])
    store_vector(out, 6, down[0])
    store_matrix(out, 12, up[1])
    store_matrix(out, 16, down[1])
    store_matrix(out, 20, down[2])


def around(base, pieces, board):
    position, run = sorted_pieces(base, pieces, board)
    mine = Piece(pieces[0])
    one, none = jnp.ones_like(mine.F[0][0]), jnp.zeros_like(mine.F[0][0])
    zero = jnp.zeros_like(mine.p[0])
    unit = [[one, none], [none, one]]
    blank = [[none, none], [none, none]]
    up = ([zero, zero], unit)
    for i, piece in enumerate(run[:-1]):
        up = choose(i < position, after(up, piece), up)
    down = ([zero, zero], blank, unit)
    for i in range(len(run) - 1, 0, -1):
        down = choose(i > position, before(run[i], down), down)
    return mine, up, down


def widen(base, pieces, board, known):
    mine, (pl_, Fl), (q, H, G) = around(base, pieces, board)
    top = act(mine.F, pl_, mine.p)
    e = act(H, top, q)
    E = times(H, times(mine.F, Fl))
    if known is None:
        return pl_, Fl, e, E, G
    a, A, b, B, D = known
    return (
        act(A, pl_, a),
        times(A, Fl),
        act(D, e, act(B, pl_, b)),
        times(D, E, times(B, Fl)),
        times(D, G),
    )


def read_known(ref):
    piece = Piece(ref)
    return piece.p, piece.F, piece.q, piece.H, piece.G


def widen_kernel(base, start, *refs):
    *pieces, out, board = refs
    known = None
    if not start:
        known = read_known(pieces.pop())
    a, A, b, B, D = widen(base, pieces, board, known)
    store_vector(out, 0, a)
    store_vector(out, 6, b)
    store_matrix(out, 12, A)
    store_matrix(out, 16, B)
    store_matrix(out, 20, D)


def block_kernel(inverse, rhs, mine, other, local, split, solved):
    fields, rows, lanes = rhs.shape
    core = lax.rem(lax.axis_index("gy"), 2)
    side = beside(rows_of(mine, 44), planes_of(other, 24))
    local[...] = rhs[...]
    for f in range(fields):
        for i in range(2):
            value = side[i][f : f + 1]
            local[f, i : i + 1] += jnp.where(core == 0, 0.0, value)
            local[f, rows - 2 + i : rows - 1 + i] += jnp.where(core == 0, value, 0.0)
    apart, together = interleave_ones(False), interleave_ones(True)
    flat = local[...].reshape(fields * rows, lanes)
    for at in range(0, lanes, 2 * LANES):
        turned = by_ones(flat[:, at : at + 2 * LANES], apart)
        split[:, :, at : at + 2 * LANES] = turned.reshape(fields, rows, 2 * LANES)
    for tile in range(lanes // (2 * LANES)):
        modes = pl.ds(tile * LANES, LANES)
        for f in range(fields):
            for p in range(2):
                at = pl.ds((2 * tile + p) * LANES, LANES)
                value = split[f, :, at]
                solved[f, :, at] = jnp.sum(inverse[:, :, modes] * value[None], axis=1)
    flat = solved[...].reshape(fields * rows, lanes)
    for at in range(0, lanes, 2 * LANES):
        turned = by_ones(flat[:, at : at + 2 * LANES], together)
        local[:, :, at : at + 2 * LANES] = turned.reshape(fields, rows, 2 * LANES)


def last_message_kernel(base, composed, out):
    upper = lax.rem(lax.div(lax.axis_index("gy"), base), 2) == 1
    out[0:6] = jnp.where(upper, composed[6:12], composed[0:6])
    out[6:10] = composed[16:20]


def ready_kernel(base, local, lu, known, ready, lift):
    upper = lax.rem(lax.div(lax.axis_index("gy"), base), 2) == 1
    a, A, b, B, D = read_known(known)
    for f in range(3):
        value = local[f]
        for k in range(2):
            value = value - lu[0, k] * a[k][f : f + 1] - lu[1, k] * b[k][f : f + 1]
        ready[f] = value
    for j in range(2):
        value = jnp.zeros_like(lift[j])
        for k in range(2):
            through_t = lu[0, k] * A[k][j] + lu[1, k] * B[k][j]
            value = value - jnp.where(upper, through_t, lu[1, k] * D[k][j])
        lift[j] = value


def final_kernel(base, ready, lift, composed, received, out, held, sems):
    upper = lax.rem(lax.div(lax.axis_index("gy"), base), 2) == 1
    mine = [composed[0:3], composed[3:6]]
    theirs = [received[0:3], received[3:6]]
    H = [[received[6 + 2 * k + j : 7 + 2 * k + j] for j in range(2)] for k in range(2)]
    state = choose(upper, theirs, act(H, mine, theirs))
    copies = []
    for f in range(3):
        held[f] = ready[f] + lift[0] * state[0][f : f + 1] + lift[1] * state[1][f : f + 1]
        copies.append(pltpu.make_async_copy(held.at[f], out.at[f], sems.at[f]))
        copies[-1].start()
    for copy in copies:
        copy.wait()


def end_pairs(gy, gz, step):
    at = lambda y, z: y * gz + z
    pairs = []
    for y in range(1, gy - 1, 2):
        pairs.append((at(y, gz - 1), at(y + 1, 2 * step)))
        pairs.append((at(y - 1, gz - 1), at(y + 1, 2 * step + 1)))
        pairs.append((at(y + 1, 0), at(y, 2 * step + 1)))
        pairs.append((at(y + 2, 0), at(y, 2 * step)))
    sources = sorted(set(range(gy * gz)) - {s for s, _ in pairs})
    targets = sorted(set(range(gy * gz)) - {t for _, t in pairs})
    if gz == 2:
        for i in range(0, len(sources), 2):
            pairs += [(sources[i], targets[i + 1]), (sources[i + 1], targets[i])]
    return pairs


def groups_of(count):
    steps, base = [(1, 2)], 2
    while 2 * base < count:
        size = 4 if base * 8 <= count else 2
        steps.append((base, size))
        base *= size
    return steps + [(base, 2)]


def per_device(velocity, explicit, bands, inverse, spikes):
    gy, gz = lax.axis_size("gy"), lax.axis_size("gz")
    own, columns = velocity.shape[1:]
    rows, modes = inverse.shape[0], inverse.shape[2]
    lanes = 2 * modes
    wide, firsts = window(rows, own, gz)
    vmem = lambda *shape: pltpu.VMEM(shape, F32)
    dma = lambda n: pltpu.SemaphoreType.DMA((n,))

    high = -(-(3 * wide + 12) // 8) * 8
    *shares, edges, coef = vmem_call(
        functools.partial(stencil_kernel, wide, firsts),
        [(high, lanes)] * gz + [(12, columns), (10, rows, LANES)],
        [velocity, explicit, jnp.transpose(bands, (1, 0, 2))],
        scratch=[vmem(3, own, columns)] * 2
        + [vmem(5, 2, rows), vmem(LANES, LANES), vmem(10, wide, LANES)]
        + [vmem(3, rows + 16, columns)] * 2
        + [dma(3)],
        name="stencil",
        far=3,
    )
    beside_edges = lax.ppermute(edges, "gy", [(i, i ^ 1) for i in range(gy)])
    pieces = [shares[0]]
    for shift in range(1, gz):
        ring = [(i, (i + shift) % gz) for i in range(gz)]
        pieces.append(lax.ppermute(shares[shift], "gz", ring))
    relays = vmem_call(
        functools.partial(relay_kernel, gz), [(12, lanes)] * (gz // 2), [edges, beside_edges], name="relay"
    )
    ends = [lax.ppermute(relay, ("gy", "gz"), end_pairs(gy, gz, step)) for step, relay in enumerate(relays)]
    lu, inv4, fixed, outer, inside = vmem_call(
        prepare_kernel,
        [(2, 2, rows, lanes), (4, rows, lanes), (28, lanes), (8, lanes), (rows, rows, modes)],
        [spikes, inverse, coef],
        scratch=[vmem(2, 2, rows, modes), dma(2)],
        flops=2 * 10**8,
        name="prepare",
        far=2,
    )
    rhs, message = vmem_call(
        functools.partial(interface_kernel, wide, firsts),
        [(3, rows, lanes), (56, lanes)],
        [inv4, fixed, outer, *pieces, *ends],
        name="interface",
    )
    other = lax.ppermute(message, "gy", [(i, i ^ 1) for i in range(gy)])
    composed, mine, theirs = vmem_call(pair_kernel, [(24, lanes)] * 3, [message, other], name="pair")

    steps = groups_of(gy)
    base, size = steps[0]
    (known,) = vmem_call(
        functools.partial(widen_kernel, base, True),
        [(24, lanes)],
        [mine, theirs],
        scratch=[vmem(size, 24, lanes)],
        flops=10**7,
        name="widen",
    )
    (local,) = vmem_call(
        block_kernel,
        [(3, rows, lanes)],
        [inside, rhs, message, other],
        scratch=[vmem(3, rows, lanes)] * 2,
        flops=2 * 10**8,
        name="block",
    )
    for base, size in steps[1:-1]:
        gathered = [composed]
        for x in range(1, size):
            gathered.append(lax.ppermute(composed, "gy", [(i, i ^ (x * base) ^ 1) for i in range(gy)]))
        board = [vmem(size, 24, lanes)]
        (composed,) = vmem_call(
            functools.partial(compose_kernel, base), [(24, lanes)], gathered, scratch=board, name="compose"
        )
        (known,) = vmem_call(
            functools.partial(widen_kernel, base, False),
            [(24, lanes)],
            [*gathered, known],
            scratch=board,
            flops=10**7,
            name="widen",
        )
    base, _ = steps[-1]
    (message,) = vmem_call(
        functools.partial(last_message_kernel, base), [(10, lanes)], [composed], name="last_message"
    )
    received = lax.ppermute(message, "gy", [(i, i ^ base ^ 1) for i in range(gy)])
    ready, lift = vmem_call(
        functools.partial(ready_kernel, base),
        [(3, rows, lanes), (2, rows, lanes)],
        [local, lu, known],
        flops=10**7,
        name="ready",
    )
    (out,) = vmem_call(
        functools.partial(final_kernel, base),
        [(3, rows, lanes)],
        [ready, lift, composed, received],
        scratch=[vmem(3, rows, lanes), dma(3)],
        name="final",
        far_out=True,
    )
    return out


def solution(mesh):
    placed = (
        P(None, ("gy", "gz"), None),
        P(None, ("gy", "gz"), None),
        P(None, None, "gy"),
        P("gy", None, "gz"),
        P(None, None, "gy", "gz"),
    )
    return jax.shard_map(
        per_device, mesh=mesh, in_specs=placed, out_specs=P(None, "gy", "gz"), check_vma=False
    )
```

time: 26.5 us -> 23.6 us (0.89)
  waiting for transfers between devices: 9.1 us -> 5.57 us
  local copies, waits for them, and re-layouts: 3.27 us -> 0 us
  Pallas kernels: 3.06 us -> 5.21 us
  starting transfers between devices: 10.8 us -> 12.5 us
    unnamed x17 -> x0, local copies, waits for them, and re-layouts: 3.27 us -> none
    ppermute x1, waiting for transfers between devices: 2.91 us -> 0.14 us  [per_device(): pieces.append(lax.ppermute(shares[shift], 'gz', ring))]
    pallas_call x10 -> x12, Pallas kernels: 3.06 us -> 5.21 us  [vmem_call(): pl.pallas_call(body, out_shape=[jax.ShapeDtypeStruct(s, F32) for s in out...]
    ppermute x1, starting transfers between devices: 2.07 us -> 3.04 us  [per_device(): pieces.append(lax.ppermute(shares[shift], 'gz', ring))]
    ppermute x6 -> x7, waiting for transfers between devices: 6.18 us -> 5.43 us  [the longest x3 2.64 us: per_device(): lax.ppermute(composed, 'gy', [(i, i ^ x * base ^ 1) for i in range(gy)])]
    ppermute x6 -> x7, starting transfers between devices: 8.7 us -> 9.43 us  [the longest x3 5.34 us: per_device(): lax.ppermute(composed, 'gy', [(i, i ^ x * base ^ 1) for i in range(gy)])]
  transfers between devices with their start and end apart: 7 -> 8, of which waited for: 7 -> 8; matrix products, arithmetic and copies ran while one was open for 0% -> 0% of each run, Pallas kernels for 6% -> 11%
where the time goes in v2:
time: 23.6 us; the launch traced here: 23.3 us
  starting transfers between devices  12.5 us (53%)
  waiting for transfers between devices  5.57 us (24%)
  Pallas kernels  5.21 us (22%)
    ppermute x3, starting transfers between devices, per_device(): lax.ppermute(composed, 'gy', [(i, i ^ x * base ^ 1) for i in range(gy)])  5.34 us
    pallas_call x12, Pallas kernels, vmem_call(): pl.pallas_call(body, out_shape=[jax.ShapeDtypeStruct(s, F32) for s in out...  5.21 us
    ppermute x1, starting transfers between devices, per_device(): pieces.append(lax.ppermute(shares[shift], 'gz', ring))  3.04 us
    ppermute x1, starting transfers between devices, per_device(): lax.ppermute(message, 'gy', [(i, i ^ base ^ 1) for i in range(gy)])  2.72 us
    ppermute x3, waiting for transfers between devices, per_device(): lax.ppermute(composed, 'gy', [(i, i ^ x * base ^ 1) for i in range(gy)])  2.64 us
    ppermute x1, waiting for transfers between devices, per_device(): beside_edges = lax.ppermute(edges, 'gy', [(i, i ^ 1) for i in range(gy)])  1.25 us
    ppermute x1, starting transfers between devices, per_device(): other = lax.ppermute(message, 'gy', [(i, i ^ 1) for i in range(gy)])  1.24 us
    ppermute x1, waiting for transfers between devices, per_device(): other = lax.ppermute(message, 'gy', [(i, i ^ 1) for i in range(gy)])  0.97 us
  transfers between devices with their start and end apart: 8, of which 8 were waited for; matrix products, arithmetic and copies ran while one was open for 0% of the time, Pallas kernels for 11%

profile of v2, /device:TPU:0, one launch (start us, length us, event | category | flops | bytes accessed | tf_op | source)
XLA Modules:
  0.0 23.3 jit_solution(3326199232751301870)
XLA Ops:
  0.0 1.4 %stencil.1 = (f32[56,512]{1,0:T(8,128)S(1)}, f32[56,512]{1,0:T(8,128)S(1)}, f32[12,1024]{1,0:T(8,128)S(1)}, f32[10,24,128]{2,1,0:T(8,128)S(1)}) custom-call(f32[3,12,1024]{2,1,0:T(8,128)} %velocity.1, f32[3,12,1024]{2,1,0:T(8,128)} %explicit.1, f32[5,2,24]{2,1,0:T(2,128)} %bitcast.1), custom_call_target="tpu_custom_call" | custom-call | bytes 295872 | tf_op jit(solution)/shard_map/stencil/pallas_call | solution.py:20
  1.4 3.0 %collective-permute-start = (f32[56,512]{1,0:T(8,128)S(1)}, f32[56,512]{1,0:T(8,128)S(1)}, u32[]{:S(2)}, u32[]{:S(2)}) collective-permute-start(f32[56,512]{1,0:T(8,128)S(1)} %get-tuple-element.27), channel_id=1, source_target_pairs={{0,1},{1,0},{2,3},{3,2},{4,5},{5,4},{6,7},{7,6},{8,9},{9,8},{10,11... | collective-permute-start | bytes 344072 | tf_op jit(solution)/shard_map/ppermute | solution.py:500
  4.4 0.0 collective-permute-start.1
  4.4 1.3 %collective-permute-done.1.beside_edges = f32[12,1024]{1,0:T(8,128)S(1)} collective-permute-done((f32[12,1024]{1,0:T(8,128)S(1)}, f32[12,1024]{1,0:T(8,128)S(1)}, u32[]{:S(2)}, u32[]{:S(2)}) %collective-permute-start.1) | collective-permute-done | bytes 49184 | tf_op jit(solution)/shard_map/ppermute | solution.py:496
  5.7 0.1 collective-permute-start.2
  5.8 1.4 %prepare.1 = (f32[2,2,24,512]{3,2,1,0:T(8,128)S(1)}, f32[4,24,512]{2,1,0:T(8,128)S(1)}, f32[28,512]{1,0:T(8,128)S(1)}, f32[8,512]{1,0:T(8,128)S(1)}, f32[24,24,256]{2,1,0:T(8,128)S(1)}) custom-call(f32[2,2,24,256]{3,2,1,0:T(8,128)} %spikes.1, f32[24,24,256]{2,1,0:T(8,128)} %inverse.1, f32[10,24,128]{2,1,0:T(8,128)S(1)} %get-tuple-element.21.coef), custom_call_target="tpu_custom_call" | custom-call | flops 200000000 | bytes 811008 | tf_op jit(solution)/shard_map/prepare/pallas_call | solution.py:20
  7.2 0.2 collective-permute-done.2.refs_2_
  7.4 0.1 collective-permute-done.refs_1_
  7.6 0.2 interface.1
  7.7 1.2 %collective-permute-start.3 = (f32[56,512]{1,0:T(8,128)S(1)}, f32[56,512]{1,0:T(8,128)S(1)}, u32[]{:S(2)}, u32[]{:S(2)}) collective-permute-start(f32[56,512]{1,0:T(8,128)S(1)} %get-tuple-element.30.mine), channel_id=1, source_target_pairs={{0,2},{2,0},{4,6},{6,4},{8,10},{10,8},{12,14},{14,12},{16,18},{18,... | collective-permute-start | bytes 344072 | tf_op jit(solution)/shard_map/ppermute | solution.py:520
  9.0 1.0 %collective-permute-done.3.other = f32[56,512]{1,0:T(8,128)S(1)} collective-permute-done((f32[56,512]{1,0:T(8,128)S(1)}, f32[56,512]{1,0:T(8,128)S(1)}, u32[]{:S(2)}, u32[]{:S(2)}) %collective-permute-start.3) | collective-permute-done | bytes 114720 | tf_op jit(solution)/shard_map/ppermute | solution.py:520
  9.9 0.2 pair.1
  10.1 3.9 %collective-permute-start.6 = (f32[24,512]{1,0:T(8,128)S(1)}, f32[24,512]{1,0:T(8,128)S(1)}, u32[]{:S(2)}, u32[]{:S(2)}) collective-permute-start(f32[24,512]{1,0:T(8,128)S(1)} %get-tuple-element.32.refs_0_), channel_id=1, source_target_pairs={{0,14},{2,12},{4,10},{6,8},{8,6},{10,4},{12,2},{14,0},{16,30},{18,... | collective-permute-start | bytes 147464 | tf_op jit(solution)/shard_map/ppermute | solution.py:544
  14.0 0.4 %collective-permute-start.5 = (f32[24,512]{1,0:T(8,128)S(1)}, f32[24,512]{1,0:T(8,128)S(1)}, u32[]{:S(2)}, u32[]{:S(2)}) collective-permute-start(f32[24,512]{1,0:T(8,128)S(1)} %get-tuple-element.32.refs_0_), channel_id=1, source_target_pairs={{0,10},{2,8},{4,14},{6,12},{8,2},{10,0},{12,6},{14,4},{16,26},{18,... | collective-permute-start | bytes 147464 | tf_op jit(solution)/shard_map/ppermute | solution.py:544
  14.4 1.0 %collective-permute-start.4 = (f32[24,512]{1,0:T(8,128)S(1)}, f32[24,512]{1,0:T(8,128)S(1)}, u32[]{:S(2)}, u32[]{:S(2)}) collective-permute-start(f32[24,512]{1,0:T(8,128)S(1)} %get-tuple-element.32.refs_0_), channel_id=1, source_target_pairs={{0,6},{2,4},{4,2},{6,0},{8,14},{10,12},{12,10},{14,8},{16,22},{18,... | collective-permute-start | bytes 147464 | tf_op jit(solution)/shard_map/ppermute | solution.py:544
  15.4 0.1 widen.2.refs_4_
  15.5 0.7 %collective-permute-done.6.refs_3_ = f32[24,512]{1,0:T(8,128)S(1)} collective-permute-done((f32[24,512]{1,0:T(8,128)S(1)}, f32[24,512]{1,0:T(8,128)S(1)}, u32[]{:S(2)}, u32[]{:S(2)}) %collective-permute-start.6) | collective-permute-done | bytes 49184 | tf_op jit(solution)/shard_map/ppermute | solution.py:544
  16.2 1.4 %collective-permute-done.5.refs_2_ = f32[24,512]{1,0:T(8,128)S(1)} collective-permute-done((f32[24,512]{1,0:T(8,128)S(1)}, f32[24,512]{1,0:T(8,128)S(1)}, u32[]{:S(2)}, u32[]{:S(2)}) %collective-permute-start.5) | collective-permute-done | bytes 49184 | tf_op jit(solution)/shard_map/ppermute | solution.py:544
  17.6 0.6 %collective-permute-done.4.refs_1_ = f32[24,512]{1,0:T(8,128)S(1)} collective-permute-done((f32[24,512]{1,0:T(8,128)S(1)}, f32[24,512]{1,0:T(8,128)S(1)}, u32[]{:S(2)}, u32[]{:S(2)}) %collective-permute-start.4) | collective-permute-done | bytes 49184 | tf_op jit(solution)/shard_map/ppermute | solution.py:544
  18.1 0.1 compose.1.composed
  18.3 2.7 %collective-permute-start.7 = (f32[10,512]{1,0:T(8,128)S(1)}, f32[10,512]{1,0:T(8,128)S(1)}, u32[]{:S(2)}, u32[]{:S(2)}) collective-permute-start(f32[10,512]{1,0:T(8,128)S(1)} %last_message.1), channel_id=1, source_target_pairs={{0,18},{2,16},{4,22},{6,20},{8,26},{10,24},{12,30},{14,28},{16,2},... | collective-permute-start | bytes 61448 | tf_op jit(solution)/shard_map/ppermute | solution.py:561
  21.0 1.0 %block.1.local = f32[3,24,512]{2,1,0:T(8,128)S(1)} custom-call(f32[24,24,256]{2,1,0:T(8,128)S(1)} %get-tuple-element.22.inverse, f32[3,24,512]{2,1,0:T(8,128)S(1)} %get-tuple-element.29.rhs, f32[56,512]{1,0:T(8,128)S(1)} %get-tuple-element.30.mine, f32[56,512]{1,0:T(8,128)S(1)} %collective-permute-done.3.other), custom_call_target="tpu_custom_call" | custom-call | flops 200000000 | bytes 966656 | tf_op jit(solution)/shard_map/block/pallas_call | solution.py:20
  22.0 0.2 widen.3.known
  22.2 0.1 ready.1
  22.3 0.4 %collective-permute-done.7.received = f32[10,512]{1,0:T(8,128)S(1)} collective-permute-done((f32[10,512]{1,0:T(8,128)S(1)}, f32[10,512]{1,0:T(8,128)S(1)}, u32[]{:S(2)}, u32[]{:S(2)}) %collective-permute-start.7) | collective-permute-done | bytes 20512 | tf_op jit(solution)/shard_map/ppermute | solution.py:561
  22.6 0.7 %final.1 = f32[3,24,512]{2,1,0:T(8,128)} custom-call(f32[3,24,512]{2,1,0:T(8,128)S(1)} %get-tuple-element.35.ready, f32[2,24,512]{2,1,0:T(8,128)S(1)} %get-tuple-element.36.lift, f32[24,512]{1,0:T(8,128)S(1)} %compose.1.composed, f32[10,512]{1,0:T(8,128)S(1)} %collective-permute-done.7.received), custom_call_target="tpu_custom_call" | custom-call | bytes 315392 | tf_op jit(solution)/shard_map/final/pallas_call | solution.py:20
  (2 shorter events, 0.0 us)
Async XLA Ops:
  1.4 6.2 %collective-permute-start = (f32[56,512]{1,0:T(8,128)S(1)}, f32[56,512]{1,0:T(8,128)S(1)}, u32[]{:S(2)}, u32[]{:S(2)}) collective-permute-start(f32[56,512]{1,0:T(8,128)S(1)} %get-tuple-element.27), channel_id=1, source_target_pairs={{0,1},{1,0},{2,3},{3,2},{4,5},{5,4},{6,7},{7,6},{8,9},{9,8},{10,11... | collective-permute-start | bytes 344072 | tf_op jit(solution)/shard_map/ppermute | solution.py:500
  4.4 1.3 %collective-permute-start.1 = (f32[12,1024]{1,0:T(8,128)S(1)}, f32[12,1024]{1,0:T(8,128)S(1)}, u32[]{:S(2)}, u32[]{:S(2)}) collective-permute-start(f32[12,1024]{1,0:T(8,128)S(1)} %get-tuple-element.28.edges), channel_id=1, source_target_pairs={{0,2},{2,0},{4,6},{6,4},{8,10},{10,8},{12,14},{14,12},{16,18},{18,... | collective-permute-start | bytes 147464 | tf_op jit(solution)/shard_map/ppermute | solution.py:496
  5.7 1.7 %collective-permute-start.2 = (f32[12,512]{1,0:T(8,128)S(1)}, f32[12,512]{1,0:T(8,128)S(1)}, u32[]{:S(2)}, u32[]{:S(2)}) collective-permute-start(f32[12,512]{1,0:T(8,128)S(1)} %relay.1), channel_id=1, source_target_pairs={{3,4},{1,5},{4,3},{6,2},{7,8},{5,9},{8,7},{10,6},{11,12},{9,13},{1... | collective-permute-start | bytes 73736 | tf_op jit(solution)/shard_map/ppermute | solution.py:504
  7.7 2.2 %collective-permute-start.3 = (f32[56,512]{1,0:T(8,128)S(1)}, f32[56,512]{1,0:T(8,128)S(1)}, u32[]{:S(2)}, u32[]{:S(2)}) collective-permute-start(f32[56,512]{1,0:T(8,128)S(1)} %get-tuple-element.30.mine), channel_id=1, source_target_pairs={{0,2},{2,0},{4,6},{6,4},{8,10},{10,8},{12,14},{14,12},{16,18},{18,... | collective-permute-start | bytes 344072 | tf_op jit(solution)/shard_map/ppermute | solution.py:520
  10.1 6.1 %collective-permute-start.6 = (f32[24,512]{1,0:T(8,128)S(1)}, f32[24,512]{1,0:T(8,128)S(1)}, u32[]{:S(2)}, u32[]{:S(2)}) collective-permute-start(f32[24,512]{1,0:T(8,128)S(1)} %get-tuple-element.32.refs_0_), channel_id=1, source_target_pairs={{0,14},{2,12},{4,10},{6,8},{8,6},{10,4},{12,2},{14,0},{16,30},{18,... | collective-permute-start | bytes 147464 | tf_op jit(solution)/shard_map/ppermute | solution.py:544
  14.0 3.5 %collective-permute-start.5 = (f32[24,512]{1,0:T(8,128)S(1)}, f32[24,512]{1,0:T(8,128)S(1)}, u32[]{:S(2)}, u32[]{:S(2)}) collective-permute-start(f32[24,512]{1,0:T(8,128)S(1)} %get-tuple-element.32.refs_0_), channel_id=1, source_target_pairs={{0,10},{2,8},{4,14},{6,12},{8,2},{10,0},{12,6},{14,4},{16,26},{18,... | collective-permute-start | bytes 147464 | tf_op jit(solution)/shard_map/ppermute | solution.py:544
  14.4 3.7 %collective-permute-start.4 = (f32[24,512]{1,0:T(8,128)S(1)}, f32[24,512]{1,0:T(8,128)S(1)}, u32[]{:S(2)}, u32[]{:S(2)}) collective-permute-start(f32[24,512]{1,0:T(8,128)S(1)} %get-tuple-element.32.refs_0_), channel_id=1, source_target_pairs={{0,6},{2,4},{4,2},{6,0},{8,14},{10,12},{12,10},{14,8},{16,22},{18,... | collective-permute-start | bytes 147464 | tf_op jit(solution)/shard_map/ppermute | solution.py:544
  18.3 4.3 %collective-permute-start.7 = (f32[10,512]{1,0:T(8,128)S(1)}, f32[10,512]{1,0:T(8,128)S(1)}, u32[]{:S(2)}, u32[]{:S(2)}) collective-permute-start(f32[10,512]{1,0:T(8,128)S(1)} %last_message.1), channel_id=1, source_target_pairs={{0,18},{2,16},{4,22},{6,20},{8,26},{10,24},{12,30},{14,28},{16,2},... | collective-permute-start | bytes 61448 | tf_op jit(solution)/shard_map/ppermute | solution.py:561

commit v3 on v2

--- a/solution.py
+++ b/solution.py
@@ -85,12 +85,10 @@
     return lambda kind, j: ref[at + 6 * kind + 3 * j : at + 6 * kind + 3 * j + 3]
 
 
-def stencil_kernel(wide, firsts, velocity, explicit, bands, *refs):
+def load_kernel(wide, firsts, velocity, explicit, bands, edges, coef, weight, vel, tot, here, there, taps, square, sems):
     groups = len(firsts)
-    outs, (edges, coef, here, there, taps, square, weight, vel, tot, sems) = refs[:groups], refs[groups:]
-    own, lanes = velocity.shape[1:]
+    own = velocity.shape[1]
     rows = coef.shape[1]
-    part = lanes // groups
     g = lax.axis_index("gz")
     copies = [
         pltpu.make_async_copy(source, target, sems.at[i])
@@ -107,15 +105,19 @@
     turned = jnp.transpose(square[...])
     for i in range(10):
         coef[i] = jnp.broadcast_to(turned[0:rows, i : i + 1], (rows, LANES))
+    for k in range(groups):
+
+        @pl.when(g == k)
+        def _(first=firsts[k]):
+            for i in range(10):
+                weight[i] = coef[i, first : first + wide]
+
     copies[1].wait()
     copies[2].wait()
     for k in range(groups):
-        base = 8 + k * own - firsts[k]
 
         @pl.when(g == k)
-        def _(base=base, first=firsts[k]):
-            for i in range(10):
-                weight[i] = coef[i, first : first + wide]
+        def _(base=8 + k * own - firsts[k]):
             for f in range(3):
                 vel[f, base : base + own] = here[f]
                 tot[f, base : base + own] = here[f] + there[f]
@@ -127,9 +129,13 @@
             top += there[f, j : j + 1]
             bottom += there[f, own - HALO + j : own - HALO + j + 1]
             edges[3 * j + f : 3 * j + f + 1] = jnp.where(g == 0, top, bottom)
+
+
+def stencil_kernel(wide, groups, shifts, vel, tot, weight, edges, *outs):
+    part = vel.shape[2] // groups
+    g = lax.axis_index("gz")
     weights = [weight[i] for i in range(10)]
-    for shift in range(groups - 1, -1, -1):
-        out = outs[shift]
+    for shift, out in zip(shifts, outs):
         begin = lax.rem(g + shift, groups) * part
         for lane in range(0, part, LANES):
             at = pl.ds(pl.multiple_of(begin + lane, LANES), LANES)
@@ -482,22 +488,31 @@
     dma = lambda n: pltpu.SemaphoreType.DMA((n,))
 
     high = -(-(3 * wide + 12) // 8) * 8
-    *shares, edges, coef = vmem_call(
-        functools.partial(stencil_kernel, wide, firsts),
-        [(high, lanes)] * gz + [(12, columns), (10, rows, LANES)],
+    padded = (3, rows + 16, columns)
+    edges, coef, weight, vel, tot = vmem_call(
+        functools.partial(load_kernel, wide, firsts),
+        [(12, columns), (10, rows, LANES), (10, wide, LANES), padded, padded],
         [velocity, explicit, jnp.transpose(bands, (1, 0, 2))],
-        scratch=[vmem(3, own, columns)] * 2
-        + [vmem(5, 2, rows), vmem(LANES, LANES), vmem(10, wide, LANES)]
-        + [vmem(3, rows + 16, columns)] * 2
-        + [dma(3)],
-        name="stencil",
+        scratch=[vmem(3, own, columns)] * 2 + [vmem(5, 2, rows), vmem(LANES, LANES), dma(3)],
+        name="load",
         far=3,
     )
     beside_edges = lax.ppermute(edges, "gy", [(i, i ^ 1) for i in range(gy)])
-    pieces = [shares[0]]
+
+    def shares(*shifts):
+        return vmem_call(
+            functools.partial(stencil_kernel, wide, gz, shifts),
+            [(high, lanes)] * len(shifts),
+            [vel, tot, weight, edges],
+            flops=2 * 10**8,
+            name="stencil",
+        )
+
+    sent = shares(*range(1, gz))
+    pieces = list(shares(0))
     for shift in range(1, gz):
         ring = [(i, (i + shift) % gz) for i in range(gz)]
-        pieces.append(lax.ppermute(shares[shift], "gz", ring))
+        pieces.append(lax.ppermute(sent[shift - 1], "gz", ring))
     relays = vmem_call(
         functools.partial(relay_kernel, gz), [(12, lanes)] * (gz // 2), [edges, beside_edges], name="relay"
     )
@@ -507,7 +522,7 @@
         [(2, 2, rows, lanes), (4, rows, lanes), (28, lanes), (8, lanes), (rows, rows, modes)],
         [spikes, inverse, coef],
         scratch=[vmem(2, 2, rows, modes), dma(2)],
-        flops=2 * 10**8,
+        flops=2 * 10**10,
         name="prepare",
         far=2,
     )

time: 23.6 us -> 22.5 us (0.953)
  starting transfers between devices: 12.5 us -> 11.5 us
    ppermute x1, waiting for transfers between devices: 1.25 us -> 0.01 us  [per_device(): beside_edges = lax.ppermute(edges, 'gy', [(i, i ^ 1) for i in range(gy)])]
    ppermute x1, starting transfers between devices: 1.24 us -> 0.07 us  [per_device(): other = lax.ppermute(message, 'gy', [(i, i ^ 1) for i in range(gy)])]
    ppermute x1, starting transfers between devices: 0.13 us -> 1.09 us  [per_device(): lax.ppermute(relay, ('gy', 'gz'), end_pairs(gy, gz, step))]
    ppermute x1, waiting for transfers between devices: 0.21 us -> 1.16 us  [per_device(): lax.ppermute(relay, ('gy', 'gz'), end_pairs(gy, gz, step))]
    ppermute x3, starting transfers between devices: 5.34 us -> 4.45 us  [per_device(): lax.ppermute(composed, 'gy', [(i, i ^ x * base ^ 1) for i in range(gy)])]
    ppermute x1, starting transfers between devices: 0.01 us -> 0.52 us  [per_device(): beside_edges = lax.ppermute(edges, 'gy', [(i, i ^ 1) for i in range(gy)])]
    ppermute x1, starting transfers between devices: 3.04 us -> 2.61 us  [per_device(): pieces.append(lax.ppermute(sent[shift - 1], 'gz', ring))]
    ppermute x1, waiting for transfers between devices: 0.97 us -> 1.31 us  [per_device(): other = lax.ppermute(message, 'gy', [(i, i ^ 1) for i in range(gy)])]
  transfers between devices with their start and end apart: 8 -> 8, of which waited for: 8 -> 6; matrix products, arithmetic and copies ran while one was open for 0% -> 0% of each run, Pallas kernels for 11% -> 13%
where the time goes in v3:
time: 22.5 us; the launch traced here: 22.3 us
  starting transfers between devices  11.5 us (51%)
  waiting for transfers between devices  5.45 us (24%)
  Pallas kernels  5.25 us (23%)
    pallas_call x14, Pallas kernels, vmem_call(): pl.pallas_call(body, out_shape=[jax.ShapeDtypeStruct(s, F32) for s in out...  5.25 us
    ppermute x3, starting transfers between devices, per_device(): lax.ppermute(composed, 'gy', [(i, i ^ x * base ^ 1) for i in range(gy)])  4.45 us
    ppermute x1, starting transfers between devices, per_device(): lax.ppermute(message, 'gy', [(i, i ^ base ^ 1) for i in range(gy)])  2.74 us
    ppermute x3, waiting for transfers between devices, per_device(): lax.ppermute(composed, 'gy', [(i, i ^ x * base ^ 1) for i in range(gy)])  2.64 us
    ppermute x1, starting transfers between devices, per_device(): pieces.append(lax.ppermute(sent[shift - 1], 'gz', ring))  2.61 us
    ppermute x1, waiting for transfers between devices, per_device(): other = lax.ppermute(message, 'gy', [(i, i ^ 1) for i in range(gy)])  1.31 us
    ppermute x1, waiting for transfers between devices, per_device(): lax.ppermute(relay, ('gy', 'gz'), end_pairs(gy, gz, step))  1.16 us
    ppermute x1, starting transfers between devices, per_device(): lax.ppermute(relay, ('gy', 'gz'), end_pairs(gy, gz, step))  1.09 us
  transfers between devices with their start and end apart: 8, of which 6 were waited for; matrix products, arithmetic and copies ran while one was open for 0% of the time, Pallas kernels for 13%

profile of v3, /device:TPU:0, one launch (start us, length us, event | category | flops | bytes accessed | tf_op | source)
XLA Modules:
  0.0 22.3 jit_solution(16207436489044676666)
XLA Ops:
  0.0 1.1 %load.1 = (f32[12,1024]{1,0:T(8,128)S(1)}, f32[10,24,128]{2,1,0:T(8,128)S(1)}, f32[10,14,128]{2,1,0:T(8,128)S(1)}, f32[3,40,1024]{2,1,0:T(8,128)S(1)}, f32[3,40,1024]{2,1,0:T(8,128)S(1)}) custom-call(f32[3,12,1024]{2,1,0:T(8,128)} %velocity.1, f32[3,12,1024]{2,1,0:T(8,128)} %explicit.1, f32[5,2,24]{2,1,0:T(2,128)} %bitcast.1), custom_call_target="tpu_custom_call" | custom-call | bytes 295872 | tf_op jit(solution)/shard_map/load/pallas_call | solution.py:20
  1.1 0.5 %collective-permute-start.1 = (f32[12,1024]{1,0:T(8,128)S(1)}, f32[12,1024]{1,0:T(8,128)S(1)}, u32[]{:S(2)}, u32[]{:S(2)}) collective-permute-start(f32[12,1024]{1,0:T(8,128)S(1)} %get-tuple-element.30.edges), channel_id=1, source_target_pairs={{0,2},{2,0},{4,6},{6,4},{8,10},{10,8},{12,14},{14,12},{16,18},{18,... | collective-permute-start | bytes 147464 | tf_op jit(solution)/shard_map/ppermute | solution.py:500
  1.6 0.1 stencil.3
  1.8 2.6 %collective-permute-start = (f32[56,512]{1,0:T(8,128)S(1)}, f32[56,512]{1,0:T(8,128)S(1)}, u32[]{:S(2)}, u32[]{:S(2)}) collective-permute-start(f32[56,512]{1,0:T(8,128)S(1)} %stencil.3), channel_id=1, source_target_pairs={{0,1},{1,0},{2,3},{3,2},{4,5},{5,4},{6,7},{7,6},{8,9},{9,8},{10,11... | collective-permute-start | bytes 344072 | tf_op jit(solution)/shard_map/ppermute | solution.py:515
  4.4 0.0 collective-permute-done.1.beside_edges
  4.4 1.1 %collective-permute-start.2 = (f32[12,512]{1,0:T(8,128)S(1)}, f32[12,512]{1,0:T(8,128)S(1)}, u32[]{:S(2)}, u32[]{:S(2)}) collective-permute-start(f32[12,512]{1,0:T(8,128)S(1)} %relay.1), channel_id=1, source_target_pairs={{3,4},{1,5},{4,3},{6,2},{7,8},{5,9},{8,7},{10,6},{11,12},{9,13},{1... | collective-permute-start | bytes 73736 | tf_op jit(solution)/shard_map/ppermute | solution.py:519
  5.5 1.4 %prepare.1 = (f32[2,2,24,512]{3,2,1,0:T(8,128)S(1)}, f32[4,24,512]{2,1,0:T(8,128)S(1)}, f32[28,512]{1,0:T(8,128)S(1)}, f32[8,512]{1,0:T(8,128)S(1)}, f32[24,24,256]{2,1,0:T(8,128)S(1)}) custom-call(f32[2,2,24,256]{3,2,1,0:T(8,128)} %spikes.1, f32[24,24,256]{2,1,0:T(8,128)} %inverse.1, f32[10,24,128]{2,1,0:T(8,128)S(1)} %get-tuple-element.22.coef), custom_call_target="tpu_custom_call" | custom-call | flops 20000000000 | bytes 811008 | tf_op jit(solution)/shard_map/prepare/pallas_call | solution.py:20
  6.9 0.1 stencil.2.refs_0_
  7.0 1.2 %collective-permute-done.2.refs_2_ = f32[12,512]{1,0:T(8,128)S(1)} collective-permute-done((f32[12,512]{1,0:T(8,128)S(1)}, f32[12,512]{1,0:T(8,128)S(1)}, u32[]{:S(2)}, u32[]{:S(2)}) %collective-permute-start.2) | collective-permute-done | bytes 24608 | tf_op jit(solution)/shard_map/ppermute | solution.py:519
  8.2 0.0 collective-permute-done.refs_1_
  8.2 0.2 interface.1
  8.4 0.1 collective-permute-start.3
  8.4 1.3 %collective-permute-done.3.other = f32[56,512]{1,0:T(8,128)S(1)} collective-permute-done((f32[56,512]{1,0:T(8,128)S(1)}, f32[56,512]{1,0:T(8,128)S(1)}, u32[]{:S(2)}, u32[]{:S(2)}) %collective-permute-start.3) | collective-permute-done | bytes 114720 | tf_op jit(solution)/shard_map/ppermute | solution.py:535
  9.7 0.2 pair.1
  9.9 3.0 %collective-permute-start.6 = (f32[24,512]{1,0:T(8,128)S(1)}, f32[24,512]{1,0:T(8,128)S(1)}, u32[]{:S(2)}, u32[]{:S(2)}) collective-permute-start(f32[24,512]{1,0:T(8,128)S(1)} %get-tuple-element.34.refs_0_), channel_id=1, source_target_pairs={{0,14},{2,12},{4,10},{6,8},{8,6},{10,4},{12,2},{14,0},{16,30},{18,... | collective-permute-start | bytes 147464 | tf_op jit(solution)/shard_map/ppermute | solution.py:559
  13.0 0.4 %collective-permute-start.5 = (f32[24,512]{1,0:T(8,128)S(1)}, f32[24,512]{1,0:T(8,128)S(1)}, u32[]{:S(2)}, u32[]{:S(2)}) collective-permute-start(f32[24,512]{1,0:T(8,128)S(1)} %get-tuple-element.34.refs_0_), channel_id=1, source_target_pairs={{0,10},{2,8},{4,14},{6,12},{8,2},{10,0},{12,6},{14,4},{16,26},{18,... | collective-permute-start | bytes 147464 | tf_op jit(solution)/shard_map/ppermute | solution.py:559
  13.4 1.0 %collective-permute-start.4 = (f32[24,512]{1,0:T(8,128)S(1)}, f32[24,512]{1,0:T(8,128)S(1)}, u32[]{:S(2)}, u32[]{:S(2)}) collective-permute-start(f32[24,512]{1,0:T(8,128)S(1)} %get-tuple-element.34.refs_0_), channel_id=1, source_target_pairs={{0,6},{2,4},{4,2},{6,0},{8,14},{10,12},{12,10},{14,8},{16,22},{18,... | collective-permute-start | bytes 147464 | tf_op jit(solution)/shard_map/ppermute | solution.py:559
  14.4 0.1 widen.2.refs_4_
  14.4 0.7 %collective-permute-done.6.refs_3_ = f32[24,512]{1,0:T(8,128)S(1)} collective-permute-done((f32[24,512]{1,0:T(8,128)S(1)}, f32[24,512]{1,0:T(8,128)S(1)}, u32[]{:S(2)}, u32[]{:S(2)}) %collective-permute-start.6) | collective-permute-done | bytes 49184 | tf_op jit(solution)/shard_map/ppermute | solution.py:559
  15.1 1.4 %collective-permute-done.5.refs_2_ = f32[24,512]{1,0:T(8,128)S(1)} collective-permute-done((f32[24,512]{1,0:T(8,128)S(1)}, f32[24,512]{1,0:T(8,128)S(1)}, u32[]{:S(2)}, u32[]{:S(2)}) %collective-permute-start.5) | collective-permute-done | bytes 49184 | tf_op jit(solution)/shard_map/ppermute | solution.py:559
  16.5 0.6 %collective-permute-done.4.refs_1_ = f32[24,512]{1,0:T(8,128)S(1)} collective-permute-done((f32[24,512]{1,0:T(8,128)S(1)}, f32[24,512]{1,0:T(8,128)S(1)}, u32[]{:S(2)}, u32[]{:S(2)}) %collective-permute-start.4) | collective-permute-done | bytes 49184 | tf_op jit(solution)/shard_map/ppermute | solution.py:559
  17.1 0.1 compose.1.composed
  17.2 2.7 %collective-permute-start.7 = (f32[10,512]{1,0:T(8,128)S(1)}, f32[10,512]{1,0:T(8,128)S(1)}, u32[]{:S(2)}, u32[]{:S(2)}) collective-permute-start(f32[10,512]{1,0:T(8,128)S(1)} %last_message.1), channel_id=1, source_target_pairs={{0,18},{2,16},{4,22},{6,20},{8,26},{10,24},{12,30},{14,28},{16,2},... | collective-permute-start | bytes 61448 | tf_op jit(solution)/shard_map/ppermute | solution.py:576
  20.0 1.0 %block.1.local = f32[3,24,512]{2,1,0:T(8,128)S(1)} custom-call(f32[24,24,256]{2,1,0:T(8,128)S(1)} %get-tuple-element.23.inverse, f32[3,24,512]{2,1,0:T(8,128)S(1)} %get-tuple-element.31.rhs, f32[56,512]{1,0:T(8,128)S(1)} %get-tuple-element.32.mine, f32[56,512]{1,0:T(8,128)S(1)} %collective-permute-done.3.other), custom_call_target="tpu_custom_call" | custom-call | flops 200000000 | bytes 966656 | tf_op jit(solution)/shard_map/block/pallas_call | solution.py:20
  20.9 0.2 widen.3.known
  21.1 0.1 ready.1
  21.2 0.3 %collective-permute-done.7.received = f32[10,512]{1,0:T(8,128)S(1)} collective-permute-done((f32[10,512]{1,0:T(8,128)S(1)}, f32[10,512]{1,0:T(8,128)S(1)}, u32[]{:S(2)}, u32[]{:S(2)}) %collective-permute-start.7) | collective-permute-done | bytes 20512 | tf_op jit(solution)/shard_map/ppermute | solution.py:576
  21.6 0.7 %final.1 = f32[3,24,512]{2,1,0:T(8,128)} custom-call(f32[3,24,512]{2,1,0:T(8,128)S(1)} %get-tuple-element.37.ready, f32[2,24,512]{2,1,0:T(8,128)S(1)} %get-tuple-element.38.lift, f32[24,512]{1,0:T(8,128)S(1)} %compose.1.composed, f32[10,512]{1,0:T(8,128)S(1)} %collective-permute-done.7.received), custom_call_target="tpu_custom_call" | custom-call | bytes 315392 | tf_op jit(solution)/shard_map/final/pallas_call | solution.py:20
  (2 shorter events, 0.0 us)
Async XLA Ops:
  1.1 3.3 %collective-permute-start.1 = (f32[12,1024]{1,0:T(8,128)S(1)}, f32[12,1024]{1,0:T(8,128)S(1)}, u32[]{:S(2)}, u32[]{:S(2)}) collective-permute-start(f32[12,1024]{1,0:T(8,128)S(1)} %get-tuple-element.30.edges), channel_id=1, source_target_pairs={{0,2},{2,0},{4,6},{6,4},{8,10},{10,8},{12,14},{14,12},{16,18},{18,... | collective-permute-start | bytes 147464 | tf_op jit(solution)/shard_map/ppermute | solution.py:500
  1.8 6.4 %collective-permute-start = (f32[56,512]{1,0:T(8,128)S(1)}, f32[56,512]{1,0:T(8,128)S(1)}, u32[]{:S(2)}, u32[]{:S(2)}) collective-permute-start(f32[56,512]{1,0:T(8,128)S(1)} %stencil.3), channel_id=1, source_target_pairs={{0,1},{1,0},{2,3},{3,2},{4,5},{5,4},{6,7},{7,6},{8,9},{9,8},{10,11... | collective-permute-start | bytes 344072 | tf_op jit(solution)/shard_map/ppermute | solution.py:515
  4.4 3.8 %collective-permute-start.2 = (f32[12,512]{1,0:T(8,128)S(1)}, f32[12,512]{1,0:T(8,128)S(1)}, u32[]{:S(2)}, u32[]{:S(2)}) collective-permute-start(f32[12,512]{1,0:T(8,128)S(1)} %relay.1), channel_id=1, source_target_pairs={{3,4},{1,5},{4,3},{6,2},{7,8},{5,9},{8,7},{10,6},{11,12},{9,13},{1... | collective-permute-start | bytes 73736 | tf_op jit(solution)/shard_map/ppermute | solution.py:519
  8.4 1.4 %collective-permute-start.3 = (f32[56,512]{1,0:T(8,128)S(1)}, f32[56,512]{1,0:T(8,128)S(1)}, u32[]{:S(2)}, u32[]{:S(2)}) collective-permute-start(f32[56,512]{1,0:T(8,128)S(1)} %get-tuple-element.32.mine), channel_id=1, source_target_pairs={{0,2},{2,0},{4,6},{6,4},{8,10},{10,8},{12,14},{14,12},{16,18},{18,... | collective-permute-start | bytes 344072 | tf_op jit(solution)/shard_map/ppermute | solution.py:535
  9.9 5.2 %collective-permute-start.6 = (f32[24,512]{1,0:T(8,128)S(1)}, f32[24,512]{1,0:T(8,128)S(1)}, u32[]{:S(2)}, u32[]{:S(2)}) collective-permute-start(f32[24,512]{1,0:T(8,128)S(1)} %get-tuple-element.34.refs_0_), channel_id=1, source_target_pairs={{0,14},{2,12},{4,10},{6,8},{8,6},{10,4},{12,2},{14,0},{16,30},{18,... | collective-permute-start | bytes 147464 | tf_op jit(solution)/shard_map/ppermute | solution.py:559
  13.0 3.5 %collective-permute-start.5 = (f32[24,512]{1,0:T(8,128)S(1)}, f32[24,512]{1,0:T(8,128)S(1)}, u32[]{:S(2)}, u32[]{:S(2)}) collective-permute-start(f32[24,512]{1,0:T(8,128)S(1)} %get-tuple-element.34.refs_0_), channel_id=1, source_target_pairs={{0,10},{2,8},{4,14},{6,12},{8,2},{10,0},{12,6},{14,4},{16,26},{18,... | collective-permute-start | bytes 147464 | tf_op jit(solution)/shard_map/ppermute | solution.py:559
  13.4 3.7 %collective-permute-start.4 = (f32[24,512]{1,0:T(8,128)S(1)}, f32[24,512]{1,0:T(8,128)S(1)}, u32[]{:S(2)}, u32[]{:S(2)}) collective-permute-start(f32[24,512]{1,0:T(8,128)S(1)} %get-tuple-element.34.refs_0_), channel_id=1, source_target_pairs={{0,6},{2,4},{4,2},{6,0},{8,14},{10,12},{12,10},{14,8},{16,22},{18,... | collective-permute-start | bytes 147464 | tf_op jit(solution)/shard_map/ppermute | solution.py:559
  17.2 4.3 %collective-permute-start.7 = (f32[10,512]{1,0:T(8,128)S(1)}, f32[10,512]{1,0:T(8,128)S(1)}, u32[]{:S(2)}, u32[]{:S(2)}) collective-permute-start(f32[10,512]{1,0:T(8,128)S(1)} %last_message.1), channel_id=1, source_target_pairs={{0,18},{2,16},{4,22},{6,20},{8,26},{10,24},{12,30},{14,28},{16,2},... | collective-permute-start | bytes 61448 | tf_op jit(solution)/shard_map/ppermute | solution.py:576

commit v4 on v3

v4 whole, which is shorter than its diff:
```python
import functools

import jax
import jax.numpy as jnp
from jax import lax
from jax.experimental import pallas as pl
from jax.experimental.pallas import tpu as pltpu
from jax.sharding import PartitionSpec as P

F32 = jnp.float32
LANES = 128
HALO = 2


def vmem_call(body, out_shapes, args, scratch=(), flops=0, name=None, far=0, far_out=False):
    near, away = pl.BlockSpec(memory_space=pltpu.VMEM), pl.BlockSpec(memory_space=pltpu.HBM)
    nbytes = sum(a.size * 4 for a in args)
    args = [pltpu.with_memory_space_constraint(a, pltpu.HBM) for a in args[:far]] + args[far:]
    return pl.pallas_call(
        body,
        out_shape=[jax.ShapeDtypeStruct(s, F32) for s in out_shapes],
        in_specs=[away] * far + [near] * (len(args) - far),
        out_specs=[away if far_out else near] * len(out_shapes),
        scratch_shapes=list(scratch),
        compiler_params=pltpu.CompilerParams(vmem_limit_bytes=16 * 2**20),
        cost_estimate=pl.CostEstimate(flops=flops, bytes_accessed=nbytes, transcendentals=0),
        name=name,
    )(*args)


def window(rows, own, groups):
    spans = [(max(g * own - HALO, 0), min(g * own + own + HALO, rows)) for g in range(groups)]
    wide = max(high - low for low, high in spans)
    return wide, [min(low, rows - wide) for low, _ in spans]


def lane_of(x):
    return lax.broadcasted_iota(jnp.int32, (x.shape[0], LANES), 1)


def take(x, lanes):
    return jnp.take_along_axis(x, lanes, axis=1, mode="promise_in_bounds")


def apart(x):
    lane = lane_of(x)
    low = lane < LANES // 2
    even = jnp.where(low, 2 * lane, 2 * lane - (LANES - 1))
    odd = jnp.where(low, 2 * lane + 1, 2 * lane - LANES)
    a, b = x[:, :LANES], x[:, LANES:]
    return jnp.where(low, take(a, even), take(b, odd)), jnp.where(low, take(a, odd), take(b, even))


def together(real, imaginary):
    lane = lane_of(real)
    half, odd = lax.shift_right_logical(lane, 1), jnp.bitwise_and(lane, 1) == 1
    parts = [
        jnp.where(odd, take(imaginary, half + at), take(real, half + at)) for at in (0, LANES // 2)
    ]
    return jnp.concatenate(parts, axis=1)


def doubled(x):
    half = lax.shift_right_logical(lane_of(x), 1)
    return jnp.concatenate([take(x, half), take(x, half + LANES // 2)], axis=1)


STATE = 24
MAPS = 12
RUN = STATE + MAPS
FIRST = STATE + 24 + MAPS + 16
LAST = 16


def side_weights(coef, upper):
    rows = coef.shape[1]
    if upper:
        taps = [[(4, rows - 2), None], [(3, rows - 1), (4, rows - 1)]]
    else:
        taps = [[(0, 0), (1, 0)], [None, (0, 1)]]
    none = jnp.zeros((1, LANES), F32)
    get = lambda tap, kind: none if tap is None else coef[2 * tap[0] + kind, tap[1] : tap[1] + 1]
    return [[[get(tap, kind) for kind in range(2)] for tap in row] for row in taps]


def beside(weights, planes):
    return [
        sum(weights[i][j][kind] * planes(kind, j) for j in range(2) for kind in range(2)) for i in range(2)
    ]


def load_kernel(wide, firsts, velocity, explicit, bands, edges, coef, weight, vel, tot, here, there, taps, square, sems):
    groups = len(firsts)
    own = velocity.shape[1]
    rows = coef.shape[1]
    g = lax.axis_index("gz")
    copies = [
        pltpu.make_async_copy(source, target, sems.at[i])
        for i, (source, target) in enumerate(((bands, taps), (velocity, here), (explicit, there)))
    ]
    for copy in copies:
        copy.start()
    square[...] = jnp.zeros_like(square)
    vel[...] = jnp.zeros_like(vel)
    tot[...] = jnp.zeros_like(tot)
    copies[0].wait()
    for d in range(5):
        square[2 * d : 2 * d + 2, 0:rows] = taps[d]
    turned = jnp.transpose(square[...])
    for i in range(10):
        coef[i] = jnp.broadcast_to(turned[0:rows, i : i + 1], (rows, LANES))
    for k in range(groups):

        @pl.when(g == k)
        def _(first=firsts[k]):
            for i in range(10):
                weight[i] = coef[i, first : first + wide]

    copies[1].wait()
    copies[2].wait()
    for k in range(groups):

        @pl.when(g == k)
        def _(base=8 + k * own - firsts[k]):
            for f in range(3):
                vel[f, base : base + own] = here[f]
                tot[f, base : base + own] = here[f] + there[f]

    for f in range(3):
        for j in range(HALO):
            top, bottom = here[f, j : j + 1], here[f, own - HALO + j : own - HALO + j + 1]
            edges[6 + 3 * j + f : 7 + 3 * j + f] = jnp.where(g == 0, top, bottom)
            top += there[f, j : j + 1]
            bottom += there[f, own - HALO + j : own - HALO + j + 1]
            edges[3 * j + f : 3 * j + f + 1] = jnp.where(g == 0, top, bottom)


def stencil_kernel(wide, groups, shifts, vel, tot, weight, edges, *outs):
    part = vel.shape[2] // groups
    g = lax.axis_index("gz")
    weights = [weight[i] for i in range(10)]
    for shift, out in zip(shifts, outs):
        begin = lax.rem(g + shift, groups) * part
        for lane in range(0, part, LANES):
            at = pl.ds(pl.multiple_of(begin + lane, LANES), LANES)
            to = pl.ds(lane, LANES)
            for f in range(3):
                total = None
                for d in range(5):
                    low = pl.ds(8 + d - 2, wide)
                    term = weights[2 * d] * tot[f, low, at] + weights[2 * d + 1] * vel[f, low, at]
                    total = term if total is None else total + term
                out[f * wide : f * wide + wide, to] = total
            out[3 * wide : 3 * wide + 12, to] = edges[0:12, at]


def store_planes(ref, at, planes):
    real, imaginary = apart(planes)
    for i in range(4):
        ref[at + 6 * i : at + 6 * i + 3] = real[3 * i : 3 * i + 3]
        ref[at + 6 * i + 3 : at + 6 * i + 6] = imaginary[3 * i : 3 * i + 3]


def planes_of(ref, at):
    return lambda kind, j: ref[at + 12 * kind + 6 * j : at + 12 * kind + 6 * j + 6]


def relay_kernel(groups, edges, beside_edges, *outs):
    core = lax.rem(lax.axis_index("gy"), 2)
    mine = jnp.where(lax.axis_index("gz") == 0, core == 0, core == 1)
    part = edges.shape[1] // groups
    for step, out in enumerate(outs):
        begin = (2 * step + 1 - core) * part
        for b in range(part // (2 * LANES)):
            at = pl.ds(pl.multiple_of(begin + 2 * LANES * b, 2 * LANES), 2 * LANES)
            store_planes(out, 24 * b, jnp.where(mine, edges[:, at], beside_edges[:, at]))


def prepare_kernel(spikes, inverse, coef, inv4, fixed, inside, near, sems):
    rows, modes = inverse.shape[1:]
    core = lax.rem(lax.axis_index("gy"), 2)
    gy, count = lax.axis_index("gy"), lax.axis_size("gy")
    copies = [pltpu.make_async_copy(spikes, near, sems.at[0])]
    for i, (low, size) in enumerate(((0, 2), (rows - 2, 2), (2, rows - 4))):
        part = pl.ds(low, size)
        copies.append(pltpu.make_async_copy(inverse.at[part], inside.at[part], sems.at[1 + i]))
    for copy in copies:
        copy.start()
    lower, upper = side_weights(coef, False), side_weights(coef, True)
    used = jnp.where(core == 0, gy > 0, gy < count - 1)
    weights = (MAPS + 16) * (modes // LANES)
    for i in range(2):
        for j in range(2):
            for kind in range(2):
                at = weights + 4 * i + 2 * j + kind
                low, high = lower[i][j][kind], upper[i][j][kind]
                fixed[at : at + 1] = jnp.where(core == 0, high, low)
                fixed[at + 8 : at + 9] = jnp.where(used, jnp.where(core == 0, low, high), 0.0)
    copies[0].wait()
    for b in range(modes // LANES):
        at, lanes = (MAPS + 16) * b, pl.ds(LANES * b, LANES)
        for k in range(2):
            for j in range(2):
                row = at + 2 * k + j
                fixed[row : row + 1] = -near[0, j, rows - 2 + k : rows - 1 + k, lanes]
                fixed[row + 4 : row + 5] = -near[0, j, k : k + 1, lanes]
                fixed[row + 8 : row + 9] = -near[1, j, k : k + 1, lanes]
    copies[1].wait()
    copies[2].wait()
    for b in range(modes // LANES):
        at, lanes = (MAPS + 16) * b + MAPS, pl.ds(LANES * b, LANES)
        for r, row in enumerate((0, 1, rows - 2, rows - 1)):
            inv4[r, :, 2 * LANES * b : 2 * LANES * (b + 1)] = doubled(inside[row, :, lanes])
            for i in range(2):
                low, high = inside[row, i : i + 1, lanes], inside[row, rows - 2 + i : rows - 1 + i, lanes]
                to = at + 2 * ((r + 2) % 4) + i
                fixed[to : to + 1] = jnp.where(core == 0, high, low)
                fixed[to + 8 : to + 9] = jnp.where(core == 0, low, high)
    copies[3].wait()


def weights_of(ref, at):
    at += ref.shape[0] - 16
    return [
        [[ref[at + 4 * i + 2 * j + kind : at + 4 * i + 2 * j + kind + 1] for kind in range(2)] for j in range(2)]
        for i in range(2)
    ]


def interface_kernel(wide, firsts, inv4, fixed, *refs):
    groups = len(firsts)
    *pieces, rhs, message, planes, values = refs
    rows, lanes = rhs.shape[1:]
    blocks = lanes // (2 * LANES)
    g = lax.axis_index("gz")
    core = lax.rem(lax.axis_index("gy"), 2)
    rhs[...] = jnp.zeros_like(rhs)
    for shift, piece in enumerate(pieces):
        source = lax.rem(g - shift + groups, groups)
        for k in range(groups):

            @pl.when(source == k)
            def _(piece=piece, k=k):
                for f in range(3):
                    rhs[f, firsts[k] : firsts[k] + wide] += piece[f * wide : f * wide + wide]
                if k in (0, groups - 1):

                    @pl.when(core == (1 if k == 0 else 0))
                    def _():
                        planes[...] = piece[3 * wide : 3 * wide + 12]

    for f in range(3):
        for r in range(4):
            row = (6 if r < 2 else 0) + 3 * (r % 2) + f
            values[row : row + 1] = jnp.sum(inv4[r] * rhs[f], axis=0, keepdims=True)
    for b in range(blocks):
        at, columns = FIRST * b, pl.ds(2 * LANES * b, 2 * LANES)
        store_planes(message, at, values[:, columns])
        store_planes(message, at + STATE, planes[:, columns])
        message[at + 48 : at + FIRST] = fixed[(MAPS + 16) * b : (MAPS + 16) * (b + 1)]
    message[FIRST * blocks : FIRST * blocks + 16] = fixed[(MAPS + 16) * blocks : (MAPS + 16) * blocks + 16]


class Piece:
    def __init__(self, ref, at):
        self.p = [ref[at : at + 6], ref[at + 6 : at + 12]]
        self.q = [ref[at + 12 : at + 18], ref[at + 18 : at + 24]]
        self.F, self.H, self.G = (matrix_of(ref, at + STATE + 4 * i) for i in range(3))


def matrix_of(ref, at):
    return [[ref[at + 2 * k + j : at + 2 * k + j + 1] for j in range(2)] for k in range(2)]


def act(matrix, vector, plus=None):
    out = [matrix[k][0] * vector[0] + matrix[k][1] * vector[1] for k in range(2)]
    return out if plus is None else [plus[k] + out[k] for k in range(2)]


def times(a, b, plus=None):
    out = [[a[k][0] * b[0][j] + a[k][1] * b[1][j] for j in range(2)] for k in range(2)]
    return out if plus is None else [[plus[k][j] + out[k][j] for j in range(2)] for k in range(2)]


def after(state, piece):
    if state is None:
        return piece.p, piece.F
    return act(piece.F, state[0], piece.p), times(piece.F, state[1])


def before(piece, state):
    if state is None:
        return piece.q, piece.H, piece.G
    q, H, G = state
    q = act(piece.G, act(H, piece.p, q), piece.q)
    H = times(piece.G, times(H, piece.F), piece.H)
    return q, H, times(piece.G, G)


def choose(flag, new, old):
    return jax.tree.map(lambda a, b: jnp.where(flag, a, b), new, old)


def store_run(ref, at, p, q, F, H, G):
    for i, vector in enumerate((p, q)):
        for k in range(2):
            ref[at + 12 * i + 6 * k : at + 12 * i + 6 * k + 6] = vector[k]
    for i, matrix in enumerate((F, H, G)):
        for k in range(2):
            for j in range(2):
                row = at + STATE + 4 * i + 2 * k + j
                ref[row : row + 1] = matrix[k][j]


def sort_pieces(base, pieces, board):
    size = len(pieces)
    position = lax.rem(lax.div(lax.axis_index("gy"), base), size)
    for i, piece in enumerate(pieces):
        board[jnp.bitwise_xor(position, (size - i) % size)] = piece[...]
    return position


def compose_kernel(base, *refs):
    *pieces, out, board = refs
    sort_pieces(base, pieces, board)
    for at in range(0, out.shape[0], RUN):
        run = [Piece(board.at[i], at) for i in range(len(pieces))]
        up = down = None
        for piece in run:
            up = after(up, piece)
        for piece in run[::-1]:
            down = before(piece, down)
        store_run(out, at, up[0], down[0], up[1], down[1], down[2])


def ends_kernel(*refs):
    *ends, out = refs
    step = lax.div(lax.axis_index("gz"), 2)
    half, size = len(ends) // 2, ends[0].shape[0]
    for k in range(2):
        end = ends[k * half][...]
        for i in range(1, half):
            end = jnp.where(step == i, ends[k * half + i][...], end)
        out[size * k : size * (k + 1)] = end


def pair_kernel(mine, other, ends, out, fixed_mine, fixed_other):
    core = lax.rem(lax.axis_index("gy"), 2)
    blocks = out.shape[0] // RUN
    for ref, across, side, target in ((mine, other, 0, fixed_mine), (other, mine, 1, fixed_other)):
        inner_weights, outer_weights = weights_of(ref, 0), weights_of(ref, 8)
        for b in range(blocks):
            at, to = FIRST * b, RUN * b
            inner = beside(inner_weights, planes_of(across, at + STATE))
            outer = beside(outer_weights, planes_of(ends, 24 * (side * blocks + b)))
            target[to + STATE : to + RUN] = ref[at + 48 : at + 48 + MAPS]
            for k in range(4):
                value = ref[at + 6 * k : at + 6 * k + 6]
                for i in range(2):
                    row = at + 48 + MAPS + 2 * k + i
                    value = value + ref[row : row + 1] * inner[i] + ref[row + 8 : row + 9] * outer[i]
                target[to + 6 * k : to + 6 * k + 6] = value
    low = jnp.where(core == 0, fixed_mine[...], fixed_other[...])
    high = jnp.where(core == 0, fixed_other[...], fixed_mine[...])
    for at in range(0, out.shape[0], RUN):
        first, second = Piece(low, at), Piece(high, at)
        up, down = after(after(None, first), second), before(first, before(second, None))
        store_run(out, at, up[0], down[0], up[1], down[1], down[2])


def widen_kernel(base, start, *refs):
    *pieces, out, board = refs
    known_ref = None if start else pieces.pop()
    position = sort_pieces(base, pieces, board)
    for at in range(0, out.shape[0], RUN):
        run = [Piece(board.at[i], at) for i in range(len(pieces))]
        mine = Piece(pieces[0], at)
        one, none = jnp.ones_like(mine.F[0][0]), jnp.zeros_like(mine.F[0][0])
        zero = [jnp.zeros_like(mine.p[0])] * 2
        unit, blank = [[one, none], [none, one]], [[none, none], [none, none]]
        up, down = (zero, unit), (zero, blank, unit)
        for i, piece in enumerate(run[:-1]):
            up = choose(i < position, after(up, piece), up)
        for i in range(len(run) - 1, 0, -1):
            down = choose(i > position, before(run[i], down), down)
        (t, F), (q, H, G) = up, down
        e = act(H, act(mine.F, t, mine.p), q)
        E = times(H, times(mine.F, F))
        if start:
            store_run(out, at, t, e, F, E, G)
        else:
            known = Piece(known_ref, at)
            a, A, b, B, D = known.p, known.F, known.q, known.H, known.G
            store_run(
                out, at, act(A, t, a), act(D, e, act(B, t, b)), times(A, F), times(D, E, times(B, F)), times(D, G)
            )


def block_kernel(inverse, rhs, mine, other, ends, local, split):
    fields, rows, lanes = rhs.shape
    core = lax.rem(lax.axis_index("gy"), 2)
    inner_weights, outer_weights = weights_of(mine, 0), weights_of(mine, 8)
    flat = rhs[...].reshape(fields * rows, lanes)
    for b in range(lanes // (2 * LANES)):
        columns = pl.ds(2 * LANES * b, 2 * LANES)
        parts = apart(flat[:, 2 * LANES * b : 2 * LANES * (b + 1)])
        inner = beside(inner_weights, planes_of(other, FIRST * b + STATE))
        outer = beside(outer_weights, planes_of(ends, 24 * b))
        solved = []
        for p in range(2):
            split[...] = parts[p].reshape(fields, rows, LANES)
            for f in range(fields):
                for i in range(2):
                    one, two = inner[i][3 * p + f : 3 * p + f + 1], outer[i][3 * p + f : 3 * p + f + 1]
                    split[f, i : i + 1] += jnp.where(core == 0, two, one)
                    split[f, rows - 2 + i : rows - 1 + i] += jnp.where(core == 0, one, two)
            factors = inverse[:, :, LANES * b : LANES * (b + 1)]
            solved.append([jnp.sum(factors * split[f][None], axis=1) for f in range(fields)])
        for f in range(fields):
            local[f, :, columns] = together(solved[0][f], solved[1][f])


def last_message_kernel(base, composed, out):
    upper = lax.rem(lax.div(lax.axis_index("gy"), base), 2) == 1
    for b in range(out.shape[0] // LAST):
        at, to = RUN * b, LAST * b
        out[to : to + 12] = jnp.where(upper, composed[at + 12 : at + 24], composed[at : at + 12])
        out[to + 12 : to + 16] = composed[at + STATE + 4 : at + STATE + 8]


def ready_kernel(base, local, spikes, known, ready, lift):
    upper = lax.rem(lax.div(lax.axis_index("gy"), base), 2) == 1
    for b in range(known.shape[0] // RUN):
        columns = pl.ds(2 * LANES * b, 2 * LANES)
        factors = [[doubled(spikes[i, k, :, LANES * b : LANES * (b + 1)]) for k in range(2)] for i in range(2)]
        run = Piece(known, RUN * b)
        maps = doubled(known[RUN * b + STATE : RUN * (b + 1)])
        A, B, D = (matrix_of(maps, 4 * i) for i in range(3))
        t, s = ([together(v[k][0:3], v[k][3:6]) for k in range(2)] for v in (run.p, run.q))
        for f in range(3):
            value = local[f, :, columns]
            for k in range(2):
                value = value - factors[0][k] * t[k][f : f + 1] - factors[1][k] * s[k][f : f + 1]
            ready[f, :, columns] = value
        for j in range(2):
            value = jnp.zeros_like(factors[0][0])
            for k in range(2):
                through_t = factors[0][k] * A[k][j] + factors[1][k] * B[k][j]
                value = value - jnp.where(upper, through_t, factors[1][k] * D[k][j])
            lift[j, :, columns] = value


def final_kernel(base, ready, lift, composed, received, out, held, sems):
    upper = lax.rem(lax.div(lax.axis_index("gy"), base), 2) == 1
    states = []
    for b in range(composed.shape[0] // RUN):
        at, to = RUN * b, LAST * b
        mine = [composed[at : at + 6], composed[at + 6 : at + 12]]
        theirs = [received[to : to + 6], received[to + 6 : to + 12]]
        state = choose(upper, theirs, act(matrix_of(received, to + 12), mine, theirs))
        states.append([together(v[0:3], v[3:6]) for v in state])
    copies = []
    for f in range(3):
        for b, state in enumerate(states):
            columns = pl.ds(2 * LANES * b, 2 * LANES)
            value = ready[f, :, columns]
            for j in range(2):
                value = value + lift[j, :, columns] * state[j][f : f + 1]
            held[f, :, columns] = value
        copies.append(pltpu.make_async_copy(held.at[f], out.at[f], sems.at[f]))
        copies[-1].start()
    for copy in copies:
        copy.wait()


def end_pairs(gy, gz, step, flip):
    at = lambda y, z: y * gz + z
    pairs = []
    for y in range(1, gy - 1, 2):
        up, down = (y + 1) ^ flip, y ^ flip
        pairs.append((at(y, gz - 1), at(up, 2 * step)))
        pairs.append((at(y - 1, gz - 1), at(up, 2 * step + 1)))
        pairs.append((at(y + 1, 0), at(down, 2 * step + 1)))
        pairs.append((at(y + 2, 0), at(down, 2 * step)))
    sources = sorted(set(range(gy * gz)) - {s for s, _ in pairs})
    targets = sorted(set(range(gy * gz)) - {t for _, t in pairs})
    if gz == 2:
        for i in range(0, len(sources), 2):
            (a, b), (c, d) = sources[i : i + 2], targets[i : i + 2]
            pairs += [(a, d), (b, c)] if a != d and b != c else [(a, c), (b, d)]
    return pairs


def groups_of(count):
    steps, base = [(1, 2)], 2
    while 2 * base < count:
        size = 4 if base * 8 <= count else 2
        steps.append((base, size))
        base *= size
    return steps + [(base, 2)]


def per_device(velocity, explicit, bands, inverse, spikes):
    gy, gz = lax.axis_size("gy"), lax.axis_size("gz")
    own, columns = velocity.shape[1:]
    rows, modes = inverse.shape[0], inverse.shape[2]
    lanes = 2 * modes
    wide, firsts = window(rows, own, gz)
    vmem = lambda *shape: pltpu.VMEM(shape, F32)
    dma = lambda n: pltpu.SemaphoreType.DMA((n,))

    high = -(-(3 * wide + 12) // 8) * 8
    padded = (3, rows + 16, columns)
    edges, coef, weight, vel, tot = vmem_call(
        functools.partial(load_kernel, wide, firsts),
        [(12, columns), (10, rows, LANES), (10, wide, LANES), padded, padded],
        [velocity, explicit, jnp.transpose(bands, (1, 0, 2))],
        scratch=[vmem(3, own, columns)] * 2 + [vmem(5, 2, rows), vmem(LANES, LANES), dma(3)],
        name="load",
        far=3,
    )
    beside_edges = lax.ppermute(edges, "gy", [(i, i ^ 1) for i in range(gy)])

    def shares(*shifts):
        return vmem_call(
            functools.partial(stencil_kernel, wide, gz, shifts),
            [(high, lanes)] * len(shifts),
            [vel, tot, weight, edges],
            flops=2 * 10**8,
            name="stencil",
        )

    sent = shares(*range(1, gz))
    pieces = list(shares(0))
    for shift in range(1, gz):
        ring = [(i, (i + shift) % gz) for i in range(gz)]
        pieces.append(lax.ppermute(sent[shift - 1], "gz", ring))
    blocks = modes // LANES
    relays = vmem_call(
        functools.partial(relay_kernel, gz), [(24 * blocks, LANES)] * (gz // 2), [edges, beside_edges], name="relay"
    )
    near, far = (
        [lax.ppermute(relay, ("gy", "gz"), end_pairs(gy, gz, step, flip)) for step, relay in enumerate(relays)]
        for flip in (0, 1)
    )
    inv4, fixed, inside, held = vmem_call(
        prepare_kernel,
        [(4, rows, lanes), ((MAPS + 16) * blocks + 16, LANES), (rows, rows, modes), (2, 2, rows, modes)],
        [spikes, inverse, coef],
        scratch=[dma(4)],
        flops=2 * 10**10,
        name="prepare",
        far=2,
    )
    rhs, message = vmem_call(
        functools.partial(interface_kernel, wide, firsts),
        [(3, rows, lanes), (FIRST * blocks + 16, LANES)],
        [inv4, fixed, *pieces],
        scratch=[vmem(12, lanes)] * 2,
        name="interface",
    )
    other = lax.ppermute(message, "gy", [(i, i ^ 1) for i in range(gy)])
    (ends,) = vmem_call(ends_kernel, [(48 * blocks, LANES)], [*near, *far], flops=2 * 10**10, name="ends")
    run = (RUN * blocks, LANES)
    composed, mine, theirs = vmem_call(pair_kernel, [run] * 3, [message, other, ends], name="pair")

    steps = groups_of(gy)
    base, size = steps[0]
    (known,) = vmem_call(
        functools.partial(widen_kernel, base, True),
        [run],
        [mine, theirs],
        scratch=[vmem(size, *run)],
        flops=10**7,
        name="widen",
    )
    (local,) = vmem_call(
        block_kernel,
        [(3, rows, lanes)],
        [inside, rhs, message, other, ends],
        scratch=[vmem(3, rows, LANES)],
        flops=2 * 10**8,
        name="block",
    )
    for base, size in steps[1:-1]:
        gathered = [composed]
        for x in range(size - 1, 0, -1):
            gathered.append(lax.ppermute(composed, "gy", [(i, i ^ (x * base) ^ 1) for i in range(gy)]))
        board = [vmem(size, *run)]
        (composed,) = vmem_call(
            functools.partial(compose_kernel, base), [run], gathered, scratch=board, name="compose"
        )
        (known,) = vmem_call(
            functools.partial(widen_kernel, base, False),
            [run],
            [*gathered, known],
            scratch=board,
            flops=10**7,
            name="widen",
        )
    base, _ = steps[-1]
    (message,) = vmem_call(
        functools.partial(last_message_kernel, base), [(LAST * blocks, LANES)], [composed], name="last_message"
    )
    received = lax.ppermute(message, "gy", [(i, i ^ base ^ 1) for i in range(gy)])
    ready, lift = vmem_call(
        functools.partial(ready_kernel, base),
        [(3, rows, lanes), (2, rows, lanes)],
        [local, held, known],
        flops=10**7,
        name="ready",
    )
    (out,) = vmem_call(
        functools.partial(final_kernel, base),
        [(3, rows, lanes)],
        [ready, lift, composed, received],
        scratch=[vmem(3, rows, lanes), dma(3)],
        name="final",
        far_out=True,
    )
    return out


def solution(mesh):
    placed = (
        P(None, ("gy", "gz"), None),
        P(None, ("gy", "gz"), None),
        P(None, None, "gy"),
        P("gy", None, "gz"),
        P(None, None, "gy", "gz"),
    )
    return jax.shard_map(
        per_device, mesh=mesh, in_specs=placed, out_specs=P(None, "gy", "gz"), check_vma=False
    )
```

time: 22.5 us -> 22 us (0.978)
  the two profiles are of different devices: /device:TPU:0 before, /device:TPU:5 now
where the time goes in v4:
time: 22 us; the launch traced here: 21.8 us
  starting transfers between devices  9.83 us (45%)
  waiting for transfers between devices  6.83 us (31%)
  Pallas kernels  5.08 us (23%)
    pallas_call x15, Pallas kernels, vmem_call(): pl.pallas_call(body, out_shape=[jax.ShapeDtypeStruct(s, F32) for s in out...  5.08 us
    ppermute x3, waiting for transfers between devices, per_device(): lax.ppermute(composed, 'gy', [(i, i ^ x * base ^ 1) for i in range(gy)])  3.76 us
    ppermute x3, starting transfers between devices, per_device(): lax.ppermute(composed, 'gy', [(i, i ^ x * base ^ 1) for i in range(gy)])  3.5 us
    ppermute x1, starting transfers between devices, per_device(): lax.ppermute(message, 'gy', [(i, i ^ base ^ 1) for i in range(gy)])  2.38 us
    ppermute x2, starting transfers between devices, per_device(): lax.ppermute(relay, ('gy', 'gz'), end_pairs(gy, gz, step, flip))  2 us
    ppermute x1, starting transfers between devices, per_device(): other = lax.ppermute(message, 'gy', [(i, i ^ 1) for i in range(gy)])  1.13 us
    ppermute x1, waiting for transfers between devices, per_device(): other = lax.ppermute(message, 'gy', [(i, i ^ 1) for i in range(gy)])  0.91 us
    ppermute x1, waiting for transfers between devices, per_device(): lax.ppermute(message, 'gy', [(i, i ^ base ^ 1) for i in range(gy)])  0.84 us
  transfers between devices with their start and end apart: 9, of which 7 were waited for; matrix products, arithmetic and copies ran while one was open for 0% of the time, Pallas kernels for 14%

profile of v4, /device:TPU:5, one launch (start us, length us, event | category | flops | bytes accessed | tf_op | source)
XLA Modules:
  0.0 21.8 jit_solution(8661494458587580217)
XLA Ops:
  0.0 1.1 %load.1 = (f32[12,1024]{1,0:T(8,128)S(1)}, f32[10,24,128]{2,1,0:T(8,128)S(1)}, f32[10,14,128]{2,1,0:T(8,128)S(1)}, f32[3,40,1024]{2,1,0:T(8,128)S(1)}, f32[3,40,1024]{2,1,0:T(8,128)S(1)}) custom-call(f32[3,12,1024]{2,1,0:T(8,128)} %velocity.1, f32[3,12,1024]{2,1,0:T(8,128)} %explicit.1, f32[5,2,24]{2,1,0:T(2,128)} %bitcast.1), custom_call_target="tpu_custom_call" | custom-call | bytes 295872 | tf_op jit(solution)/shard_map/load/pallas_call | solution.py:19
  1.1 0.7 %collective-permute-start.2 = (f32[12,1024]{1,0:T(8,128)S(1)}, f32[12,1024]{1,0:T(8,128)S(1)}, u32[]{:S(2)}, u32[]{:S(2)}) collective-permute-start(f32[12,1024]{1,0:T(8,128)S(1)} %get-tuple-element.28.edges), channel_id=1, source_target_pairs={{0,2},{2,0},{4,6},{6,4},{8,10},{10,8},{12,14},{14,12},{16,18},{18,... | collective-permute-start | bytes 147464 | tf_op jit(solution)/shard_map/ppermute | solution.py:522
  1.9 0.1 stencil.3
  2.0 0.1 collective-permute-start
  2.1 0.7 %collective-permute-done.2.beside_edges = f32[12,1024]{1,0:T(8,128)S(1)} collective-permute-done((f32[12,1024]{1,0:T(8,128)S(1)}, f32[12,1024]{1,0:T(8,128)S(1)}, u32[]{:S(2)}, u32[]{:S(2)}) %collective-permute-start.2) | collective-permute-done | bytes 49184 | tf_op jit(solution)/shard_map/ppermute | solution.py:522
  2.8 0.1 relay.1
  2.9 1.9 %collective-permute-start.3 = (f32[48,128]{1,0:T(8,128)S(1)}, f32[48,128]{1,0:T(8,128)S(1)}, u32[]{:S(2)}, u32[]{:S(2)}) collective-permute-start(f32[48,128]{1,0:T(8,128)S(1)} %relay.1), channel_id=1, source_target_pairs={{3,4},{1,5},{4,3},{6,2},{7,8},{5,9},{8,7},{10,6},{11,12},{9,13},{1... | collective-permute-start | bytes 73736 | tf_op jit(solution)/shard_map/ppermute | solution.py:543
  4.8 0.1 collective-permute-start.4
  4.9 1.2 %prepare.1 = (f32[4,24,512]{2,1,0:T(8,128)S(1)}, f32[72,128]{1,0:T(8,128)S(1)}, f32[24,24,256]{2,1,0:T(8,128)S(1)}, f32[2,2,24,256]{3,2,1,0:T(8,128)S(1)}) custom-call(f32[2,2,24,256]{3,2,1,0:T(8,128)} %spikes.1, f32[24,24,256]{2,1,0:T(8,128)} %inverse.1, f32[10,24,128]{2,1,0:T(8,128)S(1)} %get-tuple-element.21.coef), custom_call_target="tpu_custom_call" | custom-call | flops 20000000000 | bytes 811008 | tf_op jit(solution)/shard_map/prepare/pallas_call | solution.py:19
  6.1 0.1 stencil.2.refs_0_
  6.2 0.6 %collective-permute-done.refs_1_ = f32[56,512]{1,0:T(8,128)S(1)} collective-permute-done((f32[56,512]{1,0:T(8,128)S(1)}, f32[56,512]{1,0:T(8,128)S(1)}, u32[]{:S(2)}, u32[]{:S(2)}) %collective-permute-start) | collective-permute-done | bytes 114720 | tf_op jit(solution)/shard_map/ppermute | solution.py:537
  6.8 0.3 %interface.1 = (f32[3,24,512]{2,1,0:T(8,128)S(1)}, f32[168,128]{1,0:T(8,128)S(1)}) custom-call(f32[4,24,512]{2,1,0:T(8,128)S(1)} %get-tuple-element.23.inv4, f32[72,128]{1,0:T(8,128)S(1)} %get-tuple-element.24.fixed, f32[56,512]{1,0:T(8,128)S(1)} %stencil.2.refs_0_, f32[56,512]{1,0:T(8,128)S(1)} %collective-permute-done.refs_1_), custom_call_target="tpu_custom_call" | custom-call | bytes 462848 | tf_op jit(solution)/shard_map/interface/pallas_call | solution.py:19
  7.1 1.1 %collective-permute-start.1 = (f32[168,128]{1,0:T(8,128)S(1)}, f32[168,128]{1,0:T(8,128)S(1)}, u32[]{:S(2)}, u32[]{:S(2)}) collective-permute-start(f32[168,128]{1,0:T(8,128)S(1)} %get-tuple-element.30.mine), channel_id=1, source_target_pairs={{0,2},{2,0},{4,6},{6,4},{8,10},{10,8},{12,14},{14,12},{16,18},{18,... | collective-permute-start | bytes 258056 | tf_op jit(solution)/shard_map/ppermute | solution.py:562
  8.2 0.0 collective-permute-done.3.refs_0_
  8.2 0.0 collective-permute-done.4.refs_1_
  8.2 0.9 %collective-permute-done.1.other = f32[168,128]{1,0:T(8,128)S(1)} collective-permute-done((f32[168,128]{1,0:T(8,128)S(1)}, f32[168,128]{1,0:T(8,128)S(1)}, u32[]{:S(2)}, u32[]{:S(2)}) %collective-permute-start.1) | collective-permute-done | bytes 86048 | tf_op jit(solution)/shard_map/ppermute | solution.py:562
  9.1 0.1 pair.1
  9.2 3.5 %collective-permute-start.5 = (f32[72,128]{1,0:T(8,128)S(1)}, f32[72,128]{1,0:T(8,128)S(1)}, u32[]{:S(2)}, u32[]{:S(2)}) collective-permute-start(f32[72,128]{1,0:T(8,128)S(1)} %get-tuple-element.32.refs_0_), channel_id=1, source_target_pairs={{0,14},{2,12},{4,10},{6,8},{8,6},{10,4},{12,2},{14,0},{16,30},{18,... | collective-permute-start | bytes 110600 | tf_op jit(solution)/shard_map/ppermute | solution.py:588
  12.7 0.0 collective-permute-start.6
  12.7 0.0 collective-permute-start.7
  12.7 0.1 widen.2.refs_4_
  12.8 1.7 %collective-permute-done.5.refs_1_ = f32[72,128]{1,0:T(8,128)S(1)} collective-permute-done((f32[72,128]{1,0:T(8,128)S(1)}, f32[72,128]{1,0:T(8,128)S(1)}, u32[]{:S(2)}, u32[]{:S(2)}) %collective-permute-start.5) | collective-permute-done | bytes 36896 | tf_op jit(solution)/shard_map/ppermute | solution.py:588
  14.6 1.9 %collective-permute-done.6.refs_2_ = f32[72,128]{1,0:T(8,128)S(1)} collective-permute-done((f32[72,128]{1,0:T(8,128)S(1)}, f32[72,128]{1,0:T(8,128)S(1)}, u32[]{:S(2)}, u32[]{:S(2)}) %collective-permute-start.6) | collective-permute-done | bytes 36896 | tf_op jit(solution)/shard_map/ppermute | solution.py:588
  16.4 0.1 collective-permute-done.7.refs_3_
  16.6 0.1 compose.1.composed
  16.7 2.4 %collective-permute-start.8 = (f32[32,128]{1,0:T(8,128)S(1)}, f32[32,128]{1,0:T(8,128)S(1)}, u32[]{:S(2)}, u32[]{:S(2)}) collective-permute-start(f32[32,128]{1,0:T(8,128)S(1)} %last_message.1), channel_id=1, source_target_pairs={{0,18},{2,16},{4,22},{6,20},{8,26},{10,24},{12,30},{14,28},{16,2},... | collective-permute-start | bytes 49160 | tf_op jit(solution)/shard_map/ppermute | solution.py:605
  19.1 0.7 %block.1.local = f32[3,24,512]{2,1,0:T(8,128)S(1)} custom-call(f32[24,24,256]{2,1,0:T(8,128)S(1)} %get-tuple-element.22.inverse, f32[3,24,512]{2,1,0:T(8,128)S(1)} %get-tuple-element.29.rhs, f32[168,128]{1,0:T(8,128)S(1)} %get-tuple-element.30.mine, f32[168,128]{1,0:T(8,128)S(1)} %collective-permute-done.1.other, f32[96,128]{1,0:T(8,128)S(1)} %ends.1), custom_call_target="tpu_custom_call" | custom-call | flops 200000000 | bytes 958464 | tf_op jit(solution)/shard_map/block/pallas_call | solution.py:19
  19.7 0.2 widen.3.known
  19.9 0.3 %ready.1 = (f32[3,24,512]{2,1,0:T(8,128)S(1)}, f32[2,24,512]{2,1,0:T(8,128)S(1)}) custom-call(f32[3,24,512]{2,1,0:T(8,128)S(1)} %block.1.local, f32[2,2,24,256]{3,2,1,0:T(8,128)S(1)} %get-tuple-element.31.spikes, f32[72,128]{1,0:T(8,128)S(1)} %widen.3.known), custom_call_target="tpu_custom_call" | custom-call | flops 10000000 | bytes 282624 | tf_op jit(solution)/shard_map/ready/pallas_call | solution.py:19
  20.2 0.8 %collective-permute-done.8.received = f32[32,128]{1,0:T(8,128)S(1)} collective-permute-done((f32[32,128]{1,0:T(8,128)S(1)}, f32[32,128]{1,0:T(8,128)S(1)}, u32[]{:S(2)}, u32[]{:S(2)}) %collective-permute-start.8) | collective-permute-done | bytes 16416 | tf_op jit(solution)/shard_map/ppermute | solution.py:605
  21.0 0.8 %final.1 = f32[3,24,512]{2,1,0:T(8,128)} custom-call(f32[3,24,512]{2,1,0:T(8,128)S(1)} %get-tuple-element.35.ready, f32[2,24,512]{2,1,0:T(8,128)S(1)} %get-tuple-element.36.lift, f32[72,128]{1,0:T(8,128)S(1)} %compose.1.composed, f32[32,128]{1,0:T(8,128)S(1)} %collective-permute-done.8.received), custom_call_target="tpu_custom_call" | custom-call | bytes 299008 | tf_op jit(solution)/shard_map/final/pallas_call | solution.py:19
  (2 shorter events, 0.0 us)
Async XLA Ops:
  1.1 1.6 %collective-permute-start.2 = (f32[12,1024]{1,0:T(8,128)S(1)}, f32[12,1024]{1,0:T(8,128)S(1)}, u32[]{:S(2)}, u32[]{:S(2)}) collective-permute-start(f32[12,1024]{1,0:T(8,128)S(1)} %get-tuple-element.28.edges), channel_id=1, source_target_pairs={{0,2},{2,0},{4,6},{6,4},{8,10},{10,8},{12,14},{14,12},{16,18},{18,... | collective-permute-start | bytes 147464 | tf_op jit(solution)/shard_map/ppermute | solution.py:522
  2.0 4.8 %collective-permute-start = (f32[56,512]{1,0:T(8,128)S(1)}, f32[56,512]{1,0:T(8,128)S(1)}, u32[]{:S(2)}, u32[]{:S(2)}) collective-permute-start(f32[56,512]{1,0:T(8,128)S(1)} %stencil.3), channel_id=1, source_target_pairs={{0,1},{1,0},{2,3},{3,2},{4,5},{5,4},{6,7},{7,6},{8,9},{9,8},{10,11... | collective-permute-start | bytes 344072 | tf_op jit(solution)/shard_map/ppermute | solution.py:537
  2.9 5.3 %collective-permute-start.3 = (f32[48,128]{1,0:T(8,128)S(1)}, f32[48,128]{1,0:T(8,128)S(1)}, u32[]{:S(2)}, u32[]{:S(2)}) collective-permute-start(f32[48,128]{1,0:T(8,128)S(1)} %relay.1), channel_id=1, source_target_pairs={{3,4},{1,5},{4,3},{6,2},{7,8},{5,9},{8,7},{10,6},{11,12},{9,13},{1... | collective-permute-start | bytes 73736 | tf_op jit(solution)/shard_map/ppermute | solution.py:543
  4.8 3.4 %collective-permute-start.4 = (f32[48,128]{1,0:T(8,128)S(1)}, f32[48,128]{1,0:T(8,128)S(1)}, u32[]{:S(2)}, u32[]{:S(2)}) collective-permute-start(f32[48,128]{1,0:T(8,128)S(1)} %relay.1), channel_id=1, source_target_pairs={{3,6},{1,7},{4,1},{6,0},{7,10},{5,11},{8,5},{10,4},{11,14},{9,15},... | collective-permute-start | bytes 73736 | tf_op jit(solution)/shard_map/ppermute | solution.py:543
  7.1 2.1 %collective-permute-start.1 = (f32[168,128]{1,0:T(8,128)S(1)}, f32[168,128]{1,0:T(8,128)S(1)}, u32[]{:S(2)}, u32[]{:S(2)}) collective-permute-start(f32[168,128]{1,0:T(8,128)S(1)} %get-tuple-element.30.mine), channel_id=1, source_target_pairs={{0,2},{2,0},{4,6},{6,4},{8,10},{10,8},{12,14},{14,12},{16,18},{18,... | collective-permute-start | bytes 258056 | tf_op jit(solution)/shard_map/ppermute | solution.py:562
  9.2 5.3 %collective-permute-start.5 = (f32[72,128]{1,0:T(8,128)S(1)}, f32[72,128]{1,0:T(8,128)S(1)}, u32[]{:S(2)}, u32[]{:S(2)}) collective-permute-start(f32[72,128]{1,0:T(8,128)S(1)} %get-tuple-element.32.refs_0_), channel_id=1, source_target_pairs={{0,14},{2,12},{4,10},{6,8},{8,6},{10,4},{12,2},{14,0},{16,30},{18,... | collective-permute-start | bytes 110600 | tf_op jit(solution)/shard_map/ppermute | solution.py:588
  12.7 3.7 %collective-permute-start.6 = (f32[72,128]{1,0:T(8,128)S(1)}, f32[72,128]{1,0:T(8,128)S(1)}, u32[]{:S(2)}, u32[]{:S(2)}) collective-permute-start(f32[72,128]{1,0:T(8,128)S(1)} %get-tuple-element.32.refs_0_), channel_id=1, source_target_pairs={{0,10},{2,8},{4,14},{6,12},{8,2},{10,0},{12,6},{14,4},{16,26},{18,... | collective-permute-start | bytes 110600 | tf_op jit(solution)/shard_map/ppermute | solution.py:588
  12.7 3.8 %collective-permute-start.7 = (f32[72,128]{1,0:T(8,128)S(1)}, f32[72,128]{1,0:T(8,128)S(1)}, u32[]{:S(2)}, u32[]{:S(2)}) collective-permute-start(f32[72,128]{1,0:T(8,128)S(1)} %get-tuple-element.32.refs_0_), channel_id=1, source_target_pairs={{0,6},{2,4},{4,2},{6,0},{8,14},{10,12},{12,10},{14,8},{16,22},{18,... | collective-permute-start | bytes 110600 | tf_op jit(solution)/shard_map/ppermute | solution.py:588
  16.7 4.3 %collective-permute-start.8 = (f32[32,128]{1,0:T(8,128)S(1)}, f32[32,128]{1,0:T(8,128)S(1)}, u32[]{:S(2)}, u32[]{:S(2)}) collective-permute-start(f32[32,128]{1,0:T(8,128)S(1)} %last_message.1), channel_id=1, source_target_pairs={{0,18},{2,16},{4,22},{6,20},{8,26},{10,24},{12,30},{14,28},{16,2},... | collective-permute-start | bytes 49160 | tf_op jit(solution)/shard_map/ppermute | solution.py:605

commit v5 on v4

--- a/solution.py
+++ b/solution.py
@@ -68,7 +68,7 @@
 STATE = 24
 MAPS = 12
 RUN = STATE + MAPS
-FIRST = STATE + 24 + MAPS + 16
+FIRST = STATE + 12 + MAPS + 16
 LAST = 16
 
 
@@ -89,15 +89,17 @@
     ]
 
 
-def load_kernel(wide, firsts, velocity, explicit, bands, edges, coef, weight, vel, tot, here, there, taps, square, sems):
+def load_kernel(wide, firsts, velocity, explicit, bands, inverse, spikes, *refs):
+    edges, coef, weight, vel, tot, inverse_ends, spike_ends, here, there, taps, square, sems = refs
     groups = len(firsts)
     own = velocity.shape[1]
     rows = coef.shape[1]
     g = lax.axis_index("gz")
-    copies = [
-        pltpu.make_async_copy(source, target, sems.at[i])
-        for i, (source, target) in enumerate(((bands, taps), (velocity, here), (explicit, there)))
-    ]
+    moves = [(bands, taps), (velocity, here), (explicit, there)]
+    for i, (low, tiles) in enumerate(((0, 0), (rows - 2, rows - 8))):
+        moves.append((inverse.at[pl.ds(low, 2)], inverse_ends.at[pl.ds(2 * i, 2)]))
+        moves.append((spikes.at[:, :, pl.ds(tiles, 8)], spike_ends.at[:, :, pl.ds(8 * i, 8)]))
+    copies = [pltpu.make_async_copy(source, target, sems.at[i]) for i, (source, target) in enumerate(moves)]
     for copy in copies:
         copy.start()
     square[...] = jnp.zeros_like(square)
@@ -133,30 +135,96 @@
             top += there[f, j : j + 1]
             bottom += there[f, own - HALO + j : own - HALO + j + 1]
             edges[3 * j + f : 3 * j + f + 1] = jnp.where(g == 0, top, bottom)
-
-
-def stencil_kernel(wide, groups, shifts, vel, tot, weight, edges, *outs):
+    for copy in copies[3:]:
+        copy.wait()
+
+
+def stencil(vel, tot, weights, f, wide, at):
+    total = None
+    for d in range(5):
+        low = pl.ds(8 + d - 2, wide)
+        term = weights[2 * d] * tot[f, low, at] + weights[2 * d + 1] * vel[f, low, at]
+        total = term if total is None else total + term
+    return total
+
+
+def across_weights(bands):
+    rows = bands.shape[2]
+    core = lax.rem(lax.axis_index("gy"), 2)
+    get = lambda tap, kind, row: jnp.broadcast_to(bands[tap, kind : kind + 1, row : row + 1], (1, LANES))
+    none = jnp.zeros((1, LANES), F32)
+    low = [[(0, 0), (1, 0)], [None, (0, 1)]]
+    high = [[(4, rows - 2), None], [(3, rows - 1), (4, rows - 1)]]
+    pick = lambda tap, kind: none if tap is None else get(tap[0], kind, tap[1])
+    return [
+        [[jnp.where(core == 0, pick(low[i][j], kind), pick(high[i][j], kind)) for kind in range(2)] for j in range(2)]
+        for i in range(2)
+    ]
+
+
+def store_share(out, wide, tile, at, vel, tot, weights, edges, across):
+    base = (3 * wide + 6) * tile
+    for f in range(3):
+        total = None
+        for d in range(5):
+            low = pl.ds(8 + d - 2, wide)
+            term = weights[2 * d] * tot[f, low, at] + weights[2 * d + 1] * vel[f, low, at]
+            total = term if total is None else total + term
+        out[base + wide * f : base + wide * (f + 1)] = total
+    side = beside(across, lambda kind, j: edges[6 * kind + 3 * j : 6 * kind + 3 * j + 3, at])
+    for i in range(2):
+        out[base + 3 * wide + 3 * i : base + 3 * wide + 3 * i + 3] = side[i]
+
+
+def shares_kernel(wide, vel, tot, weight, edges, bands, *outs):
+    groups = len(outs) + 1
     part = vel.shape[2] // groups
     g = lax.axis_index("gz")
-    weights = [weight[i] for i in range(10)]
-    for shift, out in zip(shifts, outs):
+    weights, across = [weight[i] for i in range(10)], across_weights(bands)
+    for shift, out in enumerate(outs, 1):
         begin = lax.rem(g + shift, groups) * part
-        for lane in range(0, part, LANES):
-            at = pl.ds(pl.multiple_of(begin + lane, LANES), LANES)
-            to = pl.ds(lane, LANES)
-            for f in range(3):
-                total = None
-                for d in range(5):
-                    low = pl.ds(8 + d - 2, wide)
-                    term = weights[2 * d] * tot[f, low, at] + weights[2 * d + 1] * vel[f, low, at]
-                    total = term if total is None else total + term
-                out[f * wide : f * wide + wide, to] = total
-            out[3 * wide : 3 * wide + 12, to] = edges[0:12, at]
+        for tile in range(part // LANES):
+            at = pl.ds(pl.multiple_of(begin + LANES * tile, LANES), LANES)
+            store_share(out, wide, tile, at, vel, tot, weights, edges, across)
+
+
+def add_share(rhs, wide, firsts, source, piece):
+    for k, first in enumerate(firsts):
+
+        @pl.when(source == k)
+        def _(first=first):
+            for tile in range(rhs.shape[2] // LANES):
+                for f in range(3):
+                    row = (3 * wide + 6) * tile + wide * f
+                    rhs[f, first : first + wide, LANES * tile : LANES * (tile + 1)] += piece[row : row + wide]
+
+
+def own_kernel(wide, firsts, vel, tot, weight, edges, bands, inv4, fixed, rhs, values, side, started, share):
+    lanes = rhs.shape[2]
+    blocks = lanes // (2 * LANES)
+    g = lax.axis_index("gz")
+    weights, across = [weight[i] for i in range(10)], across_weights(bands)
+    for tile in range(lanes // LANES):
+        at = pl.ds(pl.multiple_of(g * lanes + LANES * tile, LANES), LANES)
+        store_share(share, wide, tile, at, vel, tot, weights, edges, across)
+        row = (3 * wide + 6) * tile + 3 * wide
+        side[:, LANES * tile : LANES * (tile + 1)] = share[row : row + 6]
+    rhs[...] = jnp.zeros_like(rhs)
+    add_share(rhs, wide, firsts, g, share)
+    for f in range(3):
+        for r in range(4):
+            row = (6 if r < 2 else 0) + 3 * (r % 2) + f
+            values[row : row + 1] = jnp.sum(inv4[r] * rhs[f], axis=0, keepdims=True)
+    started[...] = jnp.zeros_like(started)
+    for b in range(blocks):
+        at = FIRST * b
+        started[at + STATE + 12 : at + FIRST] = fixed[(MAPS + 16) * b : (MAPS + 16) * (b + 1)]
+    started[FIRST * blocks : FIRST * blocks + 8] = fixed[(MAPS + 16) * blocks : (MAPS + 16) * blocks + 8]
 
 
 def store_planes(ref, at, planes):
     real, imaginary = apart(planes)
-    for i in range(4):
+    for i in range(planes.shape[0] // 3):
         ref[at + 6 * i : at + 6 * i + 3] = real[3 * i : 3 * i + 3]
         ref[at + 6 * i + 3 : at + 6 * i + 6] = imaginary[3 * i : 3 * i + 3]
 
@@ -176,16 +244,10 @@
             store_planes(out, 24 * b, jnp.where(mine, edges[:, at], beside_edges[:, at]))
 
 
-def prepare_kernel(spikes, inverse, coef, inv4, fixed, inside, near, sems):
-    rows, modes = inverse.shape[1:]
+def prepare_kernel(inverse_ends, spike_ends, coef, inv4, fixed):
+    rows, modes = inverse_ends.shape[1:]
     core = lax.rem(lax.axis_index("gy"), 2)
     gy, count = lax.axis_index("gy"), lax.axis_size("gy")
-    copies = [pltpu.make_async_copy(spikes, near, sems.at[0])]
-    for i, (low, size) in enumerate(((0, 2), (rows - 2, 2), (2, rows - 4))):
-        part = pl.ds(low, size)
-        copies.append(pltpu.make_async_copy(inverse.at[part], inside.at[part], sems.at[1 + i]))
-    for copy in copies:
-        copy.start()
     lower, upper = side_weights(coef, False), side_weights(coef, True)
     used = jnp.where(core == 0, gy > 0, gy < count - 1)
     weights = (MAPS + 16) * (modes // LANES)
@@ -194,71 +256,75 @@
             for kind in range(2):
                 at = weights + 4 * i + 2 * j + kind
                 low, high = lower[i][j][kind], upper[i][j][kind]
-                fixed[at : at + 1] = jnp.where(core == 0, high, low)
-                fixed[at + 8 : at + 9] = jnp.where(used, jnp.where(core == 0, low, high), 0.0)
-    copies[0].wait()
+                fixed[at : at + 1] = jnp.where(used, jnp.where(core == 0, low, high), 0.0)
     for b in range(modes // LANES):
         at, lanes = (MAPS + 16) * b, pl.ds(LANES * b, LANES)
         for k in range(2):
             for j in range(2):
                 row = at + 2 * k + j
-                fixed[row : row + 1] = -near[0, j, rows - 2 + k : rows - 1 + k, lanes]
-                fixed[row + 4 : row + 5] = -near[0, j, k : k + 1, lanes]
-                fixed[row + 8 : row + 9] = -near[1, j, k : k + 1, lanes]
-    copies[1].wait()
-    copies[2].wait()
-    for b in range(modes // LANES):
-        at, lanes = (MAPS + 16) * b + MAPS, pl.ds(LANES * b, LANES)
-        for r, row in enumerate((0, 1, rows - 2, rows - 1)):
-            inv4[r, :, 2 * LANES * b : 2 * LANES * (b + 1)] = doubled(inside[row, :, lanes])
+                fixed[row : row + 1] = -spike_ends[0, j, 14 + k : 15 + k, lanes]
+                fixed[row + 4 : row + 5] = -spike_ends[0, j, k : k + 1, lanes]
+                fixed[row + 8 : row + 9] = -spike_ends[1, j, k : k + 1, lanes]
+        for r in range(4):
+            inv4[r, :, 2 * LANES * b : 2 * LANES * (b + 1)] = doubled(inverse_ends[r, :, lanes])
             for i in range(2):
-                low, high = inside[row, i : i + 1, lanes], inside[row, rows - 2 + i : rows - 1 + i, lanes]
-                to = at + 2 * ((r + 2) % 4) + i
+                low, high = inverse_ends[r, i : i + 1, lanes], inverse_ends[r, rows - 2 + i : rows - 1 + i, lanes]
+                to = at + MAPS + 2 * ((r + 2) % 4) + i
                 fixed[to : to + 1] = jnp.where(core == 0, high, low)
                 fixed[to + 8 : to + 9] = jnp.where(core == 0, low, high)
-    copies[3].wait()
-
-
-def weights_of(ref, at):
-    at += ref.shape[0] - 16
+
+
+def fetch_kernel(inverse, spikes, after, inside, held, sems):
+    copies = [pltpu.make_async_copy(inverse, inside, sems.at[0]), pltpu.make_async_copy(spikes, held, sems.at[1])]
+    for copy in copies:
+        copy.start()
+    for copy in copies:
+        copy.wait()
+
+
+def weights_of(ref):
+    at = ref.shape[0] - 8
     return [
         [[ref[at + 4 * i + 2 * j + kind : at + 4 * i + 2 * j + kind + 1] for kind in range(2)] for j in range(2)]
         for i in range(2)
     ]
 
 
-def interface_kernel(wide, firsts, inv4, fixed, *refs):
+def interface_kernel(wide, firsts, inv4, started, own_values, own_side, *refs):
     groups = len(firsts)
-    *pieces, rhs, message, planes, values = refs
-    rows, lanes = rhs.shape[1:]
-    blocks = lanes // (2 * LANES)
+    *pieces, message, values, side = refs
+    tiles = values.shape[1] // LANES
     g = lax.axis_index("gz")
     core = lax.rem(lax.axis_index("gy"), 2)
-    rhs[...] = jnp.zeros_like(rhs)
-    for shift, piece in enumerate(pieces):
+    message[...] = started[...]
+    values[...] = own_values[...]
+    side[...] = own_side[...]
+    for shift, piece in enumerate(pieces, 1):
         source = lax.rem(g - shift + groups, groups)
-        for k in range(groups):
+        for k, first in enumerate(firsts):
 
             @pl.when(source == k)
-            def _(piece=piece, k=k):
-                for f in range(3):
-                    rhs[f, firsts[k] : firsts[k] + wide] += piece[f * wide : f * wide + wide]
-                if k in (0, groups - 1):
-
-                    @pl.when(core == (1 if k == 0 else 0))
-                    def _():
-                        planes[...] = piece[3 * wide : 3 * wide + 12]
-
-    for f in range(3):
-        for r in range(4):
-            row = (6 if r < 2 else 0) + 3 * (r % 2) + f
-            values[row : row + 1] = jnp.sum(inv4[r] * rhs[f], axis=0, keepdims=True)
-    for b in range(blocks):
-        at, columns = FIRST * b, pl.ds(2 * LANES * b, 2 * LANES)
-        store_planes(message, at, values[:, columns])
-        store_planes(message, at + STATE, planes[:, columns])
-        message[at + 48 : at + FIRST] = fixed[(MAPS + 16) * b : (MAPS + 16) * (b + 1)]
-    message[FIRST * blocks : FIRST * blocks + 16] = fixed[(MAPS + 16) * blocks : (MAPS + 16) * blocks + 16]
+            def _(piece=piece, first=first):
+                for tile in range(tiles):
+                    to = pl.ds(LANES * tile, LANES)
+                    for f in range(3):
+                        row = (3 * wide + 6) * tile + wide * f
+                        share = piece[row : row + wide]
+                        for r in range(4):
+                            row = (6 if r < 2 else 0) + 3 * (r % 2) + f
+                            values[row : row + 1, to] += jnp.sum(
+                                inv4[r, first : first + wide, to] * share, axis=0, keepdims=True
+                            )
+
+        @pl.when(source == jnp.where(core == 0, groups - 1, 0))
+        def _(piece=piece):
+            for tile in range(tiles):
+                row = (3 * wide + 6) * tile + 3 * wide
+                side[:, LANES * tile : LANES * (tile + 1)] = piece[row : row + 6]
+
+    for b in range(tiles // 2):
+        store_planes(message, FIRST * b, values[:, 2 * LANES * b : 2 * LANES * (b + 1)])
+        store_planes(message, FIRST * b + STATE, side[:, 2 * LANES * b : 2 * LANES * (b + 1)])
 
 
 class Piece:
@@ -336,28 +402,26 @@
 def ends_kernel(*refs):
     *ends, out = refs
     step = lax.div(lax.axis_index("gz"), 2)
-    half, size = len(ends) // 2, ends[0].shape[0]
-    for k in range(2):
-        end = ends[k * half][...]
-        for i in range(1, half):
-            end = jnp.where(step == i, ends[k * half + i][...], end)
-        out[size * k : size * (k + 1)] = end
-
-
-def pair_kernel(mine, other, ends, out, fixed_mine, fixed_other):
+    end = ends[0][...]
+    for i in range(1, len(ends)):
+        end = jnp.where(step == i, ends[i][...], end)
+    out[...] = end
+
+
+def pair_kernel(mine, other, end_mine, end_other, out, fixed_mine, fixed_other):
     core = lax.rem(lax.axis_index("gy"), 2)
     blocks = out.shape[0] // RUN
-    for ref, across, side, target in ((mine, other, 0, fixed_mine), (other, mine, 1, fixed_other)):
-        inner_weights, outer_weights = weights_of(ref, 0), weights_of(ref, 8)
+    for ref, across, end, target in ((mine, other, end_mine, fixed_mine), (other, mine, end_other, fixed_other)):
+        outer_weights = weights_of(ref)
         for b in range(blocks):
             at, to = FIRST * b, RUN * b
-            inner = beside(inner_weights, planes_of(across, at + STATE))
-            outer = beside(outer_weights, planes_of(ends, 24 * (side * blocks + b)))
-            target[to + STATE : to + RUN] = ref[at + 48 : at + 48 + MAPS]
+            inner = [across[at + STATE + 6 * i : at + STATE + 6 * i + 6] for i in range(2)]
+            outer = beside(outer_weights, planes_of(end, 24 * b))
+            target[to + STATE : to + RUN] = ref[at + 36 : at + 36 + MAPS]
             for k in range(4):
                 value = ref[at + 6 * k : at + 6 * k + 6]
                 for i in range(2):
-                    row = at + 48 + MAPS + 2 * k + i
+                    row = at + 36 + MAPS + 2 * k + i
                     value = value + ref[row : row + 1] * inner[i] + ref[row + 8 : row + 9] * outer[i]
                 target[to + 6 * k : to + 6 * k + 6] = value
     low = jnp.where(core == 0, fixed_mine[...], fixed_other[...])
@@ -396,16 +460,21 @@
             )
 
 
-def block_kernel(inverse, rhs, mine, other, ends, local, split):
+def block_kernel(wide, firsts, inverse, own_rhs, mine, other, end, *refs):
+    *pieces, local, rhs, split = refs
     fields, rows, lanes = rhs.shape
+    g = lax.axis_index("gz")
+    rhs[...] = own_rhs[...]
+    for shift, piece in enumerate(pieces, 1):
+        add_share(rhs, wide, firsts, lax.rem(g - shift + len(firsts), len(firsts)), piece)
     core = lax.rem(lax.axis_index("gy"), 2)
-    inner_weights, outer_weights = weights_of(mine, 0), weights_of(mine, 8)
+    outer_weights = weights_of(mine)
     flat = rhs[...].reshape(fields * rows, lanes)
     for b in range(lanes // (2 * LANES)):
         columns = pl.ds(2 * LANES * b, 2 * LANES)
         parts = apart(flat[:, 2 * LANES * b : 2 * LANES * (b + 1)])
-        inner = beside(inner_weights, planes_of(other, FIRST * b + STATE))
-        outer = beside(outer_weights, planes_of(ends, 24 * b))
+        inner = [other[FIRST * b + STATE + 6 * i : FIRST * b + STATE + 6 * i + 6] for i in range(2)]
+        outer = beside(outer_weights, planes_of(end, 24 * b))
         solved = []
         for p in range(2):
             split[...] = parts[p].reshape(fields, rows, LANES)
@@ -473,15 +542,14 @@
         copy.wait()
 
 
-def end_pairs(gy, gz, step, flip):
+def end_pairs(gy, gz, step):
     at = lambda y, z: y * gz + z
     pairs = []
     for y in range(1, gy - 1, 2):
-        up, down = (y + 1) ^ flip, y ^ flip
-        pairs.append((at(y, gz - 1), at(up, 2 * step)))
-        pairs.append((at(y - 1, gz - 1), at(up, 2 * step + 1)))
-        pairs.append((at(y + 1, 0), at(down, 2 * step + 1)))
-        pairs.append((at(y + 2, 0), at(down, 2 * step)))
+        for core in range(2):
+            column = 2 * step + 1 - core
+            pairs.append((at(y - 1 + core, gz - 1), at(y + 1, column)))
+            pairs.append((at(y + 1 + core, 0), at(y, column)))
     sources = sorted(set(range(gy * gz)) - {s for s, _ in pairs})
     targets = sorted(set(range(gy * gz)) - {t for _, t in pairs})
     if gz == 2:
@@ -509,61 +577,74 @@
     vmem = lambda *shape: pltpu.VMEM(shape, F32)
     dma = lambda n: pltpu.SemaphoreType.DMA((n,))
 
-    high = -(-(3 * wide + 12) // 8) * 8
+    blocks = modes // LANES
+    taps = jnp.transpose(bands, (1, 0, 2))
+    to_core = lambda x: lax.ppermute(x, "gy", [(i, i ^ 1) for i in range(gy)])
+    beside_taps = to_core(taps)
     padded = (3, rows + 16, columns)
-    edges, coef, weight, vel, tot = vmem_call(
+    edges, coef, weight, vel, tot, inverse_ends, spike_ends = vmem_call(
         functools.partial(load_kernel, wide, firsts),
-        [(12, columns), (10, rows, LANES), (10, wide, LANES), padded, padded],
-        [velocity, explicit, jnp.transpose(bands, (1, 0, 2))],
-        scratch=[vmem(3, own, columns)] * 2 + [vmem(5, 2, rows), vmem(LANES, LANES), dma(3)],
+        [(12, columns), (10, rows, LANES), (10, wide, LANES), padded, padded, (4, rows, modes), (2, 2, 16, modes)],
+        [velocity, explicit, taps, inverse, spikes],
+        scratch=[vmem(3, own, columns)] * 2 + [vmem(5, 2, rows), vmem(LANES, LANES), dma(7)],
+        flops=2 * 10**10,
         name="load",
-        far=3,
-    )
-    beside_edges = lax.ppermute(edges, "gy", [(i, i ^ 1) for i in range(gy)])
-
-    def shares(*shifts):
-        return vmem_call(
-            functools.partial(stencil_kernel, wide, gz, shifts),
-            [(high, lanes)] * len(shifts),
-            [vel, tot, weight, edges],
-            flops=2 * 10**8,
-            name="stencil",
-        )
-
-    sent = shares(*range(1, gz))
-    pieces = list(shares(0))
-    for shift in range(1, gz):
-        ring = [(i, (i + shift) % gz) for i in range(gz)]
-        pieces.append(lax.ppermute(sent[shift - 1], "gz", ring))
-    blocks = modes // LANES
+        far=5,
+    )
+    beside_edges = to_core(edges)
+    share = ((3 * wide + 6) * 2 * blocks, LANES)
+    shares = vmem_call(
+        functools.partial(shares_kernel, wide),
+        [share] * (gz - 1),
+        [vel, tot, weight, edges, beside_taps],
+        flops=2 * 10**10,
+        name="shares",
+    )
+    pieces = [
+        lax.ppermute(x, "gz", [(i, (i + shift) % gz) for i in range(gz)]) for shift, x in enumerate(shares, 1)
+    ]
     relays = vmem_call(
         functools.partial(relay_kernel, gz), [(24 * blocks, LANES)] * (gz // 2), [edges, beside_edges], name="relay"
     )
-    near, far = (
-        [lax.ppermute(relay, ("gy", "gz"), end_pairs(gy, gz, step, flip)) for step, relay in enumerate(relays)]
-        for flip in (0, 1)
-    )
-    inv4, fixed, inside, held = vmem_call(
+    ends = [lax.ppermute(x, ("gy", "gz"), end_pairs(gy, gz, step)) for step, x in enumerate(relays)]
+    inv4, fixed = vmem_call(
         prepare_kernel,
-        [(4, rows, lanes), ((MAPS + 16) * blocks + 16, LANES), (rows, rows, modes), (2, 2, rows, modes)],
-        [spikes, inverse, coef],
-        scratch=[dma(4)],
+        [(4, rows, lanes), ((MAPS + 16) * blocks + 8, LANES)],
+        [inverse_ends, spike_ends, coef],
         flops=2 * 10**10,
         name="prepare",
+    )
+    first = (FIRST * blocks + 8, LANES)
+    rhs, values, side, started = vmem_call(
+        functools.partial(own_kernel, wide, firsts),
+        [(3, rows, lanes), (12, lanes), (6, lanes), first],
+        [vel, tot, weight, edges, beside_taps, inv4, fixed],
+        scratch=[vmem(*share)],
+        flops=2 * 10**8,
+        name="own",
+    )
+    (message,) = vmem_call(
+        functools.partial(interface_kernel, wide, firsts),
+        [first],
+        [inv4, started, values, side, *pieces],
+        scratch=[vmem(12, lanes), vmem(6, lanes)],
+        name="interface",
+    )
+    other = to_core(message)
+    (end,) = vmem_call(ends_kernel, [(24 * blocks, LANES)], ends, flops=2 * 10**10, name="ends")
+    other_end = to_core(end)
+    run = (RUN * blocks, LANES)
+    composed, mine, theirs = vmem_call(pair_kernel, [run] * 3, [message, other, end, other_end], name="pair")
+
+    inside, held = vmem_call(
+        fetch_kernel,
+        [(rows, rows, modes), (2, 2, rows, modes)],
+        [inverse, spikes, composed],
+        scratch=[dma(2)],
+        flops=2 * 10**10,
+        name="fetch",
         far=2,
     )
-    rhs, message = vmem_call(
-        functools.partial(interface_kernel, wide, firsts),
-        [(3, rows, lanes), (FIRST * blocks + 16, LANES)],
-        [inv4, fixed, *pieces],
-        scratch=[vmem(12, lanes)] * 2,
-        name="interface",
-    )
-    other = lax.ppermute(message, "gy", [(i, i ^ 1) for i in range(gy)])
-    (ends,) = vmem_call(ends_kernel, [(48 * blocks, LANES)], [*near, *far], flops=2 * 10**10, name="ends")
-    run = (RUN * blocks, LANES)
-    composed, mine, theirs = vmem_call(pair_kernel, [run] * 3, [message, other, ends], name="pair")
-
     steps = groups_of(gy)
     base, size = steps[0]
     (known,) = vmem_call(
@@ -575,10 +656,10 @@
         name="widen",
     )
     (local,) = vmem_call(
-        block_kernel,
+        functools.partial(block_kernel, wide, firsts),
         [(3, rows, lanes)],
-        [inside, rhs, message, other, ends],
-        scratch=[vmem(3, rows, LANES)],
+        [inside, rhs, message, other, end, *pieces],
+        scratch=[vmem(3, rows, lanes), vmem(3, rows, LANES)],
         flops=2 * 10**8,
         name="block",
     )

time: 22 us -> 22 us (level)
  the two profiles are of different devices: /device:TPU:5 before, /device:TPU:0 now
where the time goes in v5:
time: 22 us; the launch traced here: 21.8 us
  starting transfers between devices  12 us (55%)
  Pallas kernels  5.3 us (24%)
  waiting for transfers between devices  4.42 us (20%)
    pallas_call x16, Pallas kernels, vmem_call(): pl.pallas_call(body, out_shape=[jax.ShapeDtypeStruct(s, F32) for s in out...  5.3 us
    ppermute x3, starting transfers between devices, per_device(): lax.ppermute(composed, 'gy', [(i, i ^ x * base ^ 1) for i in range(gy)])  4.64 us
    ppermute x1, starting transfers between devices, per_device(): lax.ppermute(x, 'gz', [(i, (i + shift) % gz) for i in range(gz)])  3.04 us
    ppermute x1, starting transfers between devices, per_device(): lax.ppermute(message, 'gy', [(i, i ^ base ^ 1) for i in range(gy)])  2.42 us
    ppermute x1, waiting for transfers between devices, per_device(): lax.ppermute(x, 'gz', [(i, (i + shift) % gz) for i in range(gz)])  1.72 us
    ppermute x3, waiting for transfers between devices, per_device(): lax.ppermute(composed, 'gy', [(i, i ^ x * base ^ 1) for i in range(gy)])  1.28 us
    ppermute x4, starting transfers between devices, per_device(): to_core = lambda x: lax.ppermute(x, 'gy', [(i, i ^ 1) for i in range(gy)])  1.13 us
    ppermute x4, waiting for transfers between devices, per_device(): to_core = lambda x: lax.ppermute(x, 'gy', [(i, i ^ 1) for i in range(gy)])  0.86 us
  transfers between devices with their start and end apart: 10, of which 5 were waited for; matrix products, arithmetic and copies ran while one was open for 0% of the time, Pallas kernels for 20%

profile of v5, /device:TPU:0, one launch (start us, length us, event | category | flops | bytes accessed | tf_op | source)
XLA Modules:
  0.0 21.8 jit_solution(17782874432059395459)
XLA Ops:
  0.0 0.5 %collective-permute-start = (f32[5,2,24]{2,1,0:T(2,128)}, f32[5,2,24]{2,1,0:T(2,128)S(1)}, u32[]{:S(2)}, u32[]{:S(2)}) collective-permute-start(f32[5,2,24]{2,1,0:T(2,128)} %bitcast.1), channel_id=1, source_target_pairs={{0,2},{2,0},{4,6},{6,4},{8,10},{10,8},{12,14},{14,12},{16,18},{18,... | collective-permute-start | bytes 2888 | tf_op jit(solution)/shard_map/ppermute | solution.py:582
  0.5 1.2 %load.1 = (f32[12,1024]{1,0:T(8,128)S(1)}, f32[10,24,128]{2,1,0:T(8,128)S(1)}, f32[10,14,128]{2,1,0:T(8,128)S(1)}, f32[3,40,1024]{2,1,0:T(8,128)S(1)}, f32[3,40,...) custom-call(f32[3,12,1024]{2,1,0:T(8,128)} %velocity.1, f32[3,12,1024]{2,1,0:T(8,128)} %explicit.1, ...), custom_call_target="tpu_custom_call" | custom-call | flops 20000000000 | bytes 984000 | tf_op jit(solution)/shard_map/load/pallas_call | solution.py:19
  1.6 0.1 collective-permute-start.3
  1.7 0.0 collective-permute-done.bands
  1.7 0.1 shares.1
  1.9 3.0 %collective-permute-start.1 = (f32[192,128]{1,0:T(8,128)S(1)}, f32[192,128]{1,0:T(8,128)S(1)}, u32[]{:S(2)}, u32[]{:S(2)}) collective-permute-start(f32[192,128]{1,0:T(8,128)S(1)} %shares.1), channel_id=1, source_target_pairs={{0,1},{1,0},{2,3},{3,2},{4,5},{5,4},{6,7},{7,6},{8,9},{9,8},{10,11... | collective-permute-start | bytes 294920 | tf_op jit(solution)/shard_map/ppermute | solution.py:604
  4.9 0.0 collective-permute-done.3.beside_edges
  4.9 0.1 relay.1
  5.0 0.7 %collective-permute-start.4 = (f32[48,128]{1,0:T(8,128)S(1)}, f32[48,128]{1,0:T(8,128)S(1)}, u32[]{:S(2)}, u32[]{:S(2)}) collective-permute-start(f32[48,128]{1,0:T(8,128)S(1)} %relay.1), channel_id=1, source_target_pairs={{1,5},{4,3},{3,4},{6,2},{5,9},{8,7},{7,8},{10,6},{9,13},{12,11},{1... | collective-permute-start | bytes 73736 | tf_op jit(solution)/shard_map/ppermute | solution.py:609
  5.8 0.2 prepare.1
  5.9 0.3 %own.1 = (f32[3,24,512]{2,1,0:T(8,128)S(1)}, f32[12,512]{1,0:T(8,128)S(1)}, f32[6,512]{1,0:T(8,128)S(1)}, f32[136,128]{1,0:T(8,128)S(1)}) custom-call(f32[3,40,1024]{2,1,0:T(8,128)S(1)} %get-tuple-element.29.vel, f32[3,40,1024]{2,1,0:T(8,128)S(1)} %get-tuple-element.30.tot, f32[10,14,128]{2,1,0:T(8,128)S(1)} %get-tuple-element.31.weight, ...), custom_call_target="tpu_custom_call" | custom-call | flops 200000000 | bytes 1334208 | tf_op jit(solution)/shard_map/own/pallas_call | solution.py:19
  6.2 1.7 %collective-permute-done.1.refs_0_ = f32[192,128]{1,0:T(8,128)S(1)} collective-permute-done((f32[192,128]{1,0:T(8,128)S(1)}, f32[192,128]{1,0:T(8,128)S(1)}, u32[]{:S(2)}, u32[]{:S(2)}) %collective-permute-start.1) | collective-permute-done | bytes 98336 | tf_op jit(solution)/shard_map/ppermute | solution.py:604
  7.9 0.2 %interface.1.mine = f32[136,128]{1,0:T(8,128)S(1)} custom-call(f32[4,24,512]{2,1,0:T(8,128)S(1)} %get-tuple-element.28.inv4, f32[136,128]{1,0:T(8,128)S(1)} %get-tuple-element.34.started, f32[12,512]{1,0:T(8,128)S(1)} %get-tuple-element.35.own_values, f32[6,512]{1,0:T(8,128)S(1)} %get-tuple-element.36.own_side, f32[192,128]{1,0:T(8,128)S(1)} %collective-permute-done.1.refs_0_), custom_call_target="tpu_custom_call" | custom-call | bytes 401408 | tf_op jit(solution)/shard_map/interface/pallas_call | solution.py:19
  8.2 0.1 collective-permute-start.2
  8.2 0.0 collective-permute-done.4.refs_0_
  8.3 0.5 %collective-permute-start.5 = (f32[48,128]{1,0:T(8,128)S(1)}, f32[48,128]{1,0:T(8,128)S(1)}, u32[]{:S(2)}, u32[]{:S(2)}) collective-permute-start(f32[48,128]{1,0:T(8,128)S(1)} %ends.1.end_mine.end), channel_id=1, source_target_pairs={{0,2},{2,0},{4,6},{6,4},{8,10},{10,8},{12,14},{14,12},{16,18},{18,... | collective-permute-start | bytes 73736 | tf_op jit(solution)/shard_map/ppermute | solution.py:582
  8.7 0.8 %collective-permute-done.5.end_other = f32[48,128]{1,0:T(8,128)S(1)} collective-permute-done((f32[48,128]{1,0:T(8,128)S(1)}, f32[48,128]{1,0:T(8,128)S(1)}, u32[]{:S(2)}, u32[]{:S(2)}) %collective-permute-start.5) | collective-permute-done | bytes 24608 | tf_op jit(solution)/shard_map/ppermute | solution.py:582
  9.6 0.0 collective-permute-done.2.other
  9.6 0.1 pair.1
  9.7 3.2 %collective-permute-start.6 = (f32[72,128]{1,0:T(8,128)S(1)}, f32[72,128]{1,0:T(8,128)S(1)}, u32[]{:S(2)}, u32[]{:S(2)}) collective-permute-start(f32[72,128]{1,0:T(8,128)S(1)} %get-tuple-element.37.after.refs_0_), channel_id=1, source_target_pairs={{0,14},{2,12},{4,10},{6,8},{8,6},{10,4},{12,2},{14,0},{16,30},{18,... | collective-permute-start | bytes 110600 | tf_op jit(solution)/shard_map/ppermute | solution.py:669
  12.9 0.4 %collective-permute-start.7 = (f32[72,128]{1,0:T(8,128)S(1)}, f32[72,128]{1,0:T(8,128)S(1)}, u32[]{:S(2)}, u32[]{:S(2)}) collective-permute-start(f32[72,128]{1,0:T(8,128)S(1)} %get-tuple-element.37.after.refs_0_), channel_id=1, source_target_pairs={{0,10},{2,8},{4,14},{6,12},{8,2},{10,0},{12,6},{14,4},{16,26},{18,... | collective-permute-start | bytes 110600 | tf_op jit(solution)/shard_map/ppermute | solution.py:669
  13.3 1.0 %collective-permute-start.8 = (f32[72,128]{1,0:T(8,128)S(1)}, f32[72,128]{1,0:T(8,128)S(1)}, u32[]{:S(2)}, u32[]{:S(2)}) collective-permute-start(f32[72,128]{1,0:T(8,128)S(1)} %get-tuple-element.37.after.refs_0_), channel_id=1, source_target_pairs={{0,6},{2,4},{4,2},{6,0},{8,14},{10,12},{12,10},{14,8},{16,22},{18,... | collective-permute-start | bytes 110600 | tf_op jit(solution)/shard_map/ppermute | solution.py:669
  14.3 1.1 %fetch.1 = (f32[24,24,256]{2,1,0:T(8,128)S(1)}, f32[2,2,24,256]{3,2,1,0:T(8,128)S(1)}) custom-call(f32[24,24,256]{2,1,0:T(8,128)} %inverse.3, f32[2,2,24,256]{3,2,1,0:T(8,128)} %spikes.3, f32[72,128]{1,0:T(8,128)S(1)} %get-tuple-element.37.after.refs_0_), custom_call_target="tpu_custom_call" | custom-call | flops 20000000000 | bytes 724992 | tf_op jit(solution)/shard_map/fetch/pallas_call | solution.py:19
  15.4 0.1 widen.2.refs_4_
  15.5 0.0 collective-permute-done.6.refs_1_
  15.5 0.8 %collective-permute-done.7.refs_2_ = f32[72,128]{1,0:T(8,128)S(1)} collective-permute-done((f32[72,128]{1,0:T(8,128)S(1)}, f32[72,128]{1,0:T(8,128)S(1)}, u32[]{:S(2)}, u32[]{:S(2)}) %collective-permute-start.7) | collective-permute-done | bytes 36896 | tf_op jit(solution)/shard_map/ppermute | solution.py:669
  16.3 0.5 %collective-permute-done.8.refs_3_ = f32[72,128]{1,0:T(8,128)S(1)} collective-permute-done((f32[72,128]{1,0:T(8,128)S(1)}, f32[72,128]{1,0:T(8,128)S(1)}, u32[]{:S(2)}, u32[]{:S(2)}) %collective-permute-start.8) | collective-permute-done | bytes 36896 | tf_op jit(solution)/shard_map/ppermute | solution.py:669
  16.8 0.1 compose.1.composed
  16.9 2.4 %collective-permute-start.9 = (f32[32,128]{1,0:T(8,128)S(1)}, f32[32,128]{1,0:T(8,128)S(1)}, u32[]{:S(2)}, u32[]{:S(2)}) collective-permute-start(f32[32,128]{1,0:T(8,128)S(1)} %last_message.1), channel_id=1, source_target_pairs={{0,18},{2,16},{4,22},{6,20},{8,26},{10,24},{12,30},{14,28},{16,2},... | collective-permute-start | bytes 49160 | tf_op jit(solution)/shard_map/ppermute | solution.py:686
  19.3 0.7 %block.1.local = f32[3,24,512]{2,1,0:T(8,128)S(1)} custom-call(f32[24,24,256]{2,1,0:T(8,128)S(1)} %get-tuple-element.38.inverse, f32[3,24,512]{2,1,0:T(8,128)S(1)} %get-tuple-element.39.own_rhs, f32[136,128]{1,0:T(8,128)S(1)} %interface.1.mine, f32[136,128]{1,0:T(8,128)S(1)} %collective-permute-done.2.other, f32[48,128]{1,0:T(8,128)S(1)} %ends.1.end_mine.end, ...), custom_call_target="tpu_custom_call" | custom-call | flops 200000000 | bytes 999424 | tf_op jit(solution)/shard_map/block/pallas_call | solution.py:19
  20.0 0.2 widen.3.known
  20.2 0.3 %ready.1 = (f32[3,24,512]{2,1,0:T(8,128)S(1)}, f32[2,24,512]{2,1,0:T(8,128)S(1)}) custom-call(f32[3,24,512]{2,1,0:T(8,128)S(1)} %block.1.local, f32[2,2,24,256]{3,2,1,0:T(8,128)S(1)} %get-tuple-element.40.spikes, f32[72,128]{1,0:T(8,128)S(1)} %widen.3.known), custom_call_target="tpu_custom_call" | custom-call | flops 10000000 | bytes 282624 | tf_op jit(solution)/shard_map/ready/pallas_call | solution.py:19
  20.4 0.6 %collective-permute-done.9.received = f32[32,128]{1,0:T(8,128)S(1)} collective-permute-done((f32[32,128]{1,0:T(8,128)S(1)}, f32[32,128]{1,0:T(8,128)S(1)}, u32[]{:S(2)}, u32[]{:S(2)}) %collective-permute-start.9) | collective-permute-done | bytes 16416 | tf_op jit(solution)/shard_map/ppermute | solution.py:686
  21.0 0.8 %final.1 = f32[3,24,512]{2,1,0:T(8,128)} custom-call(f32[3,24,512]{2,1,0:T(8,128)S(1)} %get-tuple-element.43.ready, f32[2,24,512]{2,1,0:T(8,128)S(1)} %get-tuple-element.44.lift, f32[72,128]{1,0:T(8,128)S(1)} %compose.1.composed, f32[32,128]{1,0:T(8,128)S(1)} %collective-permute-done.9.received), custom_call_target="tpu_custom_call" | custom-call | bytes 299008 | tf_op jit(solution)/shard_map/final/pallas_call | solution.py:19
  (2 shorter events, 0.0 us)
Async XLA Ops:
  0.0 1.7 %collective-permute-start = (f32[5,2,24]{2,1,0:T(2,128)}, f32[5,2,24]{2,1,0:T(2,128)S(1)}, u32[]{:S(2)}, u32[]{:S(2)}) collective-permute-start(f32[5,2,24]{2,1,0:T(2,128)} %bitcast.1), channel_id=1, source_target_pairs={{0,2},{2,0},{4,6},{6,4},{8,10},{10,8},{12,14},{14,12},{16,18},{18,... | collective-permute-start | bytes 2888 | tf_op jit(solution)/shard_map/ppermute | solution.py:582
  1.6 3.3 %collective-permute-start.3 = (f32[12,1024]{1,0:T(8,128)S(1)}, f32[12,1024]{1,0:T(8,128)S(1)}, u32[]{:S(2)}, u32[]{:S(2)}) collective-permute-start(f32[12,1024]{1,0:T(8,128)S(1)} %get-tuple-element.32.edges), channel_id=1, source_target_pairs={{0,2},{2,0},{4,6},{6,4},{8,10},{10,8},{12,14},{14,12},{16,18},{18,... | collective-permute-start | bytes 147464 | tf_op jit(solution)/shard_map/ppermute | solution.py:582
  1.9 6.0 %collective-permute-start.1 = (f32[192,128]{1,0:T(8,128)S(1)}, f32[192,128]{1,0:T(8,128)S(1)}, u32[]{:S(2)}, u32[]{:S(2)}) collective-permute-start(f32[192,128]{1,0:T(8,128)S(1)} %shares.1), channel_id=1, source_target_pairs={{0,1},{1,0},{2,3},{3,2},{4,5},{5,4},{6,7},{7,6},{8,9},{9,8},{10,11... | collective-permute-start | bytes 294920 | tf_op jit(solution)/shard_map/ppermute | solution.py:604
  5.0 3.2 %collective-permute-start.4 = (f32[48,128]{1,0:T(8,128)S(1)}, f32[48,128]{1,0:T(8,128)S(1)}, u32[]{:S(2)}, u32[]{:S(2)}) collective-permute-start(f32[48,128]{1,0:T(8,128)S(1)} %relay.1), channel_id=1, source_target_pairs={{1,5},{4,3},{3,4},{6,2},{5,9},{8,7},{7,8},{10,6},{9,13},{12,11},{1... | collective-permute-start | bytes 73736 | tf_op jit(solution)/shard_map/ppermute | solution.py:609
  8.2 1.4 %collective-permute-start.2 = (f32[136,128]{1,0:T(8,128)S(1)}, f32[136,128]{1,0:T(8,128)S(1)}, u32[]{:S(2)}, u32[]{:S(2)}) collective-permute-start(f32[136,128]{1,0:T(8,128)S(1)} %interface.1.mine), channel_id=1, source_target_pairs={{0,2},{2,0},{4,6},{6,4},{8,10},{10,8},{12,14},{14,12},{16,18},{18,... | collective-permute-start | bytes 208904 | tf_op jit(solution)/shard_map/ppermute | solution.py:582
  8.3 1.3 %collective-permute-start.5 = (f32[48,128]{1,0:T(8,128)S(1)}, f32[48,128]{1,0:T(8,128)S(1)}, u32[]{:S(2)}, u32[]{:S(2)}) collective-permute-start(f32[48,128]{1,0:T(8,128)S(1)} %ends.1.end_mine.end), channel_id=1, source_target_pairs={{0,2},{2,0},{4,6},{6,4},{8,10},{10,8},{12,14},{14,12},{16,18},{18,... | collective-permute-start | bytes 73736 | tf_op jit(solution)/shard_map/ppermute | solution.py:582
  9.7 5.8 %collective-permute-start.6 = (f32[72,128]{1,0:T(8,128)S(1)}, f32[72,128]{1,0:T(8,128)S(1)}, u32[]{:S(2)}, u32[]{:S(2)}) collective-permute-start(f32[72,128]{1,0:T(8,128)S(1)} %get-tuple-element.37.after.refs_0_), channel_id=1, source_target_pairs={{0,14},{2,12},{4,10},{6,8},{8,6},{10,4},{12,2},{14,0},{16,30},{18,... | collective-permute-start | bytes 110600 | tf_op jit(solution)/shard_map/ppermute | solution.py:669
  12.9 3.4 %collective-permute-start.7 = (f32[72,128]{1,0:T(8,128)S(1)}, f32[72,128]{1,0:T(8,128)S(1)}, u32[]{:S(2)}, u32[]{:S(2)}) collective-permute-start(f32[72,128]{1,0:T(8,128)S(1)} %get-tuple-element.37.after.refs_0_), channel_id=1, source_target_pairs={{0,10},{2,8},{4,14},{6,12},{8,2},{10,0},{12,6},{14,4},{16,26},{18,... | collective-permute-start | bytes 110600 | tf_op jit(solution)/shard_map/ppermute | solution.py:669
  13.3 3.4 %collective-permute-start.8 = (f32[72,128]{1,0:T(8,128)S(1)}, f32[72,128]{1,0:T(8,128)S(1)}, u32[]{:S(2)}, u32[]{:S(2)}) collective-permute-start(f32[72,128]{1,0:T(8,128)S(1)} %get-tuple-element.37.after.refs_0_), channel_id=1, source_target_pairs={{0,6},{2,4},{4,2},{6,0},{8,14},{10,12},{12,10},{14,8},{16,22},{18,... | collective-permute-start | bytes 110600 | tf_op jit(solution)/shard_map/ppermute | solution.py:669
  16.9 4.1 %collective-permute-start.9 = (f32[32,128]{1,0:T(8,128)S(1)}, f32[32,128]{1,0:T(8,128)S(1)}, u32[]{:S(2)}, u32[]{:S(2)}) collective-permute-start(f32[32,128]{1,0:T(8,128)S(1)} %last_message.1), channel_id=1, source_target_pairs={{0,18},{2,16},{4,22},{6,20},{8,26},{10,24},{12,30},{14,28},{16,2},... | collective-permute-start | bytes 49160 | tf_op jit(solution)/shard_map/ppermute | solution.py:686

commit v6 on v5

--- a/solution.py
+++ b/solution.py
@@ -68,7 +68,7 @@
 STATE = 24
 MAPS = 12
 RUN = STATE + MAPS
-FIRST = STATE + 12 + MAPS + 16
+FIRST = STATE + 24 + MAPS + 16
 LAST = 16
 
 
@@ -148,22 +148,8 @@
     return total
 
 
-def across_weights(bands):
-    rows = bands.shape[2]
-    core = lax.rem(lax.axis_index("gy"), 2)
-    get = lambda tap, kind, row: jnp.broadcast_to(bands[tap, kind : kind + 1, row : row + 1], (1, LANES))
-    none = jnp.zeros((1, LANES), F32)
-    low = [[(0, 0), (1, 0)], [None, (0, 1)]]
-    high = [[(4, rows - 2), None], [(3, rows - 1), (4, rows - 1)]]
-    pick = lambda tap, kind: none if tap is None else get(tap[0], kind, tap[1])
-    return [
-        [[jnp.where(core == 0, pick(low[i][j], kind), pick(high[i][j], kind)) for kind in range(2)] for j in range(2)]
-        for i in range(2)
-    ]
-
-
-def store_share(out, wide, tile, at, vel, tot, weights, edges, across):
-    base = (3 * wide + 6) * tile
+def store_share(out, wide, tile, at, vel, tot, weights, edges):
+    base = (3 * wide + 12) * tile
     for f in range(3):
         total = None
         for d in range(5):
@@ -171,21 +157,19 @@
             term = weights[2 * d] * tot[f, low, at] + weights[2 * d + 1] * vel[f, low, at]
             total = term if total is None else total + term
         out[base + wide * f : base + wide * (f + 1)] = total
-    side = beside(across, lambda kind, j: edges[6 * kind + 3 * j : 6 * kind + 3 * j + 3, at])
-    for i in range(2):
-        out[base + 3 * wide + 3 * i : base + 3 * wide + 3 * i + 3] = side[i]
-
-
-def shares_kernel(wide, vel, tot, weight, edges, bands, *outs):
+    out[base + 3 * wide : base + 3 * wide + 12] = edges[:, at]
+
+
+def shares_kernel(wide, vel, tot, weight, edges, *outs):
     groups = len(outs) + 1
     part = vel.shape[2] // groups
     g = lax.axis_index("gz")
-    weights, across = [weight[i] for i in range(10)], across_weights(bands)
+    weights = [weight[i] for i in range(10)]
     for shift, out in enumerate(outs, 1):
         begin = lax.rem(g + shift, groups) * part
         for tile in range(part // LANES):
             at = pl.ds(pl.multiple_of(begin + LANES * tile, LANES), LANES)
-            store_share(out, wide, tile, at, vel, tot, weights, edges, across)
+            store_share(out, wide, tile, at, vel, tot, weights, edges)
 
 
 def add_share(rhs, wide, firsts, source, piece):
@@ -195,20 +179,20 @@
         def _(first=first):
             for tile in range(rhs.shape[2] // LANES):
                 for f in range(3):
-                    row = (3 * wide + 6) * tile + wide * f
+                    row = (3 * wide + 12) * tile + wide * f
                     rhs[f, first : first + wide, LANES * tile : LANES * (tile + 1)] += piece[row : row + wide]
 
 
-def own_kernel(wide, firsts, vel, tot, weight, edges, bands, inv4, fixed, rhs, values, side, started, share):
+def own_kernel(wide, firsts, vel, tot, weight, edges, inv4, fixed, rhs, values, side, started, share):
     lanes = rhs.shape[2]
     blocks = lanes // (2 * LANES)
     g = lax.axis_index("gz")
-    weights, across = [weight[i] for i in range(10)], across_weights(bands)
+    weights = [weight[i] for i in range(10)]
     for tile in range(lanes // LANES):
         at = pl.ds(pl.multiple_of(g * lanes + LANES * tile, LANES), LANES)
-        store_share(share, wide, tile, at, vel, tot, weights, edges, across)
-        row = (3 * wide + 6) * tile + 3 * wide
-        side[:, LANES * tile : LANES * (tile + 1)] = share[row : row + 6]
+        store_share(share, wide, tile, at, vel, tot, weights, edges)
+        row = (3 * wide + 12) * tile + 3 * wide
+        side[:, LANES * tile : LANES * (tile + 1)] = share[row : row + 12]
     rhs[...] = jnp.zeros_like(rhs)
     add_share(rhs, wide, firsts, g, share)
     for f in range(3):
@@ -218,8 +202,8 @@
     started[...] = jnp.zeros_like(started)
     for b in range(blocks):
         at = FIRST * b
-        started[at + STATE + 12 : at + FIRST] = fixed[(MAPS + 16) * b : (MAPS + 16) * (b + 1)]
-    started[FIRST * blocks : FIRST * blocks + 8] = fixed[(MAPS + 16) * blocks : (MAPS + 16) * blocks + 8]
+        started[at + STATE + 24 : at + FIRST] = fixed[(MAPS + 16) * b : (MAPS + 16) * (b + 1)]
+    started[FIRST * blocks : FIRST * blocks + 16] = fixed[(MAPS + 16) * blocks : (MAPS + 16) * blocks + 16]
 
 
 def store_planes(ref, at, planes):
@@ -256,7 +240,8 @@
             for kind in range(2):
                 at = weights + 4 * i + 2 * j + kind
                 low, high = lower[i][j][kind], upper[i][j][kind]
-                fixed[at : at + 1] = jnp.where(used, jnp.where(core == 0, low, high), 0.0)
+                fixed[at : at + 1] = jnp.where(core == 0, high, low)
+                fixed[at + 8 : at + 9] = jnp.where(used, jnp.where(core == 0, low, high), 0.0)
     for b in range(modes // LANES):
         at, lanes = (MAPS + 16) * b, pl.ds(LANES * b, LANES)
         for k in range(2):
@@ -282,8 +267,8 @@
         copy.wait()
 
 
-def weights_of(ref):
-    at = ref.shape[0] - 8
+def weights_of(ref, at):
+    at += ref.shape[0] - 16
     return [
         [[ref[at + 4 * i + 2 * j + kind : at + 4 * i + 2 * j + kind + 1] for kind in range(2)] for j in range(2)]
         for i in range(2)
@@ -308,7 +293,7 @@
                 for tile in range(tiles):
                     to = pl.ds(LANES * tile, LANES)
                     for f in range(3):
-                        row = (3 * wide + 6) * tile + wide * f
+                        row = (3 * wide + 12) * tile + wide * f
                         share = piece[row : row + wide]
                         for r in range(4):
                             row = (6 if r < 2 else 0) + 3 * (r % 2) + f
@@ -319,8 +304,8 @@
         @pl.when(source == jnp.where(core == 0, groups - 1, 0))
         def _(piece=piece):
             for tile in range(tiles):
-                row = (3 * wide + 6) * tile + 3 * wide
-                side[:, LANES * tile : LANES * (tile + 1)] = piece[row : row + 6]
+                row = (3 * wide + 12) * tile + 3 * wide
+                side[:, LANES * tile : LANES * (tile + 1)] = piece[row : row + 12]
 
     for b in range(tiles // 2):
         store_planes(message, FIRST * b, values[:, 2 * LANES * b : 2 * LANES * (b + 1)])
@@ -412,16 +397,16 @@
     core = lax.rem(lax.axis_index("gy"), 2)
     blocks = out.shape[0] // RUN
     for ref, across, end, target in ((mine, other, end_mine, fixed_mine), (other, mine, end_other, fixed_other)):
-        outer_weights = weights_of(ref)
+        inner_weights, outer_weights = weights_of(ref, 0), weights_of(ref, 8)
         for b in range(blocks):
             at, to = FIRST * b, RUN * b
-            inner = [across[at + STATE + 6 * i : at + STATE + 6 * i + 6] for i in range(2)]
+            inner = beside(inner_weights, planes_of(across, at + STATE))
             outer = beside(outer_weights, planes_of(end, 24 * b))
-            target[to + STATE : to + RUN] = ref[at + 36 : at + 36 + MAPS]
+            target[to + STATE : to + RUN] = ref[at + 48 : at + 48 + MAPS]
             for k in range(4):
                 value = ref[at + 6 * k : at + 6 * k + 6]
                 for i in range(2):
-                    row = at + 36 + MAPS + 2 * k + i
+                    row = at + 48 + MAPS + 2 * k + i
                     value = value + ref[row : row + 1] * inner[i] + ref[row + 8 : row + 9] * outer[i]
                 target[to + 6 * k : to + 6 * k + 6] = value
     low = jnp.where(core == 0, fixed_mine[...], fixed_other[...])
@@ -468,12 +453,12 @@
     for shift, piece in enumerate(pieces, 1):
         add_share(rhs, wide, firsts, lax.rem(g - shift + len(firsts), len(firsts)), piece)
     core = lax.rem(lax.axis_index("gy"), 2)
-    outer_weights = weights_of(mine)
+    inner_weights, outer_weights = weights_of(mine, 0), weights_of(mine, 8)
     flat = rhs[...].reshape(fields * rows, lanes)
     for b in range(lanes // (2 * LANES)):
         columns = pl.ds(2 * LANES * b, 2 * LANES)
         parts = apart(flat[:, 2 * LANES * b : 2 * LANES * (b + 1)])
-        inner = [other[FIRST * b + STATE + 6 * i : FIRST * b + STATE + 6 * i + 6] for i in range(2)]
+        inner = beside(inner_weights, planes_of(other, FIRST * b + STATE))
         outer = beside(outer_weights, planes_of(end, 24 * b))
         solved = []
         for p in range(2):
@@ -580,7 +565,6 @@
     blocks = modes // LANES
     taps = jnp.transpose(bands, (1, 0, 2))
     to_core = lambda x: lax.ppermute(x, "gy", [(i, i ^ 1) for i in range(gy)])
-    beside_taps = to_core(taps)
     padded = (3, rows + 16, columns)
     edges, coef, weight, vel, tot, inverse_ends, spike_ends = vmem_call(
         functools.partial(load_kernel, wide, firsts),
@@ -592,11 +576,11 @@
         far=5,
     )
     beside_edges = to_core(edges)
-    share = ((3 * wide + 6) * 2 * blocks, LANES)
+    share = ((3 * wide + 12) * 2 * blocks, LANES)
     shares = vmem_call(
         functools.partial(shares_kernel, wide),
         [share] * (gz - 1),
-        [vel, tot, weight, edges, beside_taps],
+        [vel, tot, weight, edges],
         flops=2 * 10**10,
         name="shares",
     )
@@ -609,16 +593,16 @@
     ends = [lax.ppermute(x, ("gy", "gz"), end_pairs(gy, gz, step)) for step, x in enumerate(relays)]
     inv4, fixed = vmem_call(
         prepare_kernel,
-        [(4, rows, lanes), ((MAPS + 16) * blocks + 8, LANES)],
+        [(4, rows, lanes), ((MAPS + 16) * blocks + 16, LANES)],
         [inverse_ends, spike_ends, coef],
         flops=2 * 10**10,
         name="prepare",
     )
-    first = (FIRST * blocks + 8, LANES)
+    first = (FIRST * blocks + 16, LANES)
     rhs, values, side, started = vmem_call(
         functools.partial(own_kernel, wide, firsts),
-        [(3, rows, lanes), (12, lanes), (6, lanes), first],
-        [vel, tot, weight, edges, beside_taps, inv4, fixed],
+        [(3, rows, lanes), (12, lanes), (12, lanes), first],
+        [vel, tot, weight, edges, inv4, fixed],
         scratch=[vmem(*share)],
         flops=2 * 10**8,
         name="own",
@@ -627,7 +611,7 @@
         functools.partial(interface_kernel, wide, firsts),
         [first],
         [inv4, started, values, side, *pieces],
-        scratch=[vmem(12, lanes), vmem(6, lanes)],
+        scratch=[vmem(12, lanes), vmem(12, lanes)],
         name="interface",
     )
     other = to_core(message)

time: 22 us -> 21.6 us (0.982)
  starting transfers between devices: 12 us -> 11.5 us
    ppermute x3, starting transfers between devices: 4.64 us -> 3.97 us  [per_device(): lax.ppermute(composed, 'gy', [(i, i ^ x * base ^ 1) for i in range(gy)])]
    ppermute x1, starting transfers between devices: 3.04 us -> 2.62 us  [per_device(): lax.ppermute(x, 'gz', [(i, (i + shift) % gz) for i in range(gz)])]
    ppermute x1, waiting for transfers between devices: 1.72 us -> 2.1 us  [per_device(): lax.ppermute(x, 'gz', [(i, (i + shift) % gz) for i in range(gz)])]
    ppermute x1, starting transfers between devices: 0.73 us -> 1.09 us  [per_device(): lax.ppermute(x, ('gy', 'gz'), end_pairs(gy, gz, step))]
    ppermute x1, starting transfers between devices: 2.42 us -> 2.76 us  [per_device(): lax.ppermute(message, 'gy', [(i, i ^ base ^ 1) for i in range(gy)])]
    ppermute x1, waiting for transfers between devices: 0.56 us -> 0.3 us  [per_device(): lax.ppermute(message, 'gy', [(i, i ^ base ^ 1) for i in range(gy)])]
    ppermute x4 -> x3, starting transfers between devices: 1.13 us -> 1.06 us  [per_device(): to_core = lambda x: lax.ppermute(x, 'gy', [(i, i ^ 1) for i in range(gy)])]
    ppermute x4 -> x3, waiting for transfers between devices: 0.86 us -> 0.85 us  [per_device(): to_core = lambda x: lax.ppermute(x, 'gy', [(i, i ^ 1) for i in range(gy)])]
  transfers between devices with their start and end apart: 10 -> 9, of which waited for: 5 -> 5; matrix products, arithmetic and copies ran while one was open for 0% -> 0% of each run, Pallas kernels for 20% -> 15%
where the time goes in v6:
time: 21.6 us; the launch traced here: 21.4 us
  starting transfers between devices  11.5 us (53%)
  Pallas kernels  5.29 us (24%)
  waiting for transfers between devices  4.48 us (21%)
    pallas_call x16, Pallas kernels, vmem_call(): pl.pallas_call(body, out_shape=[jax.ShapeDtypeStruct(s, F32) for s in out...  5.29 us
    ppermute x3, starting transfers between devices, per_device(): lax.ppermute(composed, 'gy', [(i, i ^ x * base ^ 1) for i in range(gy)])  3.97 us
    ppermute x1, starting transfers between devices, per_device(): lax.ppermute(message, 'gy', [(i, i ^ base ^ 1) for i in range(gy)])  2.76 us
    ppermute x1, starting transfers between devices, per_device(): lax.ppermute(x, 'gz', [(i, (i + shift) % gz) for i in range(gz)])  2.62 us
    ppermute x1, waiting for transfers between devices, per_device(): lax.ppermute(x, 'gz', [(i, (i + shift) % gz) for i in range(gz)])  2.1 us
    ppermute x3, waiting for transfers between devices, per_device(): lax.ppermute(composed, 'gy', [(i, i ^ x * base ^ 1) for i in range(gy)])  1.23 us
    ppermute x1, starting transfers between devices, per_device(): lax.ppermute(x, ('gy', 'gz'), end_pairs(gy, gz, step))  1.09 us
    ppermute x3, starting transfers between devices, per_device(): to_core = lambda x: lax.ppermute(x, 'gy', [(i, i ^ 1) for i in range(gy)])  1.06 us
  transfers between devices with their start and end apart: 9, of which 5 were waited for; matrix products, arithmetic and copies ran while one was open for 0% of the time, Pallas kernels for 15%

profile of v6, /device:TPU:0, one launch (start us, length us, event | category | flops | bytes accessed | tf_op | source)
XLA Modules:
  0.0 21.4 jit_solution(653107628841355536)
XLA Ops:
  0.0 1.2 %load.1 = (f32[12,1024]{1,0:T(8,128)S(1)}, f32[10,24,128]{2,1,0:T(8,128)S(1)}, f32[10,14,128]{2,1,0:T(8,128)S(1)}, f32[3,40,1024]{2,1,0:T(8,128)S(1)}, f32[3,40,...) custom-call(f32[3,12,1024]{2,1,0:T(8,128)} %velocity.1, f32[3,12,1024]{2,1,0:T(8,128)} %explicit.1, ...), custom_call_target="tpu_custom_call" | custom-call | flops 20000000000 | bytes 984000 | tf_op jit(solution)/shard_map/load/pallas_call | solution.py:19
  1.2 0.5 %collective-permute-start.2 = (f32[12,1024]{1,0:T(8,128)S(1)}, f32[12,1024]{1,0:T(8,128)S(1)}, u32[]{:S(2)}, u32[]{:S(2)}) collective-permute-start(f32[12,1024]{1,0:T(8,128)S(1)} %get-tuple-element.32.edges), channel_id=1, source_target_pairs={{0,2},{2,0},{4,6},{6,4},{8,10},{10,8},{12,14},{14,12},{16,18},{18,... | collective-permute-start | bytes 147464 | tf_op jit(solution)/shard_map/ppermute | solution.py:567
  1.7 0.1 shares.1
  1.8 2.6 %collective-permute-start = (f32[216,128]{1,0:T(8,128)S(1)}, f32[216,128]{1,0:T(8,128)S(1)}, u32[]{:S(2)}, u32[]{:S(2)}) collective-permute-start(f32[216,128]{1,0:T(8,128)S(1)} %shares.1), channel_id=1, source_target_pairs={{0,1},{1,0},{2,3},{3,2},{4,5},{5,4},{6,7},{7,6},{8,9},{9,8},{10,11... | collective-permute-start | bytes 331784 | tf_op jit(solution)/shard_map/ppermute | solution.py:588
  4.4 0.0 collective-permute-done.2.beside_edges
  4.4 0.1 relay.1
  4.5 1.1 %collective-permute-start.3 = (f32[48,128]{1,0:T(8,128)S(1)}, f32[48,128]{1,0:T(8,128)S(1)}, u32[]{:S(2)}, u32[]{:S(2)}) collective-permute-start(f32[48,128]{1,0:T(8,128)S(1)} %relay.1), channel_id=1, source_target_pairs={{1,5},{4,3},{3,4},{6,2},{5,9},{8,7},{7,8},{10,6},{9,13},{12,11},{1... | collective-permute-start | bytes 73736 | tf_op jit(solution)/shard_map/ppermute | solution.py:593
  5.6 0.2 prepare.1
  5.8 0.2 %own.1 = (f32[3,24,512]{2,1,0:T(8,128)S(1)}, f32[12,512]{1,0:T(8,128)S(1)}, f32[12,512]{1,0:T(8,128)S(1)}, f32[168,128]{1,0:T(8,128)S(1)}) custom-call(f32[3,40,1024]{2,1,0:T(8,128)S(1)} %get-tuple-element.29.vel, f32[3,40,1024]{2,1,0:T(8,128)S(1)} %get-tuple-element.30.tot, f32[10,14,128]{2,1,0:T(8,128)S(1)} %get-tuple-element.31.weight, ...), custom_call_target="tpu_custom_call" | custom-call | flops 200000000 | bytes 1337344 | tf_op jit(solution)/shard_map/own/pallas_call | solution.py:19
  6.0 2.1 %collective-permute-done.refs_0_ = f32[216,128]{1,0:T(8,128)S(1)} collective-permute-done((f32[216,128]{1,0:T(8,128)S(1)}, f32[216,128]{1,0:T(8,128)S(1)}, u32[]{:S(2)}, u32[]{:S(2)}) %collective-permute-start) | collective-permute-done | bytes 110624 | tf_op jit(solution)/shard_map/ppermute | solution.py:588
  8.1 0.2 %interface.1.mine = f32[168,128]{1,0:T(8,128)S(1)} custom-call(f32[4,24,512]{2,1,0:T(8,128)S(1)} %get-tuple-element.28.inv4, f32[168,128]{1,0:T(8,128)S(1)} %get-tuple-element.34.started, f32[12,512]{1,0:T(8,128)S(1)} %get-tuple-element.35.own_values, f32[12,512]{1,0:T(8,128)S(1)} %get-tuple-element.36.own_side, f32[216,128]{1,0:T(8,128)S(1)} %collective-permute-done.refs_0_), custom_call_target="tpu_custom_call" | custom-call | bytes 442368 | tf_op jit(solution)/shard_map/interface/pallas_call | solution.py:19
  8.4 0.1 collective-permute-start.1
  8.5 0.0 collective-permute-done.3.refs_0_
  8.5 0.5 %collective-permute-start.4 = (f32[48,128]{1,0:T(8,128)S(1)}, f32[48,128]{1,0:T(8,128)S(1)}, u32[]{:S(2)}, u32[]{:S(2)}) collective-permute-start(f32[48,128]{1,0:T(8,128)S(1)} %ends.1.end_mine.end), channel_id=1, source_target_pairs={{0,2},{2,0},{4,6},{6,4},{8,10},{10,8},{12,14},{14,12},{16,18},{18,... | collective-permute-start | bytes 73736 | tf_op jit(solution)/shard_map/ppermute | solution.py:567
  9.0 0.8 %collective-permute-done.4.end_other = f32[48,128]{1,0:T(8,128)S(1)} collective-permute-done((f32[48,128]{1,0:T(8,128)S(1)}, f32[48,128]{1,0:T(8,128)S(1)}, u32[]{:S(2)}, u32[]{:S(2)}) %collective-permute-start.4) | collective-permute-done | bytes 24608 | tf_op jit(solution)/shard_map/ppermute | solution.py:567
  9.8 0.0 collective-permute-done.1.other
  9.8 0.1 pair.1
  9.9 2.7 %collective-permute-start.5 = (f32[72,128]{1,0:T(8,128)S(1)}, f32[72,128]{1,0:T(8,128)S(1)}, u32[]{:S(2)}, u32[]{:S(2)}) collective-permute-start(f32[72,128]{1,0:T(8,128)S(1)} %get-tuple-element.37.after.refs_0_), channel_id=1, source_target_pairs={{0,14},{2,12},{4,10},{6,8},{8,6},{10,4},{12,2},{14,0},{16,30},{18,... | collective-permute-start | bytes 110600 | tf_op jit(solution)/shard_map/ppermute | solution.py:653
  12.6 0.3 %collective-permute-start.6 = (f32[72,128]{1,0:T(8,128)S(1)}, f32[72,128]{1,0:T(8,128)S(1)}, u32[]{:S(2)}, u32[]{:S(2)}) collective-permute-start(f32[72,128]{1,0:T(8,128)S(1)} %get-tuple-element.37.after.refs_0_), channel_id=1, source_target_pairs={{0,10},{2,8},{4,14},{6,12},{8,2},{10,0},{12,6},{14,4},{16,26},{18,... | collective-permute-start | bytes 110600 | tf_op jit(solution)/shard_map/ppermute | solution.py:653
  12.9 1.0 %collective-permute-start.7 = (f32[72,128]{1,0:T(8,128)S(1)}, f32[72,128]{1,0:T(8,128)S(1)}, u32[]{:S(2)}, u32[]{:S(2)}) collective-permute-start(f32[72,128]{1,0:T(8,128)S(1)} %get-tuple-element.37.after.refs_0_), channel_id=1, source_target_pairs={{0,6},{2,4},{4,2},{6,0},{8,14},{10,12},{12,10},{14,8},{16,22},{18,... | collective-permute-start | bytes 110600 | tf_op jit(solution)/shard_map/ppermute | solution.py:653
  13.9 1.1 %fetch.1 = (f32[24,24,256]{2,1,0:T(8,128)S(1)}, f32[2,2,24,256]{3,2,1,0:T(8,128)S(1)}) custom-call(f32[24,24,256]{2,1,0:T(8,128)} %inverse.3, f32[2,2,24,256]{3,2,1,0:T(8,128)} %spikes.3, f32[72,128]{1,0:T(8,128)S(1)} %get-tuple-element.37.after.refs_0_), custom_call_target="tpu_custom_call" | custom-call | flops 20000000000 | bytes 724992 | tf_op jit(solution)/shard_map/fetch/pallas_call | solution.py:19
  15.0 0.1 widen.2.refs_4_
  15.0 0.0 collective-permute-done.5.refs_1_
  15.0 1.1 %collective-permute-done.6.refs_2_ = f32[72,128]{1,0:T(8,128)S(1)} collective-permute-done((f32[72,128]{1,0:T(8,128)S(1)}, f32[72,128]{1,0:T(8,128)S(1)}, u32[]{:S(2)}, u32[]{:S(2)}) %collective-permute-start.6) | collective-permute-done | bytes 36896 | tf_op jit(solution)/shard_map/ppermute | solution.py:653
  16.1 0.1 collective-permute-done.7.refs_3_
  16.3 0.1 compose.1.composed
  16.4 2.8 %collective-permute-start.8 = (f32[32,128]{1,0:T(8,128)S(1)}, f32[32,128]{1,0:T(8,128)S(1)}, u32[]{:S(2)}, u32[]{:S(2)}) collective-permute-start(f32[32,128]{1,0:T(8,128)S(1)} %last_message.1), channel_id=1, source_target_pairs={{0,18},{2,16},{4,22},{6,20},{8,26},{10,24},{12,30},{14,28},{16,2},... | collective-permute-start | bytes 49160 | tf_op jit(solution)/shard_map/ppermute | solution.py:670
  19.1 0.7 %block.1.local = f32[3,24,512]{2,1,0:T(8,128)S(1)} custom-call(f32[24,24,256]{2,1,0:T(8,128)S(1)} %get-tuple-element.38.inverse, f32[3,24,512]{2,1,0:T(8,128)S(1)} %get-tuple-element.39.own_rhs, f32[168,128]{1,0:T(8,128)S(1)} %interface.1.mine, f32[168,128]{1,0:T(8,128)S(1)} %collective-permute-done.1.other, f32[48,128]{1,0:T(8,128)S(1)} %ends.1.end_mine.end, ...), custom_call_target="tpu_custom_call" | custom-call | flops 200000000 | bytes 1044480 | tf_op jit(solution)/shard_map/block/pallas_call | solution.py:19
  19.9 0.2 widen.3.known
  20.0 0.3 %ready.1 = (f32[3,24,512]{2,1,0:T(8,128)S(1)}, f32[2,24,512]{2,1,0:T(8,128)S(1)}) custom-call(f32[3,24,512]{2,1,0:T(8,128)S(1)} %block.1.local, f32[2,2,24,256]{3,2,1,0:T(8,128)S(1)} %get-tuple-element.40.spikes, f32[72,128]{1,0:T(8,128)S(1)} %widen.3.known), custom_call_target="tpu_custom_call" | custom-call | flops 10000000 | bytes 282624 | tf_op jit(solution)/shard_map/ready/pallas_call | solution.py:19
  20.3 0.3 %collective-permute-done.8.received = f32[32,128]{1,0:T(8,128)S(1)} collective-permute-done((f32[32,128]{1,0:T(8,128)S(1)}, f32[32,128]{1,0:T(8,128)S(1)}, u32[]{:S(2)}, u32[]{:S(2)}) %collective-permute-start.8) | collective-permute-done | bytes 16416 | tf_op jit(solution)/shard_map/ppermute | solution.py:670
  20.6 0.8 %final.1 = f32[3,24,512]{2,1,0:T(8,128)} custom-call(f32[3,24,512]{2,1,0:T(8,128)S(1)} %get-tuple-element.43.ready, f32[2,24,512]{2,1,0:T(8,128)S(1)} %get-tuple-element.44.lift, f32[72,128]{1,0:T(8,128)S(1)} %compose.1.composed, f32[32,128]{1,0:T(8,128)S(1)} %collective-permute-done.8.received), custom_call_target="tpu_custom_call" | custom-call | bytes 299008 | tf_op jit(solution)/shard_map/final/pallas_call | solution.py:19
  (2 shorter events, 0.0 us)
Async XLA Ops:
  1.2 3.3 %collective-permute-start.2 = (f32[12,1024]{1,0:T(8,128)S(1)}, f32[12,1024]{1,0:T(8,128)S(1)}, u32[]{:S(2)}, u32[]{:S(2)}) collective-permute-start(f32[12,1024]{1,0:T(8,128)S(1)} %get-tuple-element.32.edges), channel_id=1, source_target_pairs={{0,2},{2,0},{4,6},{6,4},{8,10},{10,8},{12,14},{14,12},{16,18},{18,... | collective-permute-start | bytes 147464 | tf_op jit(solution)/shard_map/ppermute | solution.py:567
  1.8 6.3 %collective-permute-start = (f32[216,128]{1,0:T(8,128)S(1)}, f32[216,128]{1,0:T(8,128)S(1)}, u32[]{:S(2)}, u32[]{:S(2)}) collective-permute-start(f32[216,128]{1,0:T(8,128)S(1)} %shares.1), channel_id=1, source_target_pairs={{0,1},{1,0},{2,3},{3,2},{4,5},{5,4},{6,7},{7,6},{8,9},{9,8},{10,11... | collective-permute-start | bytes 331784 | tf_op jit(solution)/shard_map/ppermute | solution.py:588
  4.5 3.9 %collective-permute-start.3 = (f32[48,128]{1,0:T(8,128)S(1)}, f32[48,128]{1,0:T(8,128)S(1)}, u32[]{:S(2)}, u32[]{:S(2)}) collective-permute-start(f32[48,128]{1,0:T(8,128)S(1)} %relay.1), channel_id=1, source_target_pairs={{1,5},{4,3},{3,4},{6,2},{5,9},{8,7},{7,8},{10,6},{9,13},{12,11},{1... | collective-permute-start | bytes 73736 | tf_op jit(solution)/shard_map/ppermute | solution.py:593
  8.4 1.4 %collective-permute-start.1 = (f32[168,128]{1,0:T(8,128)S(1)}, f32[168,128]{1,0:T(8,128)S(1)}, u32[]{:S(2)}, u32[]{:S(2)}) collective-permute-start(f32[168,128]{1,0:T(8,128)S(1)} %interface.1.mine), channel_id=1, source_target_pairs={{0,2},{2,0},{4,6},{6,4},{8,10},{10,8},{12,14},{14,12},{16,18},{18,... | collective-permute-start | bytes 258056 | tf_op jit(solution)/shard_map/ppermute | solution.py:567
  8.5 1.3 %collective-permute-start.4 = (f32[48,128]{1,0:T(8,128)S(1)}, f32[48,128]{1,0:T(8,128)S(1)}, u32[]{:S(2)}, u32[]{:S(2)}) collective-permute-start(f32[48,128]{1,0:T(8,128)S(1)} %ends.1.end_mine.end), channel_id=1, source_target_pairs={{0,2},{2,0},{4,6},{6,4},{8,10},{10,8},{12,14},{14,12},{16,18},{18,... | collective-permute-start | bytes 73736 | tf_op jit(solution)/shard_map/ppermute | solution.py:567
  9.9 5.1 %collective-permute-start.5 = (f32[72,128]{1,0:T(8,128)S(1)}, f32[72,128]{1,0:T(8,128)S(1)}, u32[]{:S(2)}, u32[]{:S(2)}) collective-permute-start(f32[72,128]{1,0:T(8,128)S(1)} %get-tuple-element.37.after.refs_0_), channel_id=1, source_target_pairs={{0,14},{2,12},{4,10},{6,8},{8,6},{10,4},{12,2},{14,0},{16,30},{18,... | collective-permute-start | bytes 110600 | tf_op jit(solution)/shard_map/ppermute | solution.py:653
  12.6 3.5 %collective-permute-start.6 = (f32[72,128]{1,0:T(8,128)S(1)}, f32[72,128]{1,0:T(8,128)S(1)}, u32[]{:S(2)}, u32[]{:S(2)}) collective-permute-start(f32[72,128]{1,0:T(8,128)S(1)} %get-tuple-element.37.after.refs_0_), channel_id=1, source_target_pairs={{0,10},{2,8},{4,14},{6,12},{8,2},{10,0},{12,6},{14,4},{16,26},{18,... | collective-permute-start | bytes 110600 | tf_op jit(solution)/shard_map/ppermute | solution.py:653
  12.9 3.4 %collective-permute-start.7 = (f32[72,128]{1,0:T(8,128)S(1)}, f32[72,128]{1,0:T(8,128)S(1)}, u32[]{:S(2)}, u32[]{:S(2)}) collective-permute-start(f32[72,128]{1,0:T(8,128)S(1)} %get-tuple-element.37.after.refs_0_), channel_id=1, source_target_pairs={{0,6},{2,4},{4,2},{6,0},{8,14},{10,12},{12,10},{14,8},{16,22},{18,... | collective-permute-start | bytes 110600 | tf_op jit(solution)/shard_map/ppermute | solution.py:653
  16.4 4.2 %collective-permute-start.8 = (f32[32,128]{1,0:T(8,128)S(1)}, f32[32,128]{1,0:T(8,128)S(1)}, u32[]{:S(2)}, u32[]{:S(2)}) collective-permute-start(f32[32,128]{1,0:T(8,128)S(1)} %last_message.1), channel_id=1, source_target_pairs={{0,18},{2,16},{4,22},{6,20},{8,26},{10,24},{12,30},{14,28},{16,2},... | collective-permute-start | bytes 49160 | tf_op jit(solution)/shard_map/ppermute | solution.py:670

commit v7 on v6

--- a/solution.py
+++ b/solution.py
@@ -89,16 +89,13 @@
     ]
 
 
-def load_kernel(wide, firsts, velocity, explicit, bands, inverse, spikes, *refs):
-    edges, coef, weight, vel, tot, inverse_ends, spike_ends, here, there, taps, square, sems = refs
+def load_kernel(wide, firsts, velocity, explicit, bands, *refs):
+    edges, coef, weight, vel, tot, here, there, taps, square, sems = refs
     groups = len(firsts)
     own = velocity.shape[1]
     rows = coef.shape[1]
     g = lax.axis_index("gz")
     moves = [(bands, taps), (velocity, here), (explicit, there)]
-    for i, (low, tiles) in enumerate(((0, 0), (rows - 2, rows - 8))):
-        moves.append((inverse.at[pl.ds(low, 2)], inverse_ends.at[pl.ds(2 * i, 2)]))
-        moves.append((spikes.at[:, :, pl.ds(tiles, 8)], spike_ends.at[:, :, pl.ds(8 * i, 8)]))
     copies = [pltpu.make_async_copy(source, target, sems.at[i]) for i, (source, target) in enumerate(moves)]
     for copy in copies:
         copy.start()
@@ -135,8 +132,6 @@
             top += there[f, j : j + 1]
             bottom += there[f, own - HALO + j : own - HALO + j + 1]
             edges[3 * j + f : 3 * j + f + 1] = jnp.where(g == 0, top, bottom)
-    for copy in copies[3:]:
-        copy.wait()
 
 
 def stencil(vel, tot, weights, f, wide, at):
@@ -228,8 +223,16 @@
             store_planes(out, 24 * b, jnp.where(mine, edges[:, at], beside_edges[:, at]))
 
 
-def prepare_kernel(inverse_ends, spike_ends, coef, inv4, fixed):
+def prepare_kernel(inverse, spikes, coef, inv4, fixed, inverse_ends, spike_ends, sems):
     rows, modes = inverse_ends.shape[1:]
+    copies = []
+    for i, (low, tiles) in enumerate(((0, 0), (rows - 2, rows - 8))):
+        source, target = inverse.at[pl.ds(low, 2)], inverse_ends.at[pl.ds(2 * i, 2)]
+        copies.append(pltpu.make_async_copy(source, target, sems.at[2 * i]))
+        source, target = spikes.at[:, :, pl.ds(tiles, 8)], spike_ends.at[:, :, pl.ds(8 * i, 8)]
+        copies.append(pltpu.make_async_copy(source, target, sems.at[2 * i + 1]))
+    for copy in copies:
+        copy.start()
     core = lax.rem(lax.axis_index("gy"), 2)
     gy, count = lax.axis_index("gy"), lax.axis_size("gy")
     lower, upper = side_weights(coef, False), side_weights(coef, True)
@@ -242,6 +245,8 @@
                 low, high = lower[i][j][kind], upper[i][j][kind]
                 fixed[at : at + 1] = jnp.where(core == 0, high, low)
                 fixed[at + 8 : at + 9] = jnp.where(used, jnp.where(core == 0, low, high), 0.0)
+    for copy in copies:
+        copy.wait()
     for b in range(modes // LANES):
         at, lanes = (MAPS + 16) * b, pl.ds(LANES * b, LANES)
         for k in range(2):
@@ -372,15 +377,21 @@
 
 
 def compose_kernel(base, *refs):
-    *pieces, out, board = refs
+    *pieces, out, last, board = refs
     sort_pieces(base, pieces, board)
-    for at in range(0, out.shape[0], RUN):
+    upper = lax.rem(lax.div(lax.axis_index("gy"), base * len(pieces)), 2) == 1
+    for b in range(out.shape[0] // RUN):
+        at, to = RUN * b, LAST * b
         run = [Piece(board.at[i], at) for i in range(len(pieces))]
         up = down = None
         for piece in run:
             up = after(up, piece)
         for piece in run[::-1]:
             down = before(piece, down)
+        for k in range(2):
+            last[to + 6 * k : to + 6 * k + 6] = jnp.where(upper, down[0][k], up[0][k])
+            for j in range(2):
+                last[to + 12 + 2 * k + j : to + 13 + 2 * k + j] = down[1][k][j]
         store_run(out, at, up[0], down[0], up[1], down[1], down[2])
 
 
@@ -474,14 +485,6 @@
             local[f, :, columns] = together(solved[0][f], solved[1][f])
 
 
-def last_message_kernel(base, composed, out):
-    upper = lax.rem(lax.div(lax.axis_index("gy"), base), 2) == 1
-    for b in range(out.shape[0] // LAST):
-        at, to = RUN * b, LAST * b
-        out[to : to + 12] = jnp.where(upper, composed[at + 12 : at + 24], composed[at : at + 12])
-        out[to + 12 : to + 16] = composed[at + STATE + 4 : at + STATE + 8]
-
-
 def ready_kernel(base, local, spikes, known, ready, lift):
     upper = lax.rem(lax.div(lax.axis_index("gy"), base), 2) == 1
     for b in range(known.shape[0] // RUN):
@@ -563,17 +566,16 @@
     dma = lambda n: pltpu.SemaphoreType.DMA((n,))
 
     blocks = modes // LANES
-    taps = jnp.transpose(bands, (1, 0, 2))
     to_core = lambda x: lax.ppermute(x, "gy", [(i, i ^ 1) for i in range(gy)])
     padded = (3, rows + 16, columns)
-    edges, coef, weight, vel, tot, inverse_ends, spike_ends = vmem_call(
+    edges, coef, weight, vel, tot = vmem_call(
         functools.partial(load_kernel, wide, firsts),
-        [(12, columns), (10, rows, LANES), (10, wide, LANES), padded, padded, (4, rows, modes), (2, 2, 16, modes)],
-        [velocity, explicit, taps, inverse, spikes],
-        scratch=[vmem(3, own, columns)] * 2 + [vmem(5, 2, rows), vmem(LANES, LANES), dma(7)],
+        [(12, columns), (10, rows, LANES), (10, wide, LANES), padded, padded],
+        [velocity, explicit, jnp.transpose(bands, (1, 0, 2))],
+        scratch=[vmem(3, own, columns)] * 2 + [vmem(5, 2, rows), vmem(LANES, LANES), dma(3)],
         flops=2 * 10**10,
         name="load",
-        far=5,
+        far=3,
     )
     beside_edges = to_core(edges)
     share = ((3 * wide + 12) * 2 * blocks, LANES)
@@ -594,9 +596,11 @@
     inv4, fixed = vmem_call(
         prepare_kernel,
         [(4, rows, lanes), ((MAPS + 16) * blocks + 16, LANES)],
-        [inverse_ends, spike_ends, coef],
+        [inverse, spikes, coef],
+        scratch=[vmem(4, rows, modes), vmem(2, 2, 16, modes), dma(4)],
         flops=2 * 10**10,
         name="prepare",
+        far=2,
     )
     first = (FIRST * blocks + 16, LANES)
     rhs, values, side, started = vmem_call(
@@ -652,8 +656,12 @@
         for x in range(size - 1, 0, -1):
             gathered.append(lax.ppermute(composed, "gy", [(i, i ^ (x * base) ^ 1) for i in range(gy)]))
         board = [vmem(size, *run)]
-        (composed,) = vmem_call(
-            functools.partial(compose_kernel, base), [run], gathered, scratch=board, name="compose"
+        composed, last = vmem_call(
+            functools.partial(compose_kernel, base),
+            [run, (LAST * blocks, LANES)],
+            gathered,
+            scratch=board,
+            name="compose",
         )
         (known,) = vmem_call(
             functools.partial(widen_kernel, base, False),
@@ -664,10 +672,7 @@
             name="widen",
         )
     base, _ = steps[-1]
-    (message,) = vmem_call(
-        functools.partial(last_message_kernel, base), [(LAST * blocks, LANES)], [composed], name="last_message"
-    )
-    received = lax.ppermute(message, "gy", [(i, i ^ base ^ 1) for i in range(gy)])
+    received = lax.ppermute(last, "gy", [(i, i ^ base ^ 1) for i in range(gy)])
     ready, lift = vmem_call(
         functools.partial(ready_kernel, base),
         [(3, rows, lanes), (2, rows, lanes)],

time: 21.6 us -> 21.5 us (level)
  waiting for transfers between devices: 4.48 us -> 3.59 us
  Pallas kernels: 5.29 us -> 6.12 us
    ppermute x1, waiting for transfers between devices: 2.1 us -> 1.21 us  [per_device(): lax.ppermute(x, 'gz', [(i, (i + shift) % gz) for i in range(gz)])]
    pallas_call x16 -> x15, Pallas kernels: 5.29 us -> 6.12 us  [vmem_call(): pl.pallas_call(body, out_shape=[jax.ShapeDtypeStruct(s, F32) for s in out...]
  transfers between devices with their start and end apart: 9 -> 9, of which waited for: 5 -> 5; matrix products, arithmetic and copies ran while one was open for 0% -> 0% of each run, Pallas kernels for 15% -> 19%
where the time goes in v7:
time: 21.5 us; the launch traced here: 21.3 us
  starting transfers between devices  11.5 us (53%)
  Pallas kernels  6.12 us (28%)
  waiting for transfers between devices  3.59 us (17%)
    pallas_call x15, Pallas kernels, vmem_call(): pl.pallas_call(body, out_shape=[jax.ShapeDtypeStruct(s, F32) for s in out...  6.12 us
    ppermute x3, starting transfers between devices, per_device(): lax.ppermute(composed, 'gy', [(i, i ^ x * base ^ 1) for i in range(gy)])  3.97 us
    ppermute x1, starting transfers between devices, per_device(): received = lax.ppermute(last, 'gy', [(i, i ^ base ^ 1) for i in range(gy)])  2.76 us
    ppermute x1, starting transfers between devices, per_device(): lax.ppermute(x, 'gz', [(i, (i + shift) % gz) for i in range(gz)])  2.62 us
    ppermute x3, waiting for transfers between devices, per_device(): lax.ppermute(composed, 'gy', [(i, i ^ x * base ^ 1) for i in range(gy)])  1.23 us
    ppermute x1, waiting for transfers between devices, per_device(): lax.ppermute(x, 'gz', [(i, (i + shift) % gz) for i in range(gz)])  1.21 us
    ppermute x1, starting transfers between devices, per_device(): lax.ppermute(x, ('gy', 'gz'), end_pairs(gy, gz, step))  1.09 us
    ppermute x3, starting transfers between devices, per_device(): to_core = lambda x: lax.ppermute(x, 'gy', [(i, i ^ 1) for i in range(gy)])  1.06 us
  transfers between devices with their start and end apart: 9, of which 5 were waited for; matrix products, arithmetic and copies ran while one was open for 0% of the time, Pallas kernels for 19%

profile of v7, /device:TPU:0, one launch (start us, length us, event | category | flops | bytes accessed | tf_op | source)
XLA Modules:
  0.0 21.3 jit_solution(16674378094242918395)
XLA Ops:
  0.0 1.1 %load.1 = (f32[12,1024]{1,0:T(8,128)S(1)}, f32[10,24,128]{2,1,0:T(8,128)S(1)}, f32[10,14,128]{2,1,0:T(8,128)S(1)}, f32[3,40,1024]{2,1,0:T(8,128)S(1)}, f32[3,40,1024]{2,1,0:T(8,128)S(1)}) custom-call(f32[3,12,1024]{2,1,0:T(8,128)} %velocity.1, f32[3,12,1024]{2,1,0:T(8,128)} %explicit.1, f32[5,2,24]{2,1,0:T(2,128)} %bitcast.1), custom_call_target="tpu_custom_call" | custom-call | flops 20000000000 | bytes 295872 | tf_op jit(solution)/shard_map/load/pallas_call | solution.py:19
  1.1 0.5 %collective-permute-start.2 = (f32[12,1024]{1,0:T(8,128)S(1)}, f32[12,1024]{1,0:T(8,128)S(1)}, u32[]{:S(2)}, u32[]{:S(2)}) collective-permute-start(f32[12,1024]{1,0:T(8,128)S(1)} %get-tuple-element.30.edges), channel_id=1, source_target_pairs={{0,2},{2,0},{4,6},{6,4},{8,10},{10,8},{12,14},{14,12},{16,18},{18,... | collective-permute-start | bytes 147464 | tf_op jit(solution)/shard_map/ppermute | solution.py:569
  1.6 0.1 shares.1
  1.8 2.6 %collective-permute-start = (f32[216,128]{1,0:T(8,128)S(1)}, f32[216,128]{1,0:T(8,128)S(1)}, u32[]{:S(2)}, u32[]{:S(2)}) collective-permute-start(f32[216,128]{1,0:T(8,128)S(1)} %shares.1), channel_id=1, source_target_pairs={{0,1},{1,0},{2,3},{3,2},{4,5},{5,4},{6,7},{7,6},{8,9},{9,8},{10,11... | collective-permute-start | bytes 331784 | tf_op jit(solution)/shard_map/ppermute | solution.py:590
  4.4 0.0 collective-permute-done.2.beside_edges
  4.4 0.1 relay.1
  4.5 1.1 %collective-permute-start.3 = (f32[48,128]{1,0:T(8,128)S(1)}, f32[48,128]{1,0:T(8,128)S(1)}, u32[]{:S(2)}, u32[]{:S(2)}) collective-permute-start(f32[48,128]{1,0:T(8,128)S(1)} %relay.1), channel_id=1, source_target_pairs={{1,5},{4,3},{3,4},{6,2},{5,9},{8,7},{7,8},{10,6},{9,13},{12,11},{1... | collective-permute-start | bytes 73736 | tf_op jit(solution)/shard_map/ppermute | solution.py:595
  5.6 1.0 %prepare.1 = (f32[4,24,512]{2,1,0:T(8,128)S(1)}, f32[72,128]{1,0:T(8,128)S(1)}) custom-call(f32[24,24,256]{2,1,0:T(8,128)} %inverse.3, f32[2,2,24,256]{3,2,1,0:T(8,128)} %spikes.3, f32[10,24,128]{2,1,0:T(8,128)S(1)} %get-tuple-element.25.coef), custom_call_target="tpu_custom_call" | custom-call | flops 20000000000 | bytes 811008 | tf_op jit(solution)/shard_map/prepare/pallas_call | solution.py:19
  6.6 0.3 %own.1 = (f32[3,24,512]{2,1,0:T(8,128)S(1)}, f32[12,512]{1,0:T(8,128)S(1)}, f32[12,512]{1,0:T(8,128)S(1)}, f32[168,128]{1,0:T(8,128)S(1)}) custom-call(f32[3,40,1024]{2,1,0:T(8,128)S(1)} %get-tuple-element.27.vel, f32[3,40,1024]{2,1,0:T(8,128)S(1)} %get-tuple-element.28.tot, f32[10,14,128]{2,1,0:T(8,128)S(1)} %get-tuple-element.29.weight, ...), custom_call_target="tpu_custom_call" | custom-call | flops 200000000 | bytes 1337344 | tf_op jit(solution)/shard_map/own/pallas_call | solution.py:19
  6.9 1.2 %collective-permute-done.refs_0_ = f32[216,128]{1,0:T(8,128)S(1)} collective-permute-done((f32[216,128]{1,0:T(8,128)S(1)}, f32[216,128]{1,0:T(8,128)S(1)}, u32[]{:S(2)}, u32[]{:S(2)}) %collective-permute-start) | collective-permute-done | bytes 110624 | tf_op jit(solution)/shard_map/ppermute | solution.py:590
  8.1 0.2 %interface.1.mine = f32[168,128]{1,0:T(8,128)S(1)} custom-call(f32[4,24,512]{2,1,0:T(8,128)S(1)} %get-tuple-element.26.inv4, f32[168,128]{1,0:T(8,128)S(1)} %get-tuple-element.32.started, f32[12,512]{1,0:T(8,128)S(1)} %get-tuple-element.33.own_values, f32[12,512]{1,0:T(8,128)S(1)} %get-tuple-element.34.own_side, f32[216,128]{1,0:T(8,128)S(1)} %collective-permute-done.refs_0_), custom_call_target="tpu_custom_call" | custom-call | bytes 442368 | tf_op jit(solution)/shard_map/interface/pallas_call | solution.py:19
  8.3 0.1 collective-permute-start.1
  8.4 0.0 collective-permute-done.3.refs_0_
  8.4 0.5 %collective-permute-start.4 = (f32[48,128]{1,0:T(8,128)S(1)}, f32[48,128]{1,0:T(8,128)S(1)}, u32[]{:S(2)}, u32[]{:S(2)}) collective-permute-start(f32[48,128]{1,0:T(8,128)S(1)} %ends.1.end_mine.end), channel_id=1, source_target_pairs={{0,2},{2,0},{4,6},{6,4},{8,10},{10,8},{12,14},{14,12},{16,18},{18,... | collective-permute-start | bytes 73736 | tf_op jit(solution)/shard_map/ppermute | solution.py:569
  8.9 0.8 %collective-permute-done.4.end_other = f32[48,128]{1,0:T(8,128)S(1)} collective-permute-done((f32[48,128]{1,0:T(8,128)S(1)}, f32[48,128]{1,0:T(8,128)S(1)}, u32[]{:S(2)}, u32[]{:S(2)}) %collective-permute-start.4) | collective-permute-done | bytes 24608 | tf_op jit(solution)/shard_map/ppermute | solution.py:569
  9.8 0.0 collective-permute-done.1.other
  9.8 0.1 pair.1
  9.9 2.7 %collective-permute-start.5 = (f32[72,128]{1,0:T(8,128)S(1)}, f32[72,128]{1,0:T(8,128)S(1)}, u32[]{:S(2)}, u32[]{:S(2)}) collective-permute-start(f32[72,128]{1,0:T(8,128)S(1)} %get-tuple-element.35.after.refs_0_), channel_id=1, source_target_pairs={{0,14},{2,12},{4,10},{6,8},{8,6},{10,4},{12,2},{14,0},{16,30},{18,... | collective-permute-start | bytes 110600 | tf_op jit(solution)/shard_map/ppermute | solution.py:657
  12.6 0.3 %collective-permute-start.6 = (f32[72,128]{1,0:T(8,128)S(1)}, f32[72,128]{1,0:T(8,128)S(1)}, u32[]{:S(2)}, u32[]{:S(2)}) collective-permute-start(f32[72,128]{1,0:T(8,128)S(1)} %get-tuple-element.35.after.refs_0_), channel_id=1, source_target_pairs={{0,10},{2,8},{4,14},{6,12},{8,2},{10,0},{12,6},{14,4},{16,26},{18,... | collective-permute-start | bytes 110600 | tf_op jit(solution)/shard_map/ppermute | solution.py:657
  12.8 1.0 %collective-permute-start.7 = (f32[72,128]{1,0:T(8,128)S(1)}, f32[72,128]{1,0:T(8,128)S(1)}, u32[]{:S(2)}, u32[]{:S(2)}) collective-permute-start(f32[72,128]{1,0:T(8,128)S(1)} %get-tuple-element.35.after.refs_0_), channel_id=1, source_target_pairs={{0,6},{2,4},{4,2},{6,0},{8,14},{10,12},{12,10},{14,8},{16,22},{18,... | collective-permute-start | bytes 110600 | tf_op jit(solution)/shard_map/ppermute | solution.py:657
  13.8 1.1 %fetch.1 = (f32[24,24,256]{2,1,0:T(8,128)S(1)}, f32[2,2,24,256]{3,2,1,0:T(8,128)S(1)}) custom-call(f32[24,24,256]{2,1,0:T(8,128)} %inverse.3, f32[2,2,24,256]{3,2,1,0:T(8,128)} %spikes.3, f32[72,128]{1,0:T(8,128)S(1)} %get-tuple-element.35.after.refs_0_), custom_call_target="tpu_custom_call" | custom-call | flops 20000000000 | bytes 724992 | tf_op jit(solution)/shard_map/fetch/pallas_call | solution.py:19
  14.9 0.1 widen.2.refs_4_
  15.0 0.0 collective-permute-done.5.refs_1_
  15.0 1.1 %collective-permute-done.6.refs_2_ = f32[72,128]{1,0:T(8,128)S(1)} collective-permute-done((f32[72,128]{1,0:T(8,128)S(1)}, f32[72,128]{1,0:T(8,128)S(1)}, u32[]{:S(2)}, u32[]{:S(2)}) %collective-permute-start.6) | collective-permute-done | bytes 36896 | tf_op jit(solution)/shard_map/ppermute | solution.py:657
  16.1 0.2 collective-permute-done.7.refs_3_
  16.2 0.1 compose.1
  16.3 2.8 %collective-permute-start.8 = (f32[32,128]{1,0:T(8,128)S(1)}, f32[32,128]{1,0:T(8,128)S(1)}, u32[]{:S(2)}, u32[]{:S(2)}) collective-permute-start(f32[32,128]{1,0:T(8,128)S(1)} %get-tuple-element.44), channel_id=1, source_target_pairs={{0,18},{2,16},{4,22},{6,20},{8,26},{10,24},{12,30},{14,28},{16,2},... | collective-permute-start | bytes 49160 | tf_op jit(solution)/shard_map/ppermute | solution.py:675
  19.1 0.7 %block.1.local = f32[3,24,512]{2,1,0:T(8,128)S(1)} custom-call(f32[24,24,256]{2,1,0:T(8,128)S(1)} %get-tuple-element.36.inverse, f32[3,24,512]{2,1,0:T(8,128)S(1)} %get-tuple-element.37.own_rhs, f32[168,128]{1,0:T(8,128)S(1)} %interface.1.mine, f32[168,128]{1,0:T(8,128)S(1)} %collective-permute-done.1.other, f32[48,128]{1,0:T(8,128)S(1)} %ends.1.end_mine.end, ...), custom_call_target="tpu_custom_call" | custom-call | flops 200000000 | bytes 1044480 | tf_op jit(solution)/shard_map/block/pallas_call | solution.py:19
  19.8 0.2 widen.3.known
  19.9 0.3 %ready.1 = (f32[3,24,512]{2,1,0:T(8,128)S(1)}, f32[2,24,512]{2,1,0:T(8,128)S(1)}) custom-call(f32[3,24,512]{2,1,0:T(8,128)S(1)} %block.1.local, f32[2,2,24,256]{3,2,1,0:T(8,128)S(1)} %get-tuple-element.38.spikes, f32[72,128]{1,0:T(8,128)S(1)} %widen.3.known), custom_call_target="tpu_custom_call" | custom-call | flops 10000000 | bytes 282624 | tf_op jit(solution)/shard_map/ready/pallas_call | solution.py:19
  20.2 0.3 %collective-permute-done.8.received = f32[32,128]{1,0:T(8,128)S(1)} collective-permute-done((f32[32,128]{1,0:T(8,128)S(1)}, f32[32,128]{1,0:T(8,128)S(1)}, u32[]{:S(2)}, u32[]{:S(2)}) %collective-permute-start.8) | collective-permute-done | bytes 16416 | tf_op jit(solution)/shard_map/ppermute | solution.py:675
  20.5 0.8 %final.1 = f32[3,24,512]{2,1,0:T(8,128)} custom-call(f32[3,24,512]{2,1,0:T(8,128)S(1)} %get-tuple-element.41.ready, f32[2,24,512]{2,1,0:T(8,128)S(1)} %get-tuple-element.42.lift, f32[72,128]{1,0:T(8,128)S(1)} %get-tuple-element.43.composed, f32[32,128]{1,0:T(8,128)S(1)} %collective-permute-done.8.received), custom_call_target="tpu_custom_call" | custom-call | bytes 299008 | tf_op jit(solution)/shard_map/final/pallas_call | solution.py:19
  (1 shorter events, 0.0 us)
Async XLA Ops:
  1.1 3.3 %collective-permute-start.2 = (f32[12,1024]{1,0:T(8,128)S(1)}, f32[12,1024]{1,0:T(8,128)S(1)}, u32[]{:S(2)}, u32[]{:S(2)}) collective-permute-start(f32[12,1024]{1,0:T(8,128)S(1)} %get-tuple-element.30.edges), channel_id=1, source_target_pairs={{0,2},{2,0},{4,6},{6,4},{8,10},{10,8},{12,14},{14,12},{16,18},{18,... | collective-permute-start | bytes 147464 | tf_op jit(solution)/shard_map/ppermute | solution.py:569
  1.8 6.3 %collective-permute-start = (f32[216,128]{1,0:T(8,128)S(1)}, f32[216,128]{1,0:T(8,128)S(1)}, u32[]{:S(2)}, u32[]{:S(2)}) collective-permute-start(f32[216,128]{1,0:T(8,128)S(1)} %shares.1), channel_id=1, source_target_pairs={{0,1},{1,0},{2,3},{3,2},{4,5},{5,4},{6,7},{7,6},{8,9},{9,8},{10,11... | collective-permute-start | bytes 331784 | tf_op jit(solution)/shard_map/ppermute | solution.py:590
  4.5 3.9 %collective-permute-start.3 = (f32[48,128]{1,0:T(8,128)S(1)}, f32[48,128]{1,0:T(8,128)S(1)}, u32[]{:S(2)}, u32[]{:S(2)}) collective-permute-start(f32[48,128]{1,0:T(8,128)S(1)} %relay.1), channel_id=1, source_target_pairs={{1,5},{4,3},{3,4},{6,2},{5,9},{8,7},{7,8},{10,6},{9,13},{12,11},{1... | collective-permute-start | bytes 73736 | tf_op jit(solution)/shard_map/ppermute | solution.py:595
  8.3 1.4 %collective-permute-start.1 = (f32[168,128]{1,0:T(8,128)S(1)}, f32[168,128]{1,0:T(8,128)S(1)}, u32[]{:S(2)}, u32[]{:S(2)}) collective-permute-start(f32[168,128]{1,0:T(8,128)S(1)} %interface.1.mine), channel_id=1, source_target_pairs={{0,2},{2,0},{4,6},{6,4},{8,10},{10,8},{12,14},{14,12},{16,18},{18,... | collective-permute-start | bytes 258056 | tf_op jit(solution)/shard_map/ppermute | solution.py:569
  8.4 1.3 %collective-permute-start.4 = (f32[48,128]{1,0:T(8,128)S(1)}, f32[48,128]{1,0:T(8,128)S(1)}, u32[]{:S(2)}, u32[]{:S(2)}) collective-permute-start(f32[48,128]{1,0:T(8,128)S(1)} %ends.1.end_mine.end), channel_id=1, source_target_pairs={{0,2},{2,0},{4,6},{6,4},{8,10},{10,8},{12,14},{14,12},{16,18},{18,... | collective-permute-start | bytes 73736 | tf_op jit(solution)/shard_map/ppermute | solution.py:569
  9.9 5.1 %collective-permute-start.5 = (f32[72,128]{1,0:T(8,128)S(1)}, f32[72,128]{1,0:T(8,128)S(1)}, u32[]{:S(2)}, u32[]{:S(2)}) collective-permute-start(f32[72,128]{1,0:T(8,128)S(1)} %get-tuple-element.35.after.refs_0_), channel_id=1, source_target_pairs={{0,14},{2,12},{4,10},{6,8},{8,6},{10,4},{12,2},{14,0},{16,30},{18,... | collective-permute-start | bytes 110600 | tf_op jit(solution)/shard_map/ppermute | solution.py:657
  12.6 3.5 %collective-permute-start.6 = (f32[72,128]{1,0:T(8,128)S(1)}, f32[72,128]{1,0:T(8,128)S(1)}, u32[]{:S(2)}, u32[]{:S(2)}) collective-permute-start(f32[72,128]{1,0:T(8,128)S(1)} %get-tuple-element.35.after.refs_0_), channel_id=1, source_target_pairs={{0,10},{2,8},{4,14},{6,12},{8,2},{10,0},{12,6},{14,4},{16,26},{18,... | collective-permute-start | bytes 110600 | tf_op jit(solution)/shard_map/ppermute | solution.py:657
  12.8 3.4 %collective-permute-start.7 = (f32[72,128]{1,0:T(8,128)S(1)}, f32[72,128]{1,0:T(8,128)S(1)}, u32[]{:S(2)}, u32[]{:S(2)}) collective-permute-start(f32[72,128]{1,0:T(8,128)S(1)} %get-tuple-element.35.after.refs_0_), channel_id=1, source_target_pairs={{0,6},{2,4},{4,2},{6,0},{8,14},{10,12},{12,10},{14,8},{16,22},{18,... | collective-permute-start | bytes 110600 | tf_op jit(solution)/shard_map/ppermute | solution.py:657
  16.3 4.2 %collective-permute-start.8 = (f32[32,128]{1,0:T(8,128)S(1)}, f32[32,128]{1,0:T(8,128)S(1)}, u32[]{:S(2)}, u32[]{:S(2)}) collective-permute-start(f32[32,128]{1,0:T(8,128)S(1)} %get-tuple-element.44), channel_id=1, source_target_pairs={{0,18},{2,16},{4,22},{6,20},{8,26},{10,24},{12,30},{14,28},{16,2},... | collective-permute-start | bytes 49160 | tf_op jit(solution)/shard_map/ppermute | solution.py:675

commit v8 on v7

--- a/solution.py
+++ b/solution.py
@@ -214,10 +214,11 @@
 
 def relay_kernel(groups, edges, beside_edges, *outs):
     core = lax.rem(lax.axis_index("gy"), 2)
-    mine = jnp.where(lax.axis_index("gz") == 0, core == 0, core == 1)
+    head = lax.axis_index("gz") == 0
+    mine = jnp.where(head, core == 0, core == 1)
     part = edges.shape[1] // groups
     for step, out in enumerate(outs):
-        begin = (2 * step + 1 - core) * part
+        begin = (2 * step + jnp.where(head, core, 1 - core)) * part
         for b in range(part // (2 * LANES)):
             at = pl.ds(pl.multiple_of(begin + 2 * LANES * b, 2 * LANES), 2 * LANES)
             store_planes(out, 24 * b, jnp.where(mine, edges[:, at], beside_edges[:, at]))
@@ -404,15 +405,24 @@
     out[...] = end
 
 
+def outer_share(weights, here, end, far_end, b):
+    near, far = planes_of(end, 24 * b), planes_of(far_end, 24 * b)
+    return beside(weights, lambda kind, j: jnp.where(here, near(kind, j), far(kind, j)))
+
+
 def pair_kernel(mine, other, end_mine, end_other, out, fixed_mine, fixed_other):
     core = lax.rem(lax.axis_index("gy"), 2)
+    here = lax.rem(lax.axis_index("gz"), 2) == 0
     blocks = out.shape[0] // RUN
-    for ref, across, end, target in ((mine, other, end_mine, fixed_mine), (other, mine, end_other, fixed_other)):
+    for ref, across, end, far_end, target in (
+        (mine, other, end_mine, end_other, fixed_mine),
+        (other, mine, end_other, end_mine, fixed_other),
+    ):
         inner_weights, outer_weights = weights_of(ref, 0), weights_of(ref, 8)
         for b in range(blocks):
             at, to = FIRST * b, RUN * b
             inner = beside(inner_weights, planes_of(across, at + STATE))
-            outer = beside(outer_weights, planes_of(end, 24 * b))
+            outer = outer_share(outer_weights, here, end, far_end, b)
             target[to + STATE : to + RUN] = ref[at + 48 : at + 48 + MAPS]
             for k in range(4):
                 value = ref[at + 6 * k : at + 6 * k + 6]
@@ -456,7 +466,7 @@
             )
 
 
-def block_kernel(wide, firsts, inverse, own_rhs, mine, other, end, *refs):
+def block_kernel(wide, firsts, inverse, own_rhs, mine, other, end, far_end, *refs):
     *pieces, local, rhs, split = refs
     fields, rows, lanes = rhs.shape
     g = lax.axis_index("gz")
@@ -470,7 +480,7 @@
         columns = pl.ds(2 * LANES * b, 2 * LANES)
         parts = apart(flat[:, 2 * LANES * b : 2 * LANES * (b + 1)])
         inner = beside(inner_weights, planes_of(other, FIRST * b + STATE))
-        outer = beside(outer_weights, planes_of(end, 24 * b))
+        outer = outer_share(outer_weights, lax.rem(g, 2) == 0, end, far_end, b)
         solved = []
         for p in range(2):
             split[...] = parts[p].reshape(fields, rows, LANES)
@@ -533,11 +543,10 @@
 def end_pairs(gy, gz, step):
     at = lambda y, z: y * gz + z
     pairs = []
-    for y in range(1, gy - 1, 2):
-        for core in range(2):
-            column = 2 * step + 1 - core
-            pairs.append((at(y - 1 + core, gz - 1), at(y + 1, column)))
-            pairs.append((at(y + 1 + core, 0), at(y, column)))
+    for y in range(gy - 2):
+        core = y % 2
+        pairs.append((at(y, gz - 1), at((y + 2) ^ 1, 2 * step + 1 - core)))
+        pairs.append((at(y + 2, 0), at(y ^ 1, 2 * step + core)))
     sources = sorted(set(range(gy * gz)) - {s for s, _ in pairs})
     targets = sorted(set(range(gy * gz)) - {t for _, t in pairs})
     if gz == 2:
@@ -646,7 +655,7 @@
     (local,) = vmem_call(
         functools.partial(block_kernel, wide, firsts),
         [(3, rows, lanes)],
-        [inside, rhs, message, other, end, *pieces],
+        [inside, rhs, message, other, end, other_end, *pieces],
         scratch=[vmem(3, rows, lanes), vmem(3, rows, LANES)],
         flops=2 * 10**8,
         name="block",

time: 21.5 us -> 21.5 us (level)
  waiting for transfers between devices: 3.59 us -> 4 us
  starting transfers between devices: 11.5 us -> 11.1 us
    ppermute x1, starting transfers between devices: 1.09 us -> 0.85 us  [per_device(): lax.ppermute(x, ('gy', 'gz'), end_pairs(gy, gz, step))]
    ppermute x1, waiting for transfers between devices: 1.21 us -> 1.45 us  [per_device(): lax.ppermute(x, 'gz', [(i, (i + shift) % gz) for i in range(gz)])]
    ppermute x1, starting transfers between devices: 2.76 us -> 2.52 us  [per_device(): received = lax.ppermute(last, 'gy', [(i, i ^ base ^ 1) for i in range(gy)])]
where the time goes in v8:
time: 21.5 us; the launch traced here: 21.3 us
  starting transfers between devices  11.1 us (52%)
  Pallas kernels  6.13 us (29%)
  waiting for transfers between devices  4 us (19%)
    pallas_call x15, Pallas kernels, vmem_call(): pl.pallas_call(body, out_shape=[jax.ShapeDtypeStruct(s, F32) for s in out...  6.13 us
    ppermute x3, starting transfers between devices, per_device(): lax.ppermute(composed, 'gy', [(i, i ^ x * base ^ 1) for i in range(gy)])  4.02 us
    ppermute x1, starting transfers between devices, per_device(): lax.ppermute(x, 'gz', [(i, (i + shift) % gz) for i in range(gz)])  2.62 us
    ppermute x1, starting transfers between devices, per_device(): received = lax.ppermute(last, 'gy', [(i, i ^ base ^ 1) for i in range(gy)])  2.52 us
    ppermute x1, waiting for transfers between devices, per_device(): lax.ppermute(x, 'gz', [(i, (i + shift) % gz) for i in range(gz)])  1.45 us
    ppermute x3, waiting for transfers between devices, per_device(): lax.ppermute(composed, 'gy', [(i, i ^ x * base ^ 1) for i in range(gy)])  1.23 us
    ppermute x3, starting transfers between devices, per_device(): to_core = lambda x: lax.ppermute(x, 'gy', [(i, i ^ 1) for i in range(gy)])  1.06 us
    ppermute x3, waiting for transfers between devices, per_device(): to_core = lambda x: lax.ppermute(x, 'gy', [(i, i ^ 1) for i in range(gy)])  0.85 us
  transfers between devices with their start and end apart: 9, of which 5 were waited for; matrix products, arithmetic and copies ran while one was open for 0% of the time, Pallas kernels for 19%

profile of v8, /device:TPU:0, one launch (start us, length us, event | category | flops | bytes accessed | tf_op | source)
XLA Modules:
  0.0 21.3 jit_solution(14175067779055322742)
XLA Ops:
  0.0 1.1 %load.1 = (f32[12,1024]{1,0:T(8,128)S(1)}, f32[10,24,128]{2,1,0:T(8,128)S(1)}, f32[10,14,128]{2,1,0:T(8,128)S(1)}, f32[3,40,1024]{2,1,0:T(8,128)S(1)}, f32[3,40,1024]{2,1,0:T(8,128)S(1)}) custom-call(f32[3,12,1024]{2,1,0:T(8,128)} %velocity.1, f32[3,12,1024]{2,1,0:T(8,128)} %explicit.1, f32[5,2,24]{2,1,0:T(2,128)} %bitcast.1), custom_call_target="tpu_custom_call" | custom-call | flops 20000000000 | bytes 295872 | tf_op jit(solution)/shard_map/load/pallas_call | solution.py:19
  1.1 0.5 %collective-permute-start.2 = (f32[12,1024]{1,0:T(8,128)S(1)}, f32[12,1024]{1,0:T(8,128)S(1)}, u32[]{:S(2)}, u32[]{:S(2)}) collective-permute-start(f32[12,1024]{1,0:T(8,128)S(1)} %get-tuple-element.30.edges), channel_id=1, source_target_pairs={{0,2},{2,0},{4,6},{6,4},{8,10},{10,8},{12,14},{14,12},{16,18},{18,... | collective-permute-start | bytes 147464 | tf_op jit(solution)/shard_map/ppermute | solution.py:578
  1.6 0.1 shares.1
  1.8 2.6 %collective-permute-start = (f32[216,128]{1,0:T(8,128)S(1)}, f32[216,128]{1,0:T(8,128)S(1)}, u32[]{:S(2)}, u32[]{:S(2)}) collective-permute-start(f32[216,128]{1,0:T(8,128)S(1)} %shares.1), channel_id=1, source_target_pairs={{0,1},{1,0},{2,3},{3,2},{4,5},{5,4},{6,7},{7,6},{8,9},{9,8},{10,11... | collective-permute-start | bytes 331784 | tf_op jit(solution)/shard_map/ppermute | solution.py:599
  4.4 0.0 collective-permute-done.2.beside_edges
  4.4 0.1 relay.1
  4.5 0.8 %collective-permute-start.3 = (f32[48,128]{1,0:T(8,128)S(1)}, f32[48,128]{1,0:T(8,128)S(1)}, u32[]{:S(2)}, u32[]{:S(2)}) collective-permute-start(f32[48,128]{1,0:T(8,128)S(1)} %relay.1), channel_id=1, source_target_pairs={{1,7},{4,2},{3,4},{6,1},{5,11},{8,6},{7,8},{10,5},{9,15},{12,10},{... | collective-permute-start | bytes 73736 | tf_op jit(solution)/shard_map/ppermute | solution.py:604
  5.3 1.0 %prepare.1 = (f32[4,24,512]{2,1,0:T(8,128)S(1)}, f32[72,128]{1,0:T(8,128)S(1)}) custom-call(f32[24,24,256]{2,1,0:T(8,128)} %inverse.3, f32[2,2,24,256]{3,2,1,0:T(8,128)} %spikes.3, f32[10,24,128]{2,1,0:T(8,128)S(1)} %get-tuple-element.25.coef), custom_call_target="tpu_custom_call" | custom-call | flops 20000000000 | bytes 811008 | tf_op jit(solution)/shard_map/prepare/pallas_call | solution.py:19
  6.4 0.3 %own.1 = (f32[3,24,512]{2,1,0:T(8,128)S(1)}, f32[12,512]{1,0:T(8,128)S(1)}, f32[12,512]{1,0:T(8,128)S(1)}, f32[168,128]{1,0:T(8,128)S(1)}) custom-call(f32[3,40,1024]{2,1,0:T(8,128)S(1)} %get-tuple-element.27.vel, f32[3,40,1024]{2,1,0:T(8,128)S(1)} %get-tuple-element.28.tot, f32[10,14,128]{2,1,0:T(8,128)S(1)} %get-tuple-element.29.weight, ...), custom_call_target="tpu_custom_call" | custom-call | flops 200000000 | bytes 1337344 | tf_op jit(solution)/shard_map/own/pallas_call | solution.py:19
  6.6 1.4 %collective-permute-done.refs_0_ = f32[216,128]{1,0:T(8,128)S(1)} collective-permute-done((f32[216,128]{1,0:T(8,128)S(1)}, f32[216,128]{1,0:T(8,128)S(1)}, u32[]{:S(2)}, u32[]{:S(2)}) %collective-permute-start) | collective-permute-done | bytes 110624 | tf_op jit(solution)/shard_map/ppermute | solution.py:599
  8.1 0.2 %interface.1.mine = f32[168,128]{1,0:T(8,128)S(1)} custom-call(f32[4,24,512]{2,1,0:T(8,128)S(1)} %get-tuple-element.26.inv4, f32[168,128]{1,0:T(8,128)S(1)} %get-tuple-element.32.started, f32[12,512]{1,0:T(8,128)S(1)} %get-tuple-element.33.own_values, f32[12,512]{1,0:T(8,128)S(1)} %get-tuple-element.34.own_side, f32[216,128]{1,0:T(8,128)S(1)} %collective-permute-done.refs_0_), custom_call_target="tpu_custom_call" | custom-call | bytes 442368 | tf_op jit(solution)/shard_map/interface/pallas_call | solution.py:19
  8.3 0.1 collective-permute-start.1
  8.4 0.0 collective-permute-done.3.refs_0_
  8.4 0.5 %collective-permute-start.4 = (f32[48,128]{1,0:T(8,128)S(1)}, f32[48,128]{1,0:T(8,128)S(1)}, u32[]{:S(2)}, u32[]{:S(2)}) collective-permute-start(f32[48,128]{1,0:T(8,128)S(1)} %ends.1.end_mine.end), channel_id=1, source_target_pairs={{0,2},{2,0},{4,6},{6,4},{8,10},{10,8},{12,14},{14,12},{16,18},{18,... | collective-permute-start | bytes 73736 | tf_op jit(solution)/shard_map/ppermute | solution.py:578
  8.9 0.8 %collective-permute-done.4.end_other.far_end = f32[48,128]{1,0:T(8,128)S(1)} collective-permute-done((f32[48,128]{1,0:T(8,128)S(1)}, f32[48,128]{1,0:T(8,128)S(1)}, u32[]{:S(2)}, u32[]{:S(2)}) %collective-permute-start.4) | collective-permute-done | bytes 24608 | tf_op jit(solution)/shard_map/ppermute | solution.py:578
  9.8 0.0 collective-permute-done.1.other
  9.8 0.1 pair.1
  9.9 2.7 %collective-permute-start.5 = (f32[72,128]{1,0:T(8,128)S(1)}, f32[72,128]{1,0:T(8,128)S(1)}, u32[]{:S(2)}, u32[]{:S(2)}) collective-permute-start(f32[72,128]{1,0:T(8,128)S(1)} %get-tuple-element.35.after.refs_0_), channel_id=1, source_target_pairs={{0,14},{2,12},{4,10},{6,8},{8,6},{10,4},{12,2},{14,0},{16,30},{18,... | collective-permute-start | bytes 110600 | tf_op jit(solution)/shard_map/ppermute | solution.py:666
  12.6 0.3 %collective-permute-start.6 = (f32[72,128]{1,0:T(8,128)S(1)}, f32[72,128]{1,0:T(8,128)S(1)}, u32[]{:S(2)}, u32[]{:S(2)}) collective-permute-start(f32[72,128]{1,0:T(8,128)S(1)} %get-tuple-element.35.after.refs_0_), channel_id=1, source_target_pairs={{0,10},{2,8},{4,14},{6,12},{8,2},{10,0},{12,6},{14,4},{16,26},{18,... | collective-permute-start | bytes 110600 | tf_op jit(solution)/shard_map/ppermute | solution.py:666
  12.9 1.0 %collective-permute-start.7 = (f32[72,128]{1,0:T(8,128)S(1)}, f32[72,128]{1,0:T(8,128)S(1)}, u32[]{:S(2)}, u32[]{:S(2)}) collective-permute-start(f32[72,128]{1,0:T(8,128)S(1)} %get-tuple-element.35.after.refs_0_), channel_id=1, source_target_pairs={{0,6},{2,4},{4,2},{6,0},{8,14},{10,12},{12,10},{14,8},{16,22},{18,... | collective-permute-start | bytes 110600 | tf_op jit(solution)/shard_map/ppermute | solution.py:666
  13.9 1.1 %fetch.1 = (f32[24,24,256]{2,1,0:T(8,128)S(1)}, f32[2,2,24,256]{3,2,1,0:T(8,128)S(1)}) custom-call(f32[24,24,256]{2,1,0:T(8,128)} %inverse.3, f32[2,2,24,256]{3,2,1,0:T(8,128)} %spikes.3, f32[72,128]{1,0:T(8,128)S(1)} %get-tuple-element.35.after.refs_0_), custom_call_target="tpu_custom_call" | custom-call | flops 20000000000 | bytes 724992 | tf_op jit(solution)/shard_map/fetch/pallas_call | solution.py:19
  15.0 0.1 widen.2.refs_4_
  15.0 0.0 collective-permute-done.5.refs_1_
  15.1 0.9 %collective-permute-done.6.refs_2_ = f32[72,128]{1,0:T(8,128)S(1)} collective-permute-done((f32[72,128]{1,0:T(8,128)S(1)}, f32[72,128]{1,0:T(8,128)S(1)}, u32[]{:S(2)}, u32[]{:S(2)}) %collective-permute-start.6) | collective-permute-done | bytes 36896 | tf_op jit(solution)/shard_map/ppermute | solution.py:666
  16.0 0.3 %collective-permute-done.7.refs_3_ = f32[72,128]{1,0:T(8,128)S(1)} collective-permute-done((f32[72,128]{1,0:T(8,128)S(1)}, f32[72,128]{1,0:T(8,128)S(1)}, u32[]{:S(2)}, u32[]{:S(2)}) %collective-permute-start.7) | collective-permute-done | bytes 36896 | tf_op jit(solution)/shard_map/ppermute | solution.py:666
  16.3 0.1 compose.1
  16.4 2.5 %collective-permute-start.8 = (f32[32,128]{1,0:T(8,128)S(1)}, f32[32,128]{1,0:T(8,128)S(1)}, u32[]{:S(2)}, u32[]{:S(2)}) collective-permute-start(f32[32,128]{1,0:T(8,128)S(1)} %get-tuple-element.44), channel_id=1, source_target_pairs={{0,18},{2,16},{4,22},{6,20},{8,26},{10,24},{12,30},{14,28},{16,2},... | collective-permute-start | bytes 49160 | tf_op jit(solution)/shard_map/ppermute | solution.py:684
  18.9 0.7 %block.1.local = f32[3,24,512]{2,1,0:T(8,128)S(1)} custom-call(f32[24,24,256]{2,1,0:T(8,128)S(1)} %get-tuple-element.36.inverse, f32[3,24,512]{2,1,0:T(8,128)S(1)} %get-tuple-element.37.own_rhs, f32[168,128]{1,0:T(8,128)S(1)} %interface.1.mine, f32[168,128]{1,0:T(8,128)S(1)} %collective-permute-done.1.other, f32[48,128]{1,0:T(8,128)S(1)} %ends.1.end_mine.end, ...), custom_call_target="tpu_custom_call" | custom-call | flops 200000000 | bytes 1069056 | tf_op jit(solution)/shard_map/block/pallas_call | solution.py:19
  19.6 0.2 widen.3.known
  19.8 0.3 %ready.1 = (f32[3,24,512]{2,1,0:T(8,128)S(1)}, f32[2,24,512]{2,1,0:T(8,128)S(1)}) custom-call(f32[3,24,512]{2,1,0:T(8,128)S(1)} %block.1.local, f32[2,2,24,256]{3,2,1,0:T(8,128)S(1)} %get-tuple-element.38.spikes, f32[72,128]{1,0:T(8,128)S(1)} %widen.3.known), custom_call_target="tpu_custom_call" | custom-call | flops 10000000 | bytes 282624 | tf_op jit(solution)/shard_map/ready/pallas_call | solution.py:19
  20.0 0.5 %collective-permute-done.8.received = f32[32,128]{1,0:T(8,128)S(1)} collective-permute-done((f32[32,128]{1,0:T(8,128)S(1)}, f32[32,128]{1,0:T(8,128)S(1)}, u32[]{:S(2)}, u32[]{:S(2)}) %collective-permute-start.8) | collective-permute-done | bytes 16416 | tf_op jit(solution)/shard_map/ppermute | solution.py:684
  20.5 0.8 %final.1 = f32[3,24,512]{2,1,0:T(8,128)} custom-call(f32[3,24,512]{2,1,0:T(8,128)S(1)} %get-tuple-element.41.ready, f32[2,24,512]{2,1,0:T(8,128)S(1)} %get-tuple-element.42.lift, f32[72,128]{1,0:T(8,128)S(1)} %get-tuple-element.43.composed, f32[32,128]{1,0:T(8,128)S(1)} %collective-permute-done.8.received), custom_call_target="tpu_custom_call" | custom-call | bytes 299008 | tf_op jit(solution)/shard_map/final/pallas_call | solution.py:19
  (1 shorter events, 0.0 us)
Async XLA Ops:
  1.1 3.3 %collective-permute-start.2 = (f32[12,1024]{1,0:T(8,128)S(1)}, f32[12,1024]{1,0:T(8,128)S(1)}, u32[]{:S(2)}, u32[]{:S(2)}) collective-permute-start(f32[12,1024]{1,0:T(8,128)S(1)} %get-tuple-element.30.edges), channel_id=1, source_target_pairs={{0,2},{2,0},{4,6},{6,4},{8,10},{10,8},{12,14},{14,12},{16,18},{18,... | collective-permute-start | bytes 147464 | tf_op jit(solution)/shard_map/ppermute | solution.py:578
  1.8 6.3 %collective-permute-start = (f32[216,128]{1,0:T(8,128)S(1)}, f32[216,128]{1,0:T(8,128)S(1)}, u32[]{:S(2)}, u32[]{:S(2)}) collective-permute-start(f32[216,128]{1,0:T(8,128)S(1)} %shares.1), channel_id=1, source_target_pairs={{0,1},{1,0},{2,3},{3,2},{4,5},{5,4},{6,7},{7,6},{8,9},{9,8},{10,11... | collective-permute-start | bytes 331784 | tf_op jit(solution)/shard_map/ppermute | solution.py:599
  4.5 3.9 %collective-permute-start.3 = (f32[48,128]{1,0:T(8,128)S(1)}, f32[48,128]{1,0:T(8,128)S(1)}, u32[]{:S(2)}, u32[]{:S(2)}) collective-permute-start(f32[48,128]{1,0:T(8,128)S(1)} %relay.1), channel_id=1, source_target_pairs={{1,7},{4,2},{3,4},{6,1},{5,11},{8,6},{7,8},{10,5},{9,15},{12,10},{... | collective-permute-start | bytes 73736 | tf_op jit(solution)/shard_map/ppermute | solution.py:604
  8.3 1.4 %collective-permute-start.1 = (f32[168,128]{1,0:T(8,128)S(1)}, f32[168,128]{1,0:T(8,128)S(1)}, u32[]{:S(2)}, u32[]{:S(2)}) collective-permute-start(f32[168,128]{1,0:T(8,128)S(1)} %interface.1.mine), channel_id=1, source_target_pairs={{0,2},{2,0},{4,6},{6,4},{8,10},{10,8},{12,14},{14,12},{16,18},{18,... | collective-permute-start | bytes 258056 | tf_op jit(solution)/shard_map/ppermute | solution.py:578
  8.4 1.3 %collective-permute-start.4 = (f32[48,128]{1,0:T(8,128)S(1)}, f32[48,128]{1,0:T(8,128)S(1)}, u32[]{:S(2)}, u32[]{:S(2)}) collective-permute-start(f32[48,128]{1,0:T(8,128)S(1)} %ends.1.end_mine.end), channel_id=1, source_target_pairs={{0,2},{2,0},{4,6},{6,4},{8,10},{10,8},{12,14},{14,12},{16,18},{18,... | collective-permute-start | bytes 73736 | tf_op jit(solution)/shard_map/ppermute | solution.py:578
  9.9 5.2 %collective-permute-start.5 = (f32[72,128]{1,0:T(8,128)S(1)}, f32[72,128]{1,0:T(8,128)S(1)}, u32[]{:S(2)}, u32[]{:S(2)}) collective-permute-start(f32[72,128]{1,0:T(8,128)S(1)} %get-tuple-element.35.after.refs_0_), channel_id=1, source_target_pairs={{0,14},{2,12},{4,10},{6,8},{8,6},{10,4},{12,2},{14,0},{16,30},{18,... | collective-permute-start | bytes 110600 | tf_op jit(solution)/shard_map/ppermute | solution.py:666
  12.6 3.4 %collective-permute-start.6 = (f32[72,128]{1,0:T(8,128)S(1)}, f32[72,128]{1,0:T(8,128)S(1)}, u32[]{:S(2)}, u32[]{:S(2)}) collective-permute-start(f32[72,128]{1,0:T(8,128)S(1)} %get-tuple-element.35.after.refs_0_), channel_id=1, source_target_pairs={{0,10},{2,8},{4,14},{6,12},{8,2},{10,0},{12,6},{14,4},{16,26},{18,... | collective-permute-start | bytes 110600 | tf_op jit(solution)/shard_map/ppermute | solution.py:666
  12.9 3.4 %collective-permute-start.7 = (f32[72,128]{1,0:T(8,128)S(1)}, f32[72,128]{1,0:T(8,128)S(1)}, u32[]{:S(2)}, u32[]{:S(2)}) collective-permute-start(f32[72,128]{1,0:T(8,128)S(1)} %get-tuple-element.35.after.refs_0_), channel_id=1, source_target_pairs={{0,6},{2,4},{4,2},{6,0},{8,14},{10,12},{12,10},{14,8},{16,22},{18,... | collective-permute-start | bytes 110600 | tf_op jit(solution)/shard_map/ppermute | solution.py:666
  16.4 4.1 %collective-permute-start.8 = (f32[32,128]{1,0:T(8,128)S(1)}, f32[32,128]{1,0:T(8,128)S(1)}, u32[]{:S(2)}, u32[]{:S(2)}) collective-permute-start(f32[32,128]{1,0:T(8,128)S(1)} %get-tuple-element.44), channel_id=1, source_target_pairs={{0,18},{2,16},{4,22},{6,20},{8,26},{10,24},{12,30},{14,28},{16,2},... | collective-permute-start | bytes 49160 | tf_op jit(solution)/shard_map/ppermute | solution.py:684

commit v9 on v7

--- a/solution.py
+++ b/solution.py
@@ -90,7 +90,7 @@
 
 
 def load_kernel(wide, firsts, velocity, explicit, bands, *refs):
-    edges, coef, weight, vel, tot, here, there, taps, square, sems = refs
+    edges, relayed, coef, weight, vel, tot, here, there, taps, square, sems = refs
     groups = len(firsts)
     own = velocity.shape[1]
     rows = coef.shape[1]
@@ -132,6 +132,14 @@
             top += there[f, j : j + 1]
             bottom += there[f, own - HALO + j : own - HALO + j + 1]
             edges[3 * j + f : 3 * j + f + 1] = jnp.where(g == 0, top, bottom)
+    core = lax.rem(lax.axis_index("gy"), 2)
+    part = edges.shape[1] // groups
+    for step in range(groups // 2):
+        begin = (2 * step + core) * part
+        for tile in range(part // LANES):
+            at = pl.ds(pl.multiple_of(begin + LANES * tile, LANES), LANES)
+            row = 12 * (step * (part // LANES) + tile)
+            relayed[row : row + 12] = edges[:, at]
 
 
 def stencil(vel, tot, weights, f, wide, at):
@@ -220,7 +228,9 @@
         begin = (2 * step + 1 - core) * part
         for b in range(part // (2 * LANES)):
             at = pl.ds(pl.multiple_of(begin + 2 * LANES * b, 2 * LANES), 2 * LANES)
-            store_planes(out, 24 * b, jnp.where(mine, edges[:, at], beside_edges[:, at]))
+            row = 12 * (step * (part // LANES) + 2 * b)
+            beside = jnp.concatenate([beside_edges[row : row + 12], beside_edges[row + 12 : row + 24]], axis=1)
+            store_planes(out, 24 * b, jnp.where(mine, edges[:, at], beside))
 
 
 def prepare_kernel(inverse, spikes, coef, inv4, fixed, inverse_ends, spike_ends, sems):
@@ -568,16 +578,16 @@
     blocks = modes // LANES
     to_core = lambda x: lax.ppermute(x, "gy", [(i, i ^ 1) for i in range(gy)])
     padded = (3, rows + 16, columns)
-    edges, coef, weight, vel, tot = vmem_call(
+    edges, relayed, coef, weight, vel, tot = vmem_call(
         functools.partial(load_kernel, wide, firsts),
-        [(12, columns), (10, rows, LANES), (10, wide, LANES), padded, padded],
+        [(12, columns), (24 * blocks * (gz // 2), LANES), (10, rows, LANES), (10, wide, LANES), padded, padded],
         [velocity, explicit, jnp.transpose(bands, (1, 0, 2))],
         scratch=[vmem(3, own, columns)] * 2 + [vmem(5, 2, rows), vmem(LANES, LANES), dma(3)],
         flops=2 * 10**10,
         name="load",
         far=3,
     )
-    beside_edges = to_core(edges)
+    beside_edges = to_core(relayed)
     share = ((3 * wide + 12) * 2 * blocks, LANES)
     shares = vmem_call(
         functools.partial(shares_kernel, wide),

time: 21.5 us -> 21.5 us (level)
  no operation moved by 1% of the time
where the time goes in v9:
time: 21.5 us; the launch traced here: 21.3 us
  starting transfers between devices  11.4 us (53%)
  Pallas kernels  6.14 us (29%)
  waiting for transfers between devices  3.69 us (17%)
    pallas_call x15, Pallas kernels, vmem_call(): pl.pallas_call(body, out_shape=[jax.ShapeDtypeStruct(s, F32) for s in out...  6.14 us
    ppermute x3, starting transfers between devices, per_device(): lax.ppermute(composed, 'gy', [(i, i ^ x * base ^ 1) for i in range(gy)])  4.03 us
    ppermute x1, starting transfers between devices, per_device(): received = lax.ppermute(last, 'gy', [(i, i ^ base ^ 1) for i in range(gy)])  2.64 us
    ppermute x1, starting transfers between devices, per_device(): lax.ppermute(x, 'gz', [(i, (i + shift) % gz) for i in range(gz)])  2.62 us
    ppermute x1, waiting for transfers between devices, per_device(): lax.ppermute(x, 'gz', [(i, (i + shift) % gz) for i in range(gz)])  1.26 us
    ppermute x3, waiting for transfers between devices, per_device(): lax.ppermute(composed, 'gy', [(i, i ^ x * base ^ 1) for i in range(gy)])  1.23 us
    ppermute x3, starting transfers between devices, per_device(): to_core = lambda x: lax.ppermute(x, 'gy', [(i, i ^ 1) for i in range(gy)])  1.07 us
    ppermute x1, starting transfers between devices, per_device(): lax.ppermute(x, ('gy', 'gz'), end_pairs(gy, gz, step))  1.03 us
  transfers between devices with their start and end apart: 9, of which 5 were waited for; matrix products, arithmetic and copies ran while one was open for 0% of the time, Pallas kernels for 19%

profile of v9, /device:TPU:0, one launch (start us, length us, event | category | flops | bytes accessed | tf_op | source)
XLA Modules:
  0.0 21.3 jit_solution(17156403780789982411)
XLA Ops:
  0.0 1.1 %load.1 = (f32[12,1024]{1,0:T(8,128)S(1)}, f32[48,128]{1,0:T(8,128)S(1)}, f32[10,24,128]{2,1,0:T(8,128)S(1)}, f32[10,14,128]{2,1,0:T(8,128)S(1)}, f32[3,40,1024]...) custom-call(f32[3,12,1024]{2,1,0:T(8,128)} %velocity.1, f32[3,12,1024]{2,1,0:T(8,128)} %explicit.1, f32[5,2,24]{2,1,0:T(2,128)} %bitcast.1), custom_call_target="tpu_custom_call" | custom-call | flops 20000000000 | bytes 295872 | tf_op jit(solution)/shard_map/load/pallas_call | solution.py:19
  1.1 0.5 %collective-permute-start.2 = (f32[48,128]{1,0:T(8,128)S(1)}, f32[48,128]{1,0:T(8,128)S(1)}, u32[]{:S(2)}, u32[]{:S(2)}) collective-permute-start(f32[48,128]{1,0:T(8,128)S(1)} %get-tuple-element.36), channel_id=1, source_target_pairs={{0,2},{2,0},{4,6},{6,4},{8,10},{10,8},{12,14},{14,12},{16,18},{18,... | collective-permute-start | bytes 73736 | tf_op jit(solution)/shard_map/ppermute | solution.py:579
  1.6 0.1 shares.1
  1.8 2.6 %collective-permute-start = (f32[216,128]{1,0:T(8,128)S(1)}, f32[216,128]{1,0:T(8,128)S(1)}, u32[]{:S(2)}, u32[]{:S(2)}) collective-permute-start(f32[216,128]{1,0:T(8,128)S(1)} %shares.1), channel_id=1, source_target_pairs={{0,1},{1,0},{2,3},{3,2},{4,5},{5,4},{6,7},{7,6},{8,9},{9,8},{10,11... | collective-permute-start | bytes 331784 | tf_op jit(solution)/shard_map/ppermute | solution.py:600
  4.4 0.0 collective-permute-done.2.beside_edges
  4.4 0.1 relay.1
  4.5 1.0 %collective-permute-start.3 = (f32[48,128]{1,0:T(8,128)S(1)}, f32[48,128]{1,0:T(8,128)S(1)}, u32[]{:S(2)}, u32[]{:S(2)}) collective-permute-start(f32[48,128]{1,0:T(8,128)S(1)} %relay.1), channel_id=1, source_target_pairs={{1,5},{4,3},{3,4},{6,2},{5,9},{8,7},{7,8},{10,6},{9,13},{12,11},{1... | collective-permute-start | bytes 73736 | tf_op jit(solution)/shard_map/ppermute | solution.py:605
  5.5 1.0 %prepare.1 = (f32[4,24,512]{2,1,0:T(8,128)S(1)}, f32[72,128]{1,0:T(8,128)S(1)}) custom-call(f32[24,24,256]{2,1,0:T(8,128)} %inverse.3, f32[2,2,24,256]{3,2,1,0:T(8,128)} %spikes.3, f32[10,24,128]{2,1,0:T(8,128)S(1)} %get-tuple-element.26.coef), custom_call_target="tpu_custom_call" | custom-call | flops 20000000000 | bytes 811008 | tf_op jit(solution)/shard_map/prepare/pallas_call | solution.py:19
  6.6 0.3 %own.1 = (f32[3,24,512]{2,1,0:T(8,128)S(1)}, f32[12,512]{1,0:T(8,128)S(1)}, f32[12,512]{1,0:T(8,128)S(1)}, f32[168,128]{1,0:T(8,128)S(1)}) custom-call(f32[3,40,1024]{2,1,0:T(8,128)S(1)} %get-tuple-element.28.vel, f32[3,40,1024]{2,1,0:T(8,128)S(1)} %get-tuple-element.29.tot, f32[10,14,128]{2,1,0:T(8,128)S(1)} %get-tuple-element.30.weight, ...), custom_call_target="tpu_custom_call" | custom-call | flops 200000000 | bytes 1337344 | tf_op jit(solution)/shard_map/own/pallas_call | solution.py:19
  6.8 1.3 %collective-permute-done.refs_0_ = f32[216,128]{1,0:T(8,128)S(1)} collective-permute-done((f32[216,128]{1,0:T(8,128)S(1)}, f32[216,128]{1,0:T(8,128)S(1)}, u32[]{:S(2)}, u32[]{:S(2)}) %collective-permute-start) | collective-permute-done | bytes 110624 | tf_op jit(solution)/shard_map/ppermute | solution.py:600
  8.1 0.2 %interface.1.mine = f32[168,128]{1,0:T(8,128)S(1)} custom-call(f32[4,24,512]{2,1,0:T(8,128)S(1)} %get-tuple-element.27.inv4, f32[168,128]{1,0:T(8,128)S(1)} %get-tuple-element.33.started, f32[12,512]{1,0:T(8,128)S(1)} %get-tuple-element.34.own_values, f32[12,512]{1,0:T(8,128)S(1)} %get-tuple-element.35.own_side, f32[216,128]{1,0:T(8,128)S(1)} %collective-permute-done.refs_0_), custom_call_target="tpu_custom_call" | custom-call | bytes 442368 | tf_op jit(solution)/shard_map/interface/pallas_call | solution.py:19
  8.3 0.1 collective-permute-start.1
  8.4 0.0 collective-permute-done.3.refs_0_
  8.4 0.5 %collective-permute-start.4 = (f32[48,128]{1,0:T(8,128)S(1)}, f32[48,128]{1,0:T(8,128)S(1)}, u32[]{:S(2)}, u32[]{:S(2)}) collective-permute-start(f32[48,128]{1,0:T(8,128)S(1)} %ends.1.end_mine.end), channel_id=1, source_target_pairs={{0,2},{2,0},{4,6},{6,4},{8,10},{10,8},{12,14},{14,12},{16,18},{18,... | collective-permute-start | bytes 73736 | tf_op jit(solution)/shard_map/ppermute | solution.py:579
  8.9 0.8 %collective-permute-done.4.end_other = f32[48,128]{1,0:T(8,128)S(1)} collective-permute-done((f32[48,128]{1,0:T(8,128)S(1)}, f32[48,128]{1,0:T(8,128)S(1)}, u32[]{:S(2)}, u32[]{:S(2)}) %collective-permute-start.4) | collective-permute-done | bytes 24608 | tf_op jit(solution)/shard_map/ppermute | solution.py:579
  9.8 0.0 collective-permute-done.1.other
  9.8 0.1 pair.1
  9.9 2.7 %collective-permute-start.5 = (f32[72,128]{1,0:T(8,128)S(1)}, f32[72,128]{1,0:T(8,128)S(1)}, u32[]{:S(2)}, u32[]{:S(2)}) collective-permute-start(f32[72,128]{1,0:T(8,128)S(1)} %get-tuple-element.37.after.refs_0_), channel_id=1, source_target_pairs={{0,14},{2,12},{4,10},{6,8},{8,6},{10,4},{12,2},{14,0},{16,30},{18,... | collective-permute-start | bytes 110600 | tf_op jit(solution)/shard_map/ppermute | solution.py:667
  12.6 0.3 %collective-permute-start.6 = (f32[72,128]{1,0:T(8,128)S(1)}, f32[72,128]{1,0:T(8,128)S(1)}, u32[]{:S(2)}, u32[]{:S(2)}) collective-permute-start(f32[72,128]{1,0:T(8,128)S(1)} %get-tuple-element.37.after.refs_0_), channel_id=1, source_target_pairs={{0,10},{2,8},{4,14},{6,12},{8,2},{10,0},{12,6},{14,4},{16,26},{18,... | collective-permute-start | bytes 110600 | tf_op jit(solution)/shard_map/ppermute | solution.py:667
  12.9 1.0 %collective-permute-start.7 = (f32[72,128]{1,0:T(8,128)S(1)}, f32[72,128]{1,0:T(8,128)S(1)}, u32[]{:S(2)}, u32[]{:S(2)}) collective-permute-start(f32[72,128]{1,0:T(8,128)S(1)} %get-tuple-element.37.after.refs_0_), channel_id=1, source_target_pairs={{0,6},{2,4},{4,2},{6,0},{8,14},{10,12},{12,10},{14,8},{16,22},{18,... | collective-permute-start | bytes 110600 | tf_op jit(solution)/shard_map/ppermute | solution.py:667
  13.9 1.1 %fetch.1 = (f32[24,24,256]{2,1,0:T(8,128)S(1)}, f32[2,2,24,256]{3,2,1,0:T(8,128)S(1)}) custom-call(f32[24,24,256]{2,1,0:T(8,128)} %inverse.3, f32[2,2,24,256]{3,2,1,0:T(8,128)} %spikes.3, f32[72,128]{1,0:T(8,128)S(1)} %get-tuple-element.37.after.refs_0_), custom_call_target="tpu_custom_call" | custom-call | flops 20000000000 | bytes 724992 | tf_op jit(solution)/shard_map/fetch/pallas_call | solution.py:19
  15.0 0.1 widen.2.refs_4_
  15.1 0.0 collective-permute-done.5.refs_1_
  15.1 0.9 %collective-permute-done.6.refs_2_ = f32[72,128]{1,0:T(8,128)S(1)} collective-permute-done((f32[72,128]{1,0:T(8,128)S(1)}, f32[72,128]{1,0:T(8,128)S(1)}, u32[]{:S(2)}, u32[]{:S(2)}) %collective-permute-start.6) | collective-permute-done | bytes 36896 | tf_op jit(solution)/shard_map/ppermute | solution.py:667
  16.0 0.3 %collective-permute-done.7.refs_3_ = f32[72,128]{1,0:T(8,128)S(1)} collective-permute-done((f32[72,128]{1,0:T(8,128)S(1)}, f32[72,128]{1,0:T(8,128)S(1)}, u32[]{:S(2)}, u32[]{:S(2)}) %collective-permute-start.7) | collective-permute-done | bytes 36896 | tf_op jit(solution)/shard_map/ppermute | solution.py:667
  16.3 0.1 compose.1
  16.4 2.6 %collective-permute-start.8 = (f32[32,128]{1,0:T(8,128)S(1)}, f32[32,128]{1,0:T(8,128)S(1)}, u32[]{:S(2)}, u32[]{:S(2)}) collective-permute-start(f32[32,128]{1,0:T(8,128)S(1)} %get-tuple-element.46), channel_id=1, source_target_pairs={{0,18},{2,16},{4,22},{6,20},{8,26},{10,24},{12,30},{14,28},{16,2},... | collective-permute-start | bytes 49160 | tf_op jit(solution)/shard_map/ppermute | solution.py:685
  19.0 0.7 %block.1.local = f32[3,24,512]{2,1,0:T(8,128)S(1)} custom-call(f32[24,24,256]{2,1,0:T(8,128)S(1)} %get-tuple-element.38.inverse, f32[3,24,512]{2,1,0:T(8,128)S(1)} %get-tuple-element.39.own_rhs, f32[168,128]{1,0:T(8,128)S(1)} %interface.1.mine, f32[168,128]{1,0:T(8,128)S(1)} %collective-permute-done.1.other, f32[48,128]{1,0:T(8,128)S(1)} %ends.1.end_mine.end, ...), custom_call_target="tpu_custom_call" | custom-call | flops 200000000 | bytes 1044480 | tf_op jit(solution)/shard_map/block/pallas_call | solution.py:19
  19.7 0.2 widen.3.known
  19.9 0.3 %ready.1 = (f32[3,24,512]{2,1,0:T(8,128)S(1)}, f32[2,24,512]{2,1,0:T(8,128)S(1)}) custom-call(f32[3,24,512]{2,1,0:T(8,128)S(1)} %block.1.local, f32[2,2,24,256]{3,2,1,0:T(8,128)S(1)} %get-tuple-element.40.spikes, f32[72,128]{1,0:T(8,128)S(1)} %widen.3.known), custom_call_target="tpu_custom_call" | custom-call | flops 10000000 | bytes 282624 | tf_op jit(solution)/shard_map/ready/pallas_call | solution.py:19
  20.2 0.3 %collective-permute-done.8.received = f32[32,128]{1,0:T(8,128)S(1)} collective-permute-done((f32[32,128]{1,0:T(8,128)S(1)}, f32[32,128]{1,0:T(8,128)S(1)}, u32[]{:S(2)}, u32[]{:S(2)}) %collective-permute-start.8) | collective-permute-done | bytes 16416 | tf_op jit(solution)/shard_map/ppermute | solution.py:685
  20.5 0.8 %final.1 = f32[3,24,512]{2,1,0:T(8,128)} custom-call(f32[3,24,512]{2,1,0:T(8,128)S(1)} %get-tuple-element.43.ready, f32[2,24,512]{2,1,0:T(8,128)S(1)} %get-tuple-element.44.lift, f32[72,128]{1,0:T(8,128)S(1)} %get-tuple-element.45.composed, f32[32,128]{1,0:T(8,128)S(1)} %collective-permute-done.8.received), custom_call_target="tpu_custom_call" | custom-call | bytes 299008 | tf_op jit(solution)/shard_map/final/pallas_call | solution.py:19
  (1 shorter events, 0.0 us)
Async XLA Ops:
  1.1 3.3 %collective-permute-start.2 = (f32[48,128]{1,0:T(8,128)S(1)}, f32[48,128]{1,0:T(8,128)S(1)}, u32[]{:S(2)}, u32[]{:S(2)}) collective-permute-start(f32[48,128]{1,0:T(8,128)S(1)} %get-tuple-element.36), channel_id=1, source_target_pairs={{0,2},{2,0},{4,6},{6,4},{8,10},{10,8},{12,14},{14,12},{16,18},{18,... | collective-permute-start | bytes 73736 | tf_op jit(solution)/shard_map/ppermute | solution.py:579
  1.8 6.3 %collective-permute-start = (f32[216,128]{1,0:T(8,128)S(1)}, f32[216,128]{1,0:T(8,128)S(1)}, u32[]{:S(2)}, u32[]{:S(2)}) collective-permute-start(f32[216,128]{1,0:T(8,128)S(1)} %shares.1), channel_id=1, source_target_pairs={{0,1},{1,0},{2,3},{3,2},{4,5},{5,4},{6,7},{7,6},{8,9},{9,8},{10,11... | collective-permute-start | bytes 331784 | tf_op jit(solution)/shard_map/ppermute | solution.py:600
  4.5 3.9 %collective-permute-start.3 = (f32[48,128]{1,0:T(8,128)S(1)}, f32[48,128]{1,0:T(8,128)S(1)}, u32[]{:S(2)}, u32[]{:S(2)}) collective-permute-start(f32[48,128]{1,0:T(8,128)S(1)} %relay.1), channel_id=1, source_target_pairs={{1,5},{4,3},{3,4},{6,2},{5,9},{8,7},{7,8},{10,6},{9,13},{12,11},{1... | collective-permute-start | bytes 73736 | tf_op jit(solution)/shard_map/ppermute | solution.py:605
  8.3 1.4 %collective-permute-start.1 = (f32[168,128]{1,0:T(8,128)S(1)}, f32[168,128]{1,0:T(8,128)S(1)}, u32[]{:S(2)}, u32[]{:S(2)}) collective-permute-start(f32[168,128]{1,0:T(8,128)S(1)} %interface.1.mine), channel_id=1, source_target_pairs={{0,2},{2,0},{4,6},{6,4},{8,10},{10,8},{12,14},{14,12},{16,18},{18,... | collective-permute-start | bytes 258056 | tf_op jit(solution)/shard_map/ppermute | solution.py:579
  8.4 1.3 %collective-permute-start.4 = (f32[48,128]{1,0:T(8,128)S(1)}, f32[48,128]{1,0:T(8,128)S(1)}, u32[]{:S(2)}, u32[]{:S(2)}) collective-permute-start(f32[48,128]{1,0:T(8,128)S(1)} %ends.1.end_mine.end), channel_id=1, source_target_pairs={{0,2},{2,0},{4,6},{6,4},{8,10},{10,8},{12,14},{14,12},{16,18},{18,... | collective-permute-start | bytes 73736 | tf_op jit(solution)/shard_map/ppermute | solution.py:579
  9.9 5.2 %collective-permute-start.5 = (f32[72,128]{1,0:T(8,128)S(1)}, f32[72,128]{1,0:T(8,128)S(1)}, u32[]{:S(2)}, u32[]{:S(2)}) collective-permute-start(f32[72,128]{1,0:T(8,128)S(1)} %get-tuple-element.37.after.refs_0_), channel_id=1, source_target_pairs={{0,14},{2,12},{4,10},{6,8},{8,6},{10,4},{12,2},{14,0},{16,30},{18,... | collective-permute-start | bytes 110600 | tf_op jit(solution)/shard_map/ppermute | solution.py:667
  12.6 3.4 %collective-permute-start.6 = (f32[72,128]{1,0:T(8,128)S(1)}, f32[72,128]{1,0:T(8,128)S(1)}, u32[]{:S(2)}, u32[]{:S(2)}) collective-permute-start(f32[72,128]{1,0:T(8,128)S(1)} %get-tuple-element.37.after.refs_0_), channel_id=1, source_target_pairs={{0,10},{2,8},{4,14},{6,12},{8,2},{10,0},{12,6},{14,4},{16,26},{18,... | collective-permute-start | bytes 110600 | tf_op jit(solution)/shard_map/ppermute | solution.py:667
  12.9 3.4 %collective-permute-start.7 = (f32[72,128]{1,0:T(8,128)S(1)}, f32[72,128]{1,0:T(8,128)S(1)}, u32[]{:S(2)}, u32[]{:S(2)}) collective-permute-start(f32[72,128]{1,0:T(8,128)S(1)} %get-tuple-element.37.after.refs_0_), channel_id=1, source_target_pairs={{0,6},{2,4},{4,2},{6,0},{8,14},{10,12},{12,10},{14,8},{16,22},{18,... | collective-permute-start | bytes 110600 | tf_op jit(solution)/shard_map/ppermute | solution.py:667
  16.4 4.1 %collective-permute-start.8 = (f32[32,128]{1,0:T(8,128)S(1)}, f32[32,128]{1,0:T(8,128)S(1)}, u32[]{:S(2)}, u32[]{:S(2)}) collective-permute-start(f32[32,128]{1,0:T(8,128)S(1)} %get-tuple-element.46), channel_id=1, source_target_pairs={{0,18},{2,16},{4,22},{6,20},{8,26},{10,24},{12,30},{14,28},{16,2},... | collective-permute-start | bytes 49160 | tf_op jit(solution)/shard_map/ppermute | solution.py:685

commit v10 on v8

--- a/solution.py
+++ b/solution.py
@@ -90,7 +90,7 @@
 
 
 def load_kernel(wide, firsts, velocity, explicit, bands, *refs):
-    edges, coef, weight, vel, tot, here, there, taps, square, sems = refs
+    edges, relayed, coef, weight, vel, tot, here, there, taps, square, sems = refs
     groups = len(firsts)
     own = velocity.shape[1]
     rows = coef.shape[1]
@@ -132,6 +132,14 @@
             top += there[f, j : j + 1]
             bottom += there[f, own - HALO + j : own - HALO + j + 1]
             edges[3 * j + f : 3 * j + f + 1] = jnp.where(g == 0, top, bottom)
+    core = lax.rem(lax.axis_index("gy"), 2)
+    part = edges.shape[1] // groups
+    for step in range(groups // 2):
+        begin = (2 * step + jnp.where(g == 0, 1 - core, core)) * part
+        for tile in range(part // LANES):
+            at = pl.ds(pl.multiple_of(begin + LANES * tile, LANES), LANES)
+            row = 12 * (step * (part // LANES) + tile)
+            relayed[row : row + 12] = edges[:, at]
 
 
 def stencil(vel, tot, weights, f, wide, at):
@@ -221,7 +229,9 @@
         begin = (2 * step + jnp.where(head, core, 1 - core)) * part
         for b in range(part // (2 * LANES)):
             at = pl.ds(pl.multiple_of(begin + 2 * LANES * b, 2 * LANES), 2 * LANES)
-            store_planes(out, 24 * b, jnp.where(mine, edges[:, at], beside_edges[:, at]))
+            row = 12 * (step * (part // LANES) + 2 * b)
+            beside = jnp.concatenate([beside_edges[row : row + 12], beside_edges[row + 12 : row + 24]], axis=1)
+            store_planes(out, 24 * b, jnp.where(mine, edges[:, at], beside))
 
 
 def prepare_kernel(inverse, spikes, coef, inv4, fixed, inverse_ends, spike_ends, sems):
@@ -577,16 +587,16 @@
     blocks = modes // LANES
     to_core = lambda x: lax.ppermute(x, "gy", [(i, i ^ 1) for i in range(gy)])
     padded = (3, rows + 16, columns)
-    edges, coef, weight, vel, tot = vmem_call(
+    edges, relayed, coef, weight, vel, tot = vmem_call(
         functools.partial(load_kernel, wide, firsts),
-        [(12, columns), (10, rows, LANES), (10, wide, LANES), padded, padded],
+        [(12, columns), (24 * blocks * (gz // 2), LANES), (10, rows, LANES), (10, wide, LANES), padded, padded],
         [velocity, explicit, jnp.transpose(bands, (1, 0, 2))],
         scratch=[vmem(3, own, columns)] * 2 + [vmem(5, 2, rows), vmem(LANES, LANES), dma(3)],
         flops=2 * 10**10,
         name="load",
         far=3,
     )
-    beside_edges = to_core(edges)
+    beside_edges = to_core(relayed)
     share = ((3 * wide + 12) * 2 * blocks, LANES)
     shares = vmem_call(
         functools.partial(shares_kernel, wide),

time: 21.5 us -> 21.5 us (level)
  no operation moved by 1% of the time
where the time goes in v10:
time: 21.5 us; the launch traced here: 21.3 us
  starting transfers between devices  11 us (51%)
  Pallas kernels  6.14 us (29%)
  waiting for transfers between devices  3.98 us (19%)
    pallas_call x15, Pallas kernels, vmem_call(): pl.pallas_call(body, out_shape=[jax.ShapeDtypeStruct(s, F32) for s in out...  6.14 us
    ppermute x3, starting transfers between devices, per_device(): lax.ppermute(composed, 'gy', [(i, i ^ x * base ^ 1) for i in range(gy)])  3.97 us
    ppermute x1, starting transfers between devices, per_device(): lax.ppermute(x, 'gz', [(i, (i + shift) % gz) for i in range(gz)])  2.62 us
    ppermute x1, starting transfers between devices, per_device(): received = lax.ppermute(last, 'gy', [(i, i ^ base ^ 1) for i in range(gy)])  2.58 us
    ppermute x1, waiting for transfers between devices, per_device(): lax.ppermute(x, 'gz', [(i, (i + shift) % gz) for i in range(gz)])  1.5 us
    ppermute x3, waiting for transfers between devices, per_device(): lax.ppermute(composed, 'gy', [(i, i ^ x * base ^ 1) for i in range(gy)])  1.23 us
    ppermute x3, starting transfers between devices, per_device(): to_core = lambda x: lax.ppermute(x, 'gy', [(i, i ^ 1) for i in range(gy)])  1.06 us
    ppermute x3, waiting for transfers between devices, per_device(): to_core = lambda x: lax.ppermute(x, 'gy', [(i, i ^ 1) for i in range(gy)])  0.85 us
  transfers between devices with their start and end apart: 9, of which 5 were waited for; matrix products, arithmetic and copies ran while one was open for 0% of the time, Pallas kernels for 19%

profile of v10, /device:TPU:0, one launch (start us, length us, event | category | flops | bytes accessed | tf_op | source)
XLA Modules:
  0.0 21.3 jit_solution(336242683555365581)
XLA Ops:
  0.0 1.1 %load.1 = (f32[12,1024]{1,0:T(8,128)S(1)}, f32[48,128]{1,0:T(8,128)S(1)}, f32[10,24,128]{2,1,0:T(8,128)S(1)}, f32[10,14,128]{2,1,0:T(8,128)S(1)}, f32[3,40,1024]...) custom-call(f32[3,12,1024]{2,1,0:T(8,128)} %velocity.1, f32[3,12,1024]{2,1,0:T(8,128)} %explicit.1, f32[5,2,24]{2,1,0:T(2,128)} %bitcast.1), custom_call_target="tpu_custom_call" | custom-call | flops 20000000000 | bytes 295872 | tf_op jit(solution)/shard_map/load/pallas_call | solution.py:19
  1.1 0.5 %collective-permute-start.2 = (f32[48,128]{1,0:T(8,128)S(1)}, f32[48,128]{1,0:T(8,128)S(1)}, u32[]{:S(2)}, u32[]{:S(2)}) collective-permute-start(f32[48,128]{1,0:T(8,128)S(1)} %get-tuple-element.36), channel_id=1, source_target_pairs={{0,2},{2,0},{4,6},{6,4},{8,10},{10,8},{12,14},{14,12},{16,18},{18,... | collective-permute-start | bytes 73736 | tf_op jit(solution)/shard_map/ppermute | solution.py:588
  1.6 0.1 shares.1
  1.8 2.6 %collective-permute-start = (f32[216,128]{1,0:T(8,128)S(1)}, f32[216,128]{1,0:T(8,128)S(1)}, u32[]{:S(2)}, u32[]{:S(2)}) collective-permute-start(f32[216,128]{1,0:T(8,128)S(1)} %shares.1), channel_id=1, source_target_pairs={{0,1},{1,0},{2,3},{3,2},{4,5},{5,4},{6,7},{7,6},{8,9},{9,8},{10,11... | collective-permute-start | bytes 331784 | tf_op jit(solution)/shard_map/ppermute | solution.py:609
  4.4 0.0 collective-permute-done.2.beside_edges
  4.4 0.1 relay.1
  4.5 0.8 %collective-permute-start.3 = (f32[48,128]{1,0:T(8,128)S(1)}, f32[48,128]{1,0:T(8,128)S(1)}, u32[]{:S(2)}, u32[]{:S(2)}) collective-permute-start(f32[48,128]{1,0:T(8,128)S(1)} %relay.1), channel_id=1, source_target_pairs={{1,7},{4,2},{3,4},{6,1},{5,11},{8,6},{7,8},{10,5},{9,15},{12,10},{... | collective-permute-start | bytes 73736 | tf_op jit(solution)/shard_map/ppermute | solution.py:614
  5.3 1.0 %prepare.1 = (f32[4,24,512]{2,1,0:T(8,128)S(1)}, f32[72,128]{1,0:T(8,128)S(1)}) custom-call(f32[24,24,256]{2,1,0:T(8,128)} %inverse.3, f32[2,2,24,256]{3,2,1,0:T(8,128)} %spikes.3, f32[10,24,128]{2,1,0:T(8,128)S(1)} %get-tuple-element.26.coef), custom_call_target="tpu_custom_call" | custom-call | flops 20000000000 | bytes 811008 | tf_op jit(solution)/shard_map/prepare/pallas_call | solution.py:19
  6.3 0.3 %own.1 = (f32[3,24,512]{2,1,0:T(8,128)S(1)}, f32[12,512]{1,0:T(8,128)S(1)}, f32[12,512]{1,0:T(8,128)S(1)}, f32[168,128]{1,0:T(8,128)S(1)}) custom-call(f32[3,40,1024]{2,1,0:T(8,128)S(1)} %get-tuple-element.28.vel, f32[3,40,1024]{2,1,0:T(8,128)S(1)} %get-tuple-element.29.tot, f32[10,14,128]{2,1,0:T(8,128)S(1)} %get-tuple-element.30.weight, ...), custom_call_target="tpu_custom_call" | custom-call | flops 200000000 | bytes 1337344 | tf_op jit(solution)/shard_map/own/pallas_call | solution.py:19
  6.6 1.5 %collective-permute-done.refs_0_ = f32[216,128]{1,0:T(8,128)S(1)} collective-permute-done((f32[216,128]{1,0:T(8,128)S(1)}, f32[216,128]{1,0:T(8,128)S(1)}, u32[]{:S(2)}, u32[]{:S(2)}) %collective-permute-start) | collective-permute-done | bytes 110624 | tf_op jit(solution)/shard_map/ppermute | solution.py:609
  8.1 0.2 %interface.1.mine = f32[168,128]{1,0:T(8,128)S(1)} custom-call(f32[4,24,512]{2,1,0:T(8,128)S(1)} %get-tuple-element.27.inv4, f32[168,128]{1,0:T(8,128)S(1)} %get-tuple-element.33.started, f32[12,512]{1,0:T(8,128)S(1)} %get-tuple-element.34.own_values, f32[12,512]{1,0:T(8,128)S(1)} %get-tuple-element.35.own_side, f32[216,128]{1,0:T(8,128)S(1)} %collective-permute-done.refs_0_), custom_call_target="tpu_custom_call" | custom-call | bytes 442368 | tf_op jit(solution)/shard_map/interface/pallas_call | solution.py:19
  8.3 0.1 collective-permute-start.1
  8.4 0.0 collective-permute-done.3.refs_0_
  8.4 0.5 %collective-permute-start.4 = (f32[48,128]{1,0:T(8,128)S(1)}, f32[48,128]{1,0:T(8,128)S(1)}, u32[]{:S(2)}, u32[]{:S(2)}) collective-permute-start(f32[48,128]{1,0:T(8,128)S(1)} %ends.1.end_mine.end), channel_id=1, source_target_pairs={{0,2},{2,0},{4,6},{6,4},{8,10},{10,8},{12,14},{14,12},{16,18},{18,... | collective-permute-start | bytes 73736 | tf_op jit(solution)/shard_map/ppermute | solution.py:588
  8.9 0.8 %collective-permute-done.4.end_other.far_end = f32[48,128]{1,0:T(8,128)S(1)} collective-permute-done((f32[48,128]{1,0:T(8,128)S(1)}, f32[48,128]{1,0:T(8,128)S(1)}, u32[]{:S(2)}, u32[]{:S(2)}) %collective-permute-start.4) | collective-permute-done | bytes 24608 | tf_op jit(solution)/shard_map/ppermute | solution.py:588
  9.8 0.0 collective-permute-done.1.other
  9.8 0.1 pair.1
  9.9 2.7 %collective-permute-start.5 = (f32[72,128]{1,0:T(8,128)S(1)}, f32[72,128]{1,0:T(8,128)S(1)}, u32[]{:S(2)}, u32[]{:S(2)}) collective-permute-start(f32[72,128]{1,0:T(8,128)S(1)} %get-tuple-element.37.after.refs_0_), channel_id=1, source_target_pairs={{0,14},{2,12},{4,10},{6,8},{8,6},{10,4},{12,2},{14,0},{16,30},{18,... | collective-permute-start | bytes 110600 | tf_op jit(solution)/shard_map/ppermute | solution.py:676
  12.6 0.2 %collective-permute-start.6 = (f32[72,128]{1,0:T(8,128)S(1)}, f32[72,128]{1,0:T(8,128)S(1)}, u32[]{:S(2)}, u32[]{:S(2)}) collective-permute-start(f32[72,128]{1,0:T(8,128)S(1)} %get-tuple-element.37.after.refs_0_), channel_id=1, source_target_pairs={{0,10},{2,8},{4,14},{6,12},{8,2},{10,0},{12,6},{14,4},{16,26},{18,... | collective-permute-start | bytes 110600 | tf_op jit(solution)/shard_map/ppermute | solution.py:676
  12.9 1.0 %collective-permute-start.7 = (f32[72,128]{1,0:T(8,128)S(1)}, f32[72,128]{1,0:T(8,128)S(1)}, u32[]{:S(2)}, u32[]{:S(2)}) collective-permute-start(f32[72,128]{1,0:T(8,128)S(1)} %get-tuple-element.37.after.refs_0_), channel_id=1, source_target_pairs={{0,6},{2,4},{4,2},{6,0},{8,14},{10,12},{12,10},{14,8},{16,22},{18,... | collective-permute-start | bytes 110600 | tf_op jit(solution)/shard_map/ppermute | solution.py:676
  13.8 1.1 %fetch.1 = (f32[24,24,256]{2,1,0:T(8,128)S(1)}, f32[2,2,24,256]{3,2,1,0:T(8,128)S(1)}) custom-call(f32[24,24,256]{2,1,0:T(8,128)} %inverse.3, f32[2,2,24,256]{3,2,1,0:T(8,128)} %spikes.3, f32[72,128]{1,0:T(8,128)S(1)} %get-tuple-element.37.after.refs_0_), custom_call_target="tpu_custom_call" | custom-call | flops 20000000000 | bytes 724992 | tf_op jit(solution)/shard_map/fetch/pallas_call | solution.py:19
  14.9 0.1 widen.2.refs_4_
  15.0 0.0 collective-permute-done.5.refs_1_
  15.0 1.1 %collective-permute-done.6.refs_2_ = f32[72,128]{1,0:T(8,128)S(1)} collective-permute-done((f32[72,128]{1,0:T(8,128)S(1)}, f32[72,128]{1,0:T(8,128)S(1)}, u32[]{:S(2)}, u32[]{:S(2)}) %collective-permute-start.6) | collective-permute-done | bytes 36896 | tf_op jit(solution)/shard_map/ppermute | solution.py:676
  16.1 0.1 collective-permute-done.7.refs_3_
  16.2 0.1 compose.1
  16.3 2.6 %collective-permute-start.8 = (f32[32,128]{1,0:T(8,128)S(1)}, f32[32,128]{1,0:T(8,128)S(1)}, u32[]{:S(2)}, u32[]{:S(2)}) collective-permute-start(f32[32,128]{1,0:T(8,128)S(1)} %get-tuple-element.46), channel_id=1, source_target_pairs={{0,18},{2,16},{4,22},{6,20},{8,26},{10,24},{12,30},{14,28},{16,2},... | collective-permute-start | bytes 49160 | tf_op jit(solution)/shard_map/ppermute | solution.py:694
  18.9 0.7 %block.1.local = f32[3,24,512]{2,1,0:T(8,128)S(1)} custom-call(f32[24,24,256]{2,1,0:T(8,128)S(1)} %get-tuple-element.38.inverse, f32[3,24,512]{2,1,0:T(8,128)S(1)} %get-tuple-element.39.own_rhs, f32[168,128]{1,0:T(8,128)S(1)} %interface.1.mine, f32[168,128]{1,0:T(8,128)S(1)} %collective-permute-done.1.other, f32[48,128]{1,0:T(8,128)S(1)} %ends.1.end_mine.end, ...), custom_call_target="tpu_custom_call" | custom-call | flops 200000000 | bytes 1069056 | tf_op jit(solution)/shard_map/block/pallas_call | solution.py:19
  19.6 0.2 widen.3.known
  19.8 0.3 %ready.1 = (f32[3,24,512]{2,1,0:T(8,128)S(1)}, f32[2,24,512]{2,1,0:T(8,128)S(1)}) custom-call(f32[3,24,512]{2,1,0:T(8,128)S(1)} %block.1.local, f32[2,2,24,256]{3,2,1,0:T(8,128)S(1)} %get-tuple-element.40.spikes, f32[72,128]{1,0:T(8,128)S(1)} %widen.3.known), custom_call_target="tpu_custom_call" | custom-call | flops 10000000 | bytes 282624 | tf_op jit(solution)/shard_map/ready/pallas_call | solution.py:19
  20.1 0.4 %collective-permute-done.8.received = f32[32,128]{1,0:T(8,128)S(1)} collective-permute-done((f32[32,128]{1,0:T(8,128)S(1)}, f32[32,128]{1,0:T(8,128)S(1)}, u32[]{:S(2)}, u32[]{:S(2)}) %collective-permute-start.8) | collective-permute-done | bytes 16416 | tf_op jit(solution)/shard_map/ppermute | solution.py:694
  20.5 0.8 %final.1 = f32[3,24,512]{2,1,0:T(8,128)} custom-call(f32[3,24,512]{2,1,0:T(8,128)S(1)} %get-tuple-element.43.ready, f32[2,24,512]{2,1,0:T(8,128)S(1)} %get-tuple-element.44.lift, f32[72,128]{1,0:T(8,128)S(1)} %get-tuple-element.45.composed, f32[32,128]{1,0:T(8,128)S(1)} %collective-permute-done.8.received), custom_call_target="tpu_custom_call" | custom-call | bytes 299008 | tf_op jit(solution)/shard_map/final/pallas_call | solution.py:19
  (1 shorter events, 0.0 us)
Async XLA Ops:
  1.1 3.3 %collective-permute-start.2 = (f32[48,128]{1,0:T(8,128)S(1)}, f32[48,128]{1,0:T(8,128)S(1)}, u32[]{:S(2)}, u32[]{:S(2)}) collective-permute-start(f32[48,128]{1,0:T(8,128)S(1)} %get-tuple-element.36), channel_id=1, source_target_pairs={{0,2},{2,0},{4,6},{6,4},{8,10},{10,8},{12,14},{14,12},{16,18},{18,... | collective-permute-start | bytes 73736 | tf_op jit(solution)/shard_map/ppermute | solution.py:588
  1.8 6.3 %collective-permute-start = (f32[216,128]{1,0:T(8,128)S(1)}, f32[216,128]{1,0:T(8,128)S(1)}, u32[]{:S(2)}, u32[]{:S(2)}) collective-permute-start(f32[216,128]{1,0:T(8,128)S(1)} %shares.1), channel_id=1, source_target_pairs={{0,1},{1,0},{2,3},{3,2},{4,5},{5,4},{6,7},{7,6},{8,9},{9,8},{10,11... | collective-permute-start | bytes 331784 | tf_op jit(solution)/shard_map/ppermute | solution.py:609
  4.5 3.9 %collective-permute-start.3 = (f32[48,128]{1,0:T(8,128)S(1)}, f32[48,128]{1,0:T(8,128)S(1)}, u32[]{:S(2)}, u32[]{:S(2)}) collective-permute-start(f32[48,128]{1,0:T(8,128)S(1)} %relay.1), channel_id=1, source_target_pairs={{1,7},{4,2},{3,4},{6,1},{5,11},{8,6},{7,8},{10,5},{9,15},{12,10},{... | collective-permute-start | bytes 73736 | tf_op jit(solution)/shard_map/ppermute | solution.py:614
  8.3 1.4 %collective-permute-start.1 = (f32[168,128]{1,0:T(8,128)S(1)}, f32[168,128]{1,0:T(8,128)S(1)}, u32[]{:S(2)}, u32[]{:S(2)}) collective-permute-start(f32[168,128]{1,0:T(8,128)S(1)} %interface.1.mine), channel_id=1, source_target_pairs={{0,2},{2,0},{4,6},{6,4},{8,10},{10,8},{12,14},{14,12},{16,18},{18,... | collective-permute-start | bytes 258056 | tf_op jit(solution)/shard_map/ppermute | solution.py:588
  8.4 1.3 %collective-permute-start.4 = (f32[48,128]{1,0:T(8,128)S(1)}, f32[48,128]{1,0:T(8,128)S(1)}, u32[]{:S(2)}, u32[]{:S(2)}) collective-permute-start(f32[48,128]{1,0:T(8,128)S(1)} %ends.1.end_mine.end), channel_id=1, source_target_pairs={{0,2},{2,0},{4,6},{6,4},{8,10},{10,8},{12,14},{14,12},{16,18},{18,... | collective-permute-start | bytes 73736 | tf_op jit(solution)/shard_map/ppermute | solution.py:588
  9.9 5.1 %collective-permute-start.5 = (f32[72,128]{1,0:T(8,128)S(1)}, f32[72,128]{1,0:T(8,128)S(1)}, u32[]{:S(2)}, u32[]{:S(2)}) collective-permute-start(f32[72,128]{1,0:T(8,128)S(1)} %get-tuple-element.37.after.refs_0_), channel_id=1, source_target_pairs={{0,14},{2,12},{4,10},{6,8},{8,6},{10,4},{12,2},{14,0},{16,30},{18,... | collective-permute-start | bytes 110600 | tf_op jit(solution)/shard_map/ppermute | solution.py:676
  12.6 3.5 %collective-permute-start.6 = (f32[72,128]{1,0:T(8,128)S(1)}, f32[72,128]{1,0:T(8,128)S(1)}, u32[]{:S(2)}, u32[]{:S(2)}) collective-permute-start(f32[72,128]{1,0:T(8,128)S(1)} %get-tuple-element.37.after.refs_0_), channel_id=1, source_target_pairs={{0,10},{2,8},{4,14},{6,12},{8,2},{10,0},{12,6},{14,4},{16,26},{18,... | collective-permute-start | bytes 110600 | tf_op jit(solution)/shard_map/ppermute | solution.py:676
  12.9 3.4 %collective-permute-start.7 = (f32[72,128]{1,0:T(8,128)S(1)}, f32[72,128]{1,0:T(8,128)S(1)}, u32[]{:S(2)}, u32[]{:S(2)}) collective-permute-start(f32[72,128]{1,0:T(8,128)S(1)} %get-tuple-element.37.after.refs_0_), channel_id=1, source_target_pairs={{0,6},{2,4},{4,2},{6,0},{8,14},{10,12},{12,10},{14,8},{16,22},{18,... | collective-permute-start | bytes 110600 | tf_op jit(solution)/shard_map/ppermute | solution.py:676
  16.3 4.1 %collective-permute-start.8 = (f32[32,128]{1,0:T(8,128)S(1)}, f32[32,128]{1,0:T(8,128)S(1)}, u32[]{:S(2)}, u32[]{:S(2)}) collective-permute-start(f32[32,128]{1,0:T(8,128)S(1)} %get-tuple-element.46), channel_id=1, source_target_pairs={{0,18},{2,16},{4,22},{6,20},{8,26},{10,24},{12,30},{14,28},{16,2},... | collective-permute-start | bytes 49160 | tf_op jit(solution)/shard_map/ppermute | solution.py:694
